TPU v7x, 32 devices: a whole 2x2x4 slice. The times are simulated.
32 devices in a mesh: pipe: 2 (over x), dp: 2 (over y), tensor: 8 (over z, core).
Axes of the slice: x: 2, y: 2, z: 4, core: 2. Of those that a mesh axis runs over, the one named last changes fastest.
Arguments:
- states: bfloat16 [1152, 8, 1024], P('tensor', 'dp'), may hold values from -6 to 6
- cotangent: bfloat16 [1152, 8, 1024], P('tensor', 'dp'), may hold values from -6 to 6
- lengths: int32 [8, 4], P('dp'), may hold values from 1 to 525, 1152 in all within a row
- timesteps: int32 [8, 4], P('dp'), may hold values from 0 to 4999
- time_weight: float32 [2, 1024], P('pipe'), may hold values from -6 to 6
- time_bias: float32 [2, 1024], P('pipe'), may hold values from -3 to 3
- query_weight: bfloat16 [2, 1024, 1024], P('pipe', None, 'tensor'), may hold values from -0.1875 to 0.1875
- query_bias: float32 [2, 1024], P('pipe', 'tensor'), may hold values from -3 to 3
- key_weight: bfloat16 [2, 1024, 1024], P('pipe', None, 'tensor'), may hold values from -0.1875 to 0.1875
- value_weight: bfloat16 [2, 1024, 1024], P('pipe', None, 'tensor'), may hold values from -0.1875 to 0.1875
- value_bias: float32 [2, 1024], P('pipe', 'tensor'), may hold values from -3 to 3
- out_weight: bfloat16 [2, 1024, 1024], P('pipe', 'tensor'), may hold values from -3.5 to 3.5
- out_bias: float32 [2, 1024], P('pipe'), may hold values from -3 to 3
- attn_gain: float32 [2, 1024], P('pipe'), may hold values from 0.5 to 1.5
- attn_shift: float32 [2, 1024], P('pipe'), may hold values from -3 to 3
- ffn_in: bfloat16 [2, 1024, 4096], P('pipe', None, 'tensor'), may hold values from -0.1875 to 0.1875
- ffn_in_bias: bfloat16 [2, 4096], P('pipe', 'tensor'), may hold values from -3 to 3
- ffn_out: bfloat16 [2, 4096, 1024], P('pipe', 'tensor'), may hold values from -0.09375 to 0.09375
- ffn_out_bias: float32 [2, 1024], P('pipe'), may hold values from -3 to 3
- ffn_gain: float32 [2, 1024], P('pipe'), may hold values from 0.5 to 1.5
- ffn_shift: float32 [2, 1024], P('pipe'), may hold values from -3 to 3
Outputs:
- layer_out: bfloat16 [2, 1152, 8, 1024], P('pipe', 'tensor', 'dp')
- input_grad: bfloat16 [2, 1152, 8, 1024], P('pipe', 'tensor', 'dp')
- time_weight_grad: float32 [2, 1024], P('pipe')
- time_bias_grad: float32 [2, 1024], P('pipe')
- query_weight_grad: float32 [2, 1024, 1024], P('pipe', 'dp', 'tensor')
- query_bias_grad: float32 [2, 1024], P('pipe', 'tensor')
- key_weight_grad: float32 [2, 1024, 1024], P('pipe', 'dp', 'tensor')
- value_weight_grad: float32 [2, 1024, 1024], P('pipe', 'dp', 'tensor')
- value_bias_grad: float32 [2, 1024], P('pipe', 'tensor')
- out_weight_grad: float32 [2, 1024, 1024], P('pipe', 'tensor', 'dp')
- out_bias_grad: float32 [2, 1024], P('pipe')
- attn_gain_grad: float32 [2, 1024], P('pipe')
- attn_shift_grad: float32 [2, 1024], P('pipe')
- ffn_in_grad: float32 [2, 1024, 4096], P('pipe', 'dp', 'tensor')
- ffn_in_bias_grad: float32 [2, 4096], P('pipe', 'tensor')
- ffn_out_grad: float32 [2, 4096, 1024], P('pipe', 'tensor', 'dp')
- ffn_out_bias_grad: float32 [2, 1024], P('pipe')
- ffn_gain_grad: float32 [2, 1024], P('pipe')
- ffn_shift_grad: float32 [2, 1024], P('pipe')
- stats: float32 [2, 3], P('pipe')
Inputs may be any that keep to these rules, and one draw needn't show every extreme that they name: `lengths`: each row sums to 1152, and its largest entry is exactly 525.
All inputs are finite; a program needn't handle non-finite values.
Results may differ from a plain program's by a relative error of at most 0.03.
Values may be sent and summed in bfloat16 or wider, within the bound.
A program may use at most 256 MiB of HBM per device.

v0:
```python
import math

import jax
import jax.numpy as jnp
from jax import lax
from jax.sharding import PartitionSpec as P

HDIM = 64
SEQ_LEN = 1152
STEPS = 5000
MICRO = 4
SEQ_MB = 1


epsilon = 1e-05


def passed_along(shard, axis, by):
    size = lax.axis_size(axis)
    pairs = [(i, i + by) for i in range(size) if 0 <= i + by < size]
    return lax.ppermute(shard, axis, pairs)


def norm_parts(summed):
    centered = summed - jnp.mean(summed, axis=-1, keepdims=True)
    inverse = lax.rsqrt(jnp.mean(centered * centered, axis=-1, keepdims=True) + epsilon)
    return (centered * inverse, inverse)


def norm_back(upstream, normed, inverse, gain):
    scaled = upstream * gain
    return inverse * (
        scaled
        - jnp.mean(scaled, axis=-1, keepdims=True)
        - normed * jnp.mean(scaled * normed, axis=-1, keepdims=True)
    )


def token_sum(values):
    return jnp.sum(values.astype(jnp.float32), axis=(0, 1))


def place_block(vector, full_size, block_at):
    holder = jnp.zeros((full_size,), jnp.float32)
    return lax.dynamic_update_slice_in_dim(holder, vector, block_at * vector.shape[0], 0)


def gelu_exact(values):
    return jax.nn.gelu(values, approximate=False)


def per_device(
    states,
    cotangent,
    lengths,
    timesteps,
    time_weight,
    time_bias,
    query_weight,
    query_bias,
    key_weight,
    value_weight,
    value_bias,
    out_weight,
    out_bias,
    attn_gain,
    attn_shift,
    ffn_in,
    ffn_in_bias,
    ffn_out,
    ffn_out_bias,
    ffn_gain,
    ffn_shift,
):
    shard_rows, seq_count, model_width = states.shape
    section_at = lax.axis_index("pipe")
    sections = lax.axis_size("pipe")
    tensor_at = lax.axis_index("tensor")
    tensor_size = lax.axis_size("tensor")
    dp_size = lax.axis_size("dp")
    time_weight, time_bias, out_bias = (time_weight[0], time_bias[0], out_bias[0])
    attn_gain, attn_shift, ffn_out_bias = (attn_gain[0], attn_shift[0], ffn_out_bias[0])
    ffn_gain, ffn_shift = (ffn_gain[0], ffn_shift[0])
    query_weight, key_weight, value_weight = (query_weight[0], key_weight[0], value_weight[0])
    query_bias, value_bias, out_weight = (query_bias[0], value_bias[0], out_weight[0])
    ffn_in, ffn_in_bias, ffn_out = (ffn_in[0], ffn_in_bias[0], ffn_out[0])
    head_cols = query_weight.shape[1]
    heads_here = head_cols // HDIM
    score_scale = 1.0 / math.sqrt(HDIM)
    joined = jnp.concatenate([query_weight, key_weight, value_weight], axis=1)
    joined_bias = jnp.concatenate([query_bias, jnp.zeros_like(query_bias), value_bias])
    ffn_bias_wide = ffn_in_bias.astype(jnp.float32)
    item_ends = jnp.cumsum(lengths, axis=1)
    places = jnp.arange(SEQ_LEN, dtype=jnp.int32)
    segment_all = jnp.sum(
        (item_ends[None, :, :] <= places[:, None, None]).astype(jnp.int32), axis=2
    )
    item_pick = (
        segment_all[:, :, None] == jnp.arange(lengths.shape[1], dtype=jnp.int32)[None, None, :]
    )
    time_all = (
        jnp.sum(jnp.where(item_pick, timesteps[None, :, :].astype(jnp.float32), 0.0), axis=2)
        / STEPS
    )
    time_local = lax.dynamic_slice_in_dim(time_all, tensor_at * shard_rows, shard_rows, 0)

    def split_heads(qkv_low):
        length = qkv_low.shape[0]
        queries = qkv_low[:, :, :head_cols].reshape(length, -1, heads_here, HDIM)
        keys_all = qkv_low[:, :, head_cols : 2 * head_cols].reshape(length, -1, heads_here, HDIM)
        values = qkv_low[:, :, 2 * head_cols :].reshape(length, -1, heads_here, HDIM)
        return (queries, keys_all, values)

    def masked_scores(queries, keys_all, segment):
        same_item = segment.T[:, None, :, None] == segment.T[:, None, None, :]
        scores = (
            jnp.einsum("qshd,kshd->shqk", queries, keys_all, preferred_element_type=jnp.float32)
            * score_scale
        )
        return jnp.where(same_item, scores, -1e30)

    ticks = MICRO + sections - 1
    arriving = jnp.zeros((shard_rows, SEQ_MB, model_width), jnp.bfloat16)
    layer_rows = jnp.zeros_like(states)
    stored = None
    stat_sum = jnp.zeros((3,), jnp.float32)
    for tick_at in range(ticks):
        micro_at = tick_at - section_at
        active = (micro_at >= 0) & (micro_at < MICRO)
        slot_at = jnp.clip(micro_at, 0, MICRO - 1)
        offset = slot_at * SEQ_MB
        own_rows = lax.dynamic_slice_in_dim(states, offset, SEQ_MB, 1)
        inputs = jnp.where(section_at == 0, own_rows, arriving)
        time_rows = lax.dynamic_slice_in_dim(time_local, offset, SEQ_MB, 1)
        segment = lax.dynamic_slice_in_dim(segment_all, offset, SEQ_MB, 1)
        residual = inputs.astype(jnp.float32) + time_rows[:, :, None] * time_weight + time_bias
        forward_rounded = residual.astype(jnp.bfloat16)
        project_summed = jnp.einsum(
            "tsd,dc->tsc",
            lax.all_gather(forward_rounded, "tensor", axis=0, tiled=True),
            joined,
            preferred_element_type=jnp.float32,
        )
        forward_qkv_low = (project_summed + joined_bias).astype(jnp.bfloat16)
        forward_length = forward_qkv_low.shape[0]
        forward_queries, forward_keys_all, forward_values = split_heads(forward_qkv_low)
        forward_scores = masked_scores(forward_queries, forward_keys_all, segment)
        row_top = jnp.max(forward_scores, axis=-1, keepdims=True)
        weights = jnp.exp(forward_scores - row_top)
        row_total = jnp.sum(weights, axis=-1, keepdims=True)
        probs_low = (weights / row_total).astype(jnp.bfloat16)
        forward_log_total = row_top + jnp.log(row_total)
        forward_mixed_low = (
            jnp.einsum(
                "shqk,kshd->qshd", probs_low, forward_values, preferred_element_type=jnp.float32
            )
            .astype(jnp.bfloat16)
            .reshape(forward_length, -1, head_cols)
        )
        branch = (
            lax.psum_scatter(
                jnp.einsum(
                    "tsh,hd->tsd", forward_mixed_low, out_weight, preferred_element_type=jnp.float32
                ).astype(jnp.bfloat16),
                "tensor",
                scatter_dimension=0,
                tiled=True,
            ).astype(jnp.float32)
            + out_bias
        )
        forward_first_normed, forward_first_inverse = norm_parts(residual + branch)
        first_out = forward_first_normed * attn_gain + attn_shift
        forward_first_low = first_out.astype(jnp.bfloat16)
        forward_pre_act = (
            jnp.einsum(
                "tsd,df->tsf",
                lax.all_gather(forward_first_low, "tensor", axis=0, tiled=True),
                ffn_in,
                preferred_element_type=jnp.float32,
            )
            + ffn_bias_wide
        )
        forward_hidden = gelu_exact(forward_pre_act).astype(jnp.bfloat16)
        ffn_branch = (
            lax.psum_scatter(
                jnp.einsum(
                    "tsf,fd->tsd", forward_hidden, ffn_out, preferred_element_type=jnp.float32
                ).astype(jnp.bfloat16),
                "tensor",
                scatter_dimension=0,
                tiled=True,
            ).astype(jnp.float32)
            + ffn_out_bias
        )
        forward_second_normed, forward_second_inverse = norm_parts(first_out + ffn_branch)
        layer_y = (forward_second_normed * ffn_gain + ffn_shift).astype(jnp.bfloat16)
        forward_kept_acts = (
            forward_rounded,
            forward_qkv_low,
            forward_mixed_low,
            forward_log_total,
            forward_first_normed,
            forward_first_inverse,
            forward_first_low,
            forward_pre_act,
            forward_hidden,
            forward_second_normed,
            forward_second_inverse,
        )
        stat_terms = jnp.stack(
            [
                jnp.sum(residual * residual),
                jnp.sum(branch * branch),
                jnp.sum(ffn_branch * ffn_branch),
            ]
        )
        layer_y, kept_acts, stat_terms = (layer_y, forward_kept_acts, stat_terms)
        stat_sum = stat_sum + jnp.where(active, stat_terms, 0.0)
        if stored is None:
            stored = jax.tree.map(lambda a: jnp.zeros((MICRO,) + a.shape, a.dtype), kept_acts)
        stored = jax.tree.map(
            lambda s, a: s.at[slot_at].set(jnp.where(active, a, s[slot_at])), stored, kept_acts
        )
        previous = lax.dynamic_slice_in_dim(layer_rows, offset, SEQ_MB, 1)
        layer_rows = lax.dynamic_update_slice_in_dim(
            layer_rows, jnp.where(active, layer_y, previous), offset, 1
        )
        arriving = passed_along(layer_y, "pipe", 1)
    returning = jnp.zeros((shard_rows, SEQ_MB, model_width), jnp.bfloat16)
    grad_rows = jnp.zeros_like(states)
    totals = None
    for tick_at in range(ticks):
        micro_at = tick_at - (sections - 1 - section_at)
        active = (micro_at >= 0) & (micro_at < MICRO)
        slot_at = jnp.clip(micro_at, 0, MICRO - 1)
        offset = slot_at * SEQ_MB
        own_rows = lax.dynamic_slice_in_dim(cotangent, offset, SEQ_MB, 1)
        grad_out = jnp.where(section_at == sections - 1, own_rows, returning)
        time_rows = lax.dynamic_slice_in_dim(time_local, offset, SEQ_MB, 1)
        segment = lax.dynamic_slice_in_dim(segment_all, offset, SEQ_MB, 1)
        kept_acts = jax.tree.map(lambda s: s[slot_at], stored)
        (
            rounded,
            backward_qkv_low,
            mixed_low,
            log_total,
            first_normed,
            first_inverse,
            first_low,
            pre_act,
            hidden,
            second_normed,
            second_inverse,
        ) = kept_acts
        upstream = grad_out.astype(jnp.float32)
        backward_grad_gain_two = token_sum(upstream * second_normed)
        backward_grad_shift_two = token_sum(upstream)
        grad_second = norm_back(upstream, second_normed, second_inverse, ffn_gain)
        grad_ffn = grad_second.astype(jnp.bfloat16)
        backward_grad_out_bias = token_sum(grad_ffn)
        gelu_value, gelu_pull = jax.vjp(gelu_exact, pre_act)
        ffn_grad_all = lax.all_gather(grad_ffn, "tensor", axis=0, tiled=True)
        first_all = lax.all_gather(first_low, "tensor", axis=0, tiled=True)
        grad_hidden = jnp.einsum(
            "tsd,fd->tsf", ffn_grad_all, ffn_out, preferred_element_type=jnp.float32
        )
        grad_pre = gelu_pull(grad_hidden)[0].astype(jnp.bfloat16)
        backward_grad_ffn_in = jnp.einsum(
            "tsd,tsf->df", first_all, grad_pre, preferred_element_type=jnp.float32
        )
        backward_grad_ffn_out = jnp.einsum(
            "tsf,tsd->fd", hidden, ffn_grad_all, preferred_element_type=jnp.float32
        )
        grad_first = grad_second + lax.psum_scatter(
            jnp.einsum("tsf,df->tsd", grad_pre, ffn_in, preferred_element_type=jnp.float32).astype(
                jnp.bfloat16
            ),
            "tensor",
            scatter_dimension=0,
            tiled=True,
        ).astype(jnp.float32)
        backward_grad_in_bias = token_sum(grad_pre)
        backward_grad_gain_one = token_sum(grad_first * first_normed)
        backward_grad_shift_one = token_sum(grad_first)
        grad_resid = norm_back(grad_first, first_normed, first_inverse, attn_gain)
        grad_branch = grad_resid.astype(jnp.bfloat16)
        backward_grad_attn_bias = token_sum(grad_branch)
        branch_all = lax.all_gather(grad_branch, "tensor", axis=0, tiled=True)
        rounded_all = lax.all_gather(rounded, "tensor", axis=0, tiled=True)
        backward_length = branch_all.shape[0]
        backward_grad_out_weight = jnp.einsum(
            "tsh,tsd->hd", mixed_low, branch_all, preferred_element_type=jnp.float32
        )
        grad_mixed = jnp.einsum(
            "tsd,hd->tsh", branch_all, out_weight, preferred_element_type=jnp.float32
        ).astype(jnp.bfloat16)
        grad_mixed = grad_mixed.reshape(backward_length, -1, heads_here, HDIM)
        backward_queries, backward_keys_all, backward_values = split_heads(backward_qkv_low)
        backward_scores = masked_scores(backward_queries, backward_keys_all, segment)
        probs = jnp.exp(backward_scores - log_total)
        grad_probs = jnp.einsum(
            "qshd,kshd->shqk", grad_mixed, backward_values, preferred_element_type=jnp.float32
        )
        inner_sum = jnp.sum(probs * grad_probs, axis=-1, keepdims=True)
        grad_scores = (probs * (grad_probs - inner_sum)).astype(jnp.bfloat16)
        grad_queries = (
            jnp.einsum(
                "shqk,kshd->qshd",
                grad_scores,
                backward_keys_all,
                preferred_element_type=jnp.float32,
            )
            * score_scale
        ).astype(jnp.bfloat16)
        grad_keys = (
            jnp.einsum(
                "shqk,qshd->kshd", grad_scores, backward_queries, preferred_element_type=jnp.float32
            )
            * score_scale
        ).astype(jnp.bfloat16)
        grad_values = jnp.einsum(
            "shqk,qshd->kshd",
            probs.astype(jnp.bfloat16),
            grad_mixed,
            preferred_element_type=jnp.float32,
        ).astype(jnp.bfloat16)
        grad_qkv = jnp.concatenate(
            [
                grad_queries.reshape(backward_length, -1, head_cols),
                grad_keys.reshape(backward_length, -1, head_cols),
                grad_values.reshape(backward_length, -1, head_cols),
            ],
            axis=2,
        )
        backward_grad_joined = jnp.einsum(
            "tsd,tsc->dc", rounded_all, grad_qkv, preferred_element_type=jnp.float32
        )
        bias_sums = token_sum(grad_qkv)
        grad_input = grad_resid + lax.psum_scatter(
            jnp.einsum("tsc,dc->tsd", grad_qkv, joined, preferred_element_type=jnp.float32).astype(
                jnp.bfloat16
            ),
            "tensor",
            scatter_dimension=0,
            tiled=True,
        ).astype(jnp.float32)
        backward_grad_time_weight = token_sum(grad_input * time_rows[:, :, None])
        backward_grad_time_bias = token_sum(grad_input)
        matrices = (
            backward_grad_joined,
            backward_grad_out_weight,
            backward_grad_ffn_in,
            backward_grad_ffn_out,
        )
        backward_vectors = (
            backward_grad_time_weight,
            backward_grad_time_bias,
            backward_grad_attn_bias,
            backward_grad_gain_one,
            backward_grad_shift_one,
            backward_grad_out_bias,
            backward_grad_gain_two,
            backward_grad_shift_two,
        )
        backward_head_terms = (
            bias_sums[:head_cols],
            bias_sums[2 * head_cols :],
            backward_grad_in_bias,
        )
        grad_in = grad_input.astype(jnp.bfloat16)
        terms = (matrices, backward_vectors, backward_head_terms)
        if totals is None:
            totals = jax.tree.map(lambda b: jnp.where(active, b, jnp.zeros_like(b)), terms)
        else:
            totals = jax.tree.map(
                lambda a, b: a + jnp.where(active, b, jnp.zeros_like(b)), totals, terms
            )
        previous = lax.dynamic_slice_in_dim(grad_rows, offset, SEQ_MB, 1)
        grad_rows = lax.dynamic_update_slice_in_dim(
            grad_rows, jnp.where(active, grad_in, previous), offset, 1
        )
        returning = passed_along(grad_in, "pipe", -1)
    (grad_joined, grad_out_weight, grad_ffn_in, grad_ffn_out), vectors, head_terms = totals
    grad_query_bias, grad_value_bias, grad_in_bias = head_terms
    grad_query = grad_joined[:, :head_cols]
    grad_key = grad_joined[:, head_cols : 2 * head_cols]
    grad_value = grad_joined[:, 2 * head_cols :]
    shares = (
        lax.psum_scatter(
            grad_query.astype(jnp.bfloat16), "dp", scatter_dimension=0, tiled=True
        ).astype(jnp.float32),
        lax.psum_scatter(
            grad_key.astype(jnp.bfloat16), "dp", scatter_dimension=0, tiled=True
        ).astype(jnp.float32),
        lax.psum_scatter(
            grad_value.astype(jnp.bfloat16), "dp", scatter_dimension=0, tiled=True
        ).astype(jnp.float32),
        lax.psum_scatter(
            grad_out_weight.astype(jnp.bfloat16), "dp", scatter_dimension=1, tiled=True
        ).astype(jnp.float32),
        lax.psum_scatter(
            grad_ffn_in.astype(jnp.bfloat16), "dp", scatter_dimension=0, tiled=True
        ).astype(jnp.float32),
        lax.psum_scatter(
            grad_ffn_out.astype(jnp.bfloat16), "dp", scatter_dimension=1, tiled=True
        ).astype(jnp.float32),
    )
    ffn_width = ffn_in.shape[1] * tensor_size
    (
        grad_time_weight,
        grad_time_bias,
        grad_attn_bias,
        grad_gain_one,
        grad_shift_one,
        grad_out_bias,
        grad_gain_two,
        grad_shift_two,
    ) = vectors
    summed = lax.psum(
        (
            grad_time_weight,
            grad_time_bias,
            grad_attn_bias,
            grad_gain_one,
            grad_shift_one,
            grad_out_bias,
            grad_gain_two,
            grad_shift_two,
            place_block(grad_query_bias, model_width, tensor_at),
            place_block(grad_value_bias, model_width, tensor_at),
            place_block(grad_in_bias, ffn_width, tensor_at),
            stat_sum,
        ),
        ("dp", "tensor"),
    )
    query_bias_grad = lax.dynamic_slice_in_dim(summed[8], tensor_at * head_cols, head_cols, 0)
    value_bias_grad = lax.dynamic_slice_in_dim(summed[9], tensor_at * head_cols, head_cols, 0)
    in_cols = ffn_in.shape[1]
    ffn_bias_grad = lax.dynamic_slice_in_dim(summed[10], tensor_at * in_cols, in_cols, 0)
    element_count = float(SEQ_LEN * seq_count * dp_size * model_width)
    stats = jnp.sqrt(summed[11] / element_count)
    return (
        layer_rows[None],
        grad_rows[None],
        summed[0][None],
        summed[1][None],
        shares[0][None],
        query_bias_grad[None],
        shares[1][None],
        shares[2][None],
        value_bias_grad[None],
        shares[3][None],
        summed[2][None],
        summed[3][None],
        summed[4][None],
        shares[4][None],
        ffn_bias_grad[None],
        shares[5][None],
        summed[5][None],
        summed[6][None],
        summed[7][None],
        stats[None],
    )


def solution(mesh):
    return jax.shard_map(
        per_device,
        mesh=mesh,
        in_specs=(
            P("tensor", "dp", None),
            P("tensor", "dp", None),
            P("dp", None),
            P("dp", None),
            P("pipe", None),
            P("pipe", None),
            P("pipe", None, "tensor"),
            P("pipe", "tensor"),
            P("pipe", None, "tensor"),
            P("pipe", None, "tensor"),
            P("pipe", "tensor"),
            P("pipe", "tensor", None),
            P("pipe", None),
            P("pipe", None),
            P("pipe", None),
            P("pipe", None, "tensor"),
            P("pipe", "tensor"),
            P("pipe", "tensor", None),
            P("pipe", None),
            P("pipe", None),
            P("pipe", None),
        ),
        out_specs=(
            P("pipe", "tensor", "dp", None),
            P("pipe", "tensor", "dp", None),
            P("pipe", None),
            P("pipe", None),
            P("pipe", "dp", "tensor"),
            P("pipe", "tensor"),
            P("pipe", "dp", "tensor"),
            P("pipe", "dp", "tensor"),
            P("pipe", "tensor"),
            P("pipe", "tensor", "dp"),
            P("pipe", None),
            P("pipe", None),
            P("pipe", None),
            P("pipe", "dp", "tensor"),
            P("pipe", "tensor"),
            P("pipe", "tensor", "dp"),
            P("pipe", None),
            P("pipe", None),
            P("pipe", None),
            P("pipe", None),
        ),
        check_vma=False,
    )
```

profile of v0, /device:TPU:0, one launch (start us, length us, event | category | flops | bytes accessed | tf_op | source)
XLA Modules:
  0.0 2314.2 jit_solution(15704321916165522315)
XLA Ops:
  23.0 31.6 %all-gather.41.cloned.1.call-done = bf16[1152,1,1024]{2,0,1:T(8,128)(2,1)} async-done(((bf16[144,1,1024]{2,0,1:T(8,128)(2,1)}), bf16[1152,1,1024]{2,0,1:T(8,128)(2,1)}) %all-gather.41.cloned.1.call-update) | async-done | bytes 2359312 | tf_op jit(solution)/shard_map/all_gather | solution.py:140
  69.9 35.4 %reduce-scatter.27.cloned.1.call-done = bf16[144,1,1024]{2,0,1:T(8,128)(2,1)} async-done(((bf16[1152,1,1024]{2,0,1:T(8,128)(2,1)}), bf16[144,1,1024]{2,0,1:T(8,128)(2,1)}) %reduce-scatter.27.cloned.1.call-update) | async-done | bytes 294928 | tf_op jit(solution)/shard_map/reduce_scatter | solution.py:161
  113.2 30.7 %all-gather.43.cloned.1.call-done = bf16[1152,1,1024]{2,0,1:T(8,128)(2,1)} async-done(((bf16[144,1,1024]{2,0,1:T(8,128)(2,1)}), bf16[1152,1,1024]{2,0,1:T(8,128)(2,1)}) %all-gather.43.cloned.1.call-update) | async-done | bytes 2359312 | tf_op jit(solution)/shard_map/all_gather | solution.py:177
  157.9 35.5 %reduce-scatter.29.cloned.1.call-done = bf16[144,1,1024]{2,0,1:T(8,128)(2,1)} async-done(((bf16[1152,1,1024]{2,0,1:T(8,128)(2,1)}), bf16[144,1,1024]{2,0,1:T(8,128)(2,1)}) %reduce-scatter.29.cloned.1.call-update) | async-done | bytes 294928 | tf_op jit(solution)/shard_map/reduce_scatter | solution.py:185
  213.1 29.1 %all-gather.45.cloned.1.call-done = bf16[1152,1,1024]{2,0,1:T(8,128)(2,1)} async-done(((bf16[144,1,1024]{2,0,1:T(8,128)(2,1)}), bf16[1152,1,1024]{2,0,1:T(8,128)(2,1)}) %all-gather.45.cloned.1.call-update) | async-done | bytes 2359312 | tf_op jit(solution)/shard_map/all_gather | solution.py:140
  256.5 34.6 %reduce-scatter.31.cloned.1.call-done = bf16[144,1,1024]{2,0,1:T(8,128)(2,1)} async-done(((bf16[1152,1,1024]{2,0,1:T(8,128)(2,1)}), bf16[144,1,1024]{2,0,1:T(8,128)(2,1)}) %reduce-scatter.31.cloned.1.call-update) | async-done | bytes 294928 | tf_op jit(solution)/shard_map/reduce_scatter | solution.py:161
  300.1 28.1 %all-gather.47.cloned.1.call-done = bf16[1152,1,1024]{2,0,1:T(8,128)(2,1)} async-done(((bf16[144,1,1024]{2,0,1:T(8,128)(2,1)}), bf16[1152,1,1024]{2,0,1:T(8,128)(2,1)}) %all-gather.47.cloned.1.call-update) | async-done | bytes 2359312 | tf_op jit(solution)/shard_map/all_gather | solution.py:177
  341.0 35.4 %reduce-scatter.33.cloned.1.call-done = bf16[144,1,1024]{2,0,1:T(8,128)(2,1)} async-done(((bf16[1152,1,1024]{2,0,1:T(8,128)(2,1)}), bf16[144,1,1024]{2,0,1:T(8,128)(2,1)}) %reduce-scatter.33.cloned.1.call-update) | async-done | bytes 294928 | tf_op jit(solution)/shard_map/reduce_scatter | solution.py:185
  395.4 29.2 %all-gather.49.cloned.1.call-done = bf16[1152,1,1024]{2,0,1:T(8,128)(2,1)} async-done(((bf16[144,1,1024]{2,0,1:T(8,128)(2,1)}), bf16[1152,1,1024]{2,0,1:T(8,128)(2,1)}) %all-gather.49.cloned.1.call-update) | async-done | bytes 2359312 | tf_op jit(solution)/shard_map/all_gather | solution.py:140
  438.7 34.5 %reduce-scatter.35.cloned.1.call-done = bf16[144,1,1024]{2,0,1:T(8,128)(2,1)} async-done(((bf16[1152,1,1024]{2,0,1:T(8,128)(2,1)}), bf16[144,1,1024]{2,0,1:T(8,128)(2,1)}) %reduce-scatter.35.cloned.1.call-update) | async-done | bytes 294928 | tf_op jit(solution)/shard_map/reduce_scatter | solution.py:161
  481.9 28.4 %all-gather.51.cloned.1.call-done = bf16[1152,1,1024]{2,0,1:T(8,128)(2,1)} async-done(((bf16[144,1,1024]{2,0,1:T(8,128)(2,1)}), bf16[1152,1,1024]{2,0,1:T(8,128)(2,1)}) %all-gather.51.cloned.1.call-update) | async-done | bytes 2359312 | tf_op jit(solution)/shard_map/all_gather | solution.py:177
  523.1 35.5 %reduce-scatter.37.cloned.1.call-done = bf16[144,1,1024]{2,0,1:T(8,128)(2,1)} async-done(((bf16[1152,1,1024]{2,0,1:T(8,128)(2,1)}), bf16[144,1,1024]{2,0,1:T(8,128)(2,1)}) %reduce-scatter.37.cloned.1.call-update) | async-done | bytes 294928 | tf_op jit(solution)/shard_map/reduce_scatter | solution.py:185
  577.7 28.9 %all-gather.53.cloned.1.call-done = bf16[1152,1,1024]{2,0,1:T(8,128)(2,1)} async-done(((bf16[144,1,1024]{2,0,1:T(8,128)(2,1)}), bf16[1152,1,1024]{2,0,1:T(8,128)(2,1)}) %all-gather.53.cloned.1.call-update) | async-done | bytes 2359312 | tf_op jit(solution)/shard_map/all_gather | solution.py:140
  620.8 34.5 %reduce-scatter.39.cloned.1.call-done = bf16[144,1,1024]{2,0,1:T(8,128)(2,1)} async-done(((bf16[1152,1,1024]{2,0,1:T(8,128)(2,1)}), bf16[144,1,1024]{2,0,1:T(8,128)(2,1)}) %reduce-scatter.39.cloned.1.call-update) | async-done | bytes 294928 | tf_op jit(solution)/shard_map/reduce_scatter | solution.py:161
  664.2 28.1 %all-gather.55.cloned.1.call-done = bf16[1152,1,1024]{2,0,1:T(8,128)(2,1)} async-done(((bf16[144,1,1024]{2,0,1:T(8,128)(2,1)}), bf16[1152,1,1024]{2,0,1:T(8,128)(2,1)}) %all-gather.55.cloned.1.call-update) | async-done | bytes 2359312 | tf_op jit(solution)/shard_map/all_gather | solution.py:177
  705.1 35.5 %reduce-scatter.41.cloned.1.call-done = bf16[144,1,1024]{2,0,1:T(8,128)(2,1)} async-done(((bf16[1152,1,1024]{2,0,1:T(8,128)(2,1)}), bf16[144,1,1024]{2,0,1:T(8,128)(2,1)}) %reduce-scatter.41.cloned.1.call-update) | async-done | bytes 294928 | tf_op jit(solution)/shard_map/reduce_scatter | solution.py:185
  760.4 28.2 %all-gather.57.cloned.1.call-done = bf16[1152,1,1024]{2,0,1:T(8,128)(2,1)} async-done(((bf16[144,1,1024]{2,0,1:T(8,128)(2,1)}), bf16[1152,1,1024]{2,0,1:T(8,128)(2,1)}) %all-gather.57.cloned.1.call-update) | async-done | bytes 2359312 | tf_op jit(solution)/shard_map/all_gather | solution.py:140
  802.8 34.4 %reduce-scatter.43.cloned.1.call-done = bf16[144,1,1024]{2,0,1:T(8,128)(2,1)} async-done(((bf16[1152,1,1024]{2,0,1:T(8,128)(2,1)}), bf16[144,1,1024]{2,0,1:T(8,128)(2,1)}) %reduce-scatter.43.cloned.1.call-update) | async-done | bytes 294928 | tf_op jit(solution)/shard_map/reduce_scatter | solution.py:161
  845.0 29.3 %all-gather.59.cloned.1.call-done = bf16[1152,1,1024]{2,0,1:T(8,128)(2,1)} async-done(((bf16[144,1,1024]{2,0,1:T(8,128)(2,1)}), bf16[1152,1,1024]{2,0,1:T(8,128)(2,1)}) %all-gather.59.cloned.1.call-update) | async-done | bytes 2359312 | tf_op jit(solution)/shard_map/all_gather | solution.py:177
  904.5 18.0 reduce-scatter.45.cloned.1.call-done
  981.5 27.5 %reduce-scatter.47.cloned.1.call-done = bf16[144,1,1024]{2,0,1:T(8,128)(2,1)} async-done(((bf16[1152,1,1024]{2,0,1:T(8,128)(2,1)}), bf16[144,1,1024]{2,0,1:T(8,128)(2,1)}) %reduce-scatter.47.cloned.1.call-update) | async-done | bytes 294928 | tf_op jit(solution)/shard_map/reduce_scatter | solution.py:274
  1027.5 17.5 all-gather.63.cloned.1.call-done
  1062.2 35.7 %reduce-scatter.49.cloned.1.call-done = bf16[144,1,1024]{2,0,1:T(8,128)(2,1)} async-done(((bf16[1152,1,1024]{2,0,1:T(8,128)(2,1)}), bf16[144,1,1024]{2,0,1:T(8,128)(2,1)}) %reduce-scatter.49.cloned.1.call-update) | async-done | bytes 294928 | tf_op jit(solution)/shard_map/reduce_scatter | solution.py:339
  1112.0 30.2 %all-gather.65.cloned.1.call-done = bf16[1152,1,1024]{2,0,1:T(8,128)(2,1)} async-done(((bf16[144,1,1024]{2,0,1:T(8,128)(2,1)}), bf16[1152,1,1024]{2,0,1:T(8,128)(2,1)}) %all-gather.65.cloned.1.call-update) | async-done | bytes 2359312 | tf_op jit(solution)/shard_map/all_gather | solution.py:262
  1155.5 35.6 %reduce-scatter.51.cloned.1.call-done = bf16[144,1,1024]{2,0,1:T(8,128)(2,1)} async-done(((bf16[1152,1,1024]{2,0,1:T(8,128)(2,1)}), bf16[144,1,1024]{2,0,1:T(8,128)(2,1)}) %reduce-scatter.51.cloned.1.call-update) | async-done | bytes 294928 | tf_op jit(solution)/shard_map/reduce_scatter | solution.py:274
  1200.6 26.3 %all-gather.67.cloned.1.call-done = bf16[1152,1,1024]{2,0,1:T(8,128)(2,1)} async-done(((bf16[144,1,1024]{2,0,1:T(8,128)(2,1)}), bf16[1152,1,1024]{2,0,1:T(8,128)(2,1)}) %all-gather.67.cloned.1.call-update) | async-done | bytes 2359312 | tf_op jit(solution)/shard_map/all_gather | solution.py:288
  1244.2 35.5 %reduce-scatter.53.cloned.1.call-done = bf16[144,1,1024]{2,0,1:T(8,128)(2,1)} async-done(((bf16[1152,1,1024]{2,0,1:T(8,128)(2,1)}), bf16[144,1,1024]{2,0,1:T(8,128)(2,1)}) %reduce-scatter.53.cloned.1.call-update) | async-done | bytes 294928 | tf_op jit(solution)/shard_map/reduce_scatter | solution.py:339
  1295.7 30.3 %all-gather.69.cloned.1.call-done = bf16[1152,1,1024]{2,0,1:T(8,128)(2,1)} async-done(((bf16[144,1,1024]{2,0,1:T(8,128)(2,1)}), bf16[1152,1,1024]{2,0,1:T(8,128)(2,1)}) %all-gather.69.cloned.1.call-update) | async-done | bytes 2359312 | tf_op jit(solution)/shard_map/all_gather | solution.py:262
  1339.3 35.5 %reduce-scatter.55.cloned.1.call-done = bf16[144,1,1024]{2,0,1:T(8,128)(2,1)} async-done(((bf16[1152,1,1024]{2,0,1:T(8,128)(2,1)}), bf16[144,1,1024]{2,0,1:T(8,128)(2,1)}) %reduce-scatter.55.cloned.1.call-update) | async-done | bytes 294928 | tf_op jit(solution)/shard_map/reduce_scatter | solution.py:274
  1379.8 30.8 %all-gather.71.cloned.1.call-done = bf16[1152,1,1024]{2,0,1:T(8,128)(2,1)} async-done(((bf16[144,1,1024]{2,0,1:T(8,128)(2,1)}), bf16[1152,1,1024]{2,0,1:T(8,128)(2,1)}) %all-gather.71.cloned.1.call-update) | async-done | bytes 2359312 | tf_op jit(solution)/shard_map/all_gather | solution.py:288
  1428.0 35.5 %reduce-scatter.57.cloned.1.call-done = bf16[144,1,1024]{2,0,1:T(8,128)(2,1)} async-done(((bf16[1152,1,1024]{2,0,1:T(8,128)(2,1)}), bf16[144,1,1024]{2,0,1:T(8,128)(2,1)}) %reduce-scatter.57.cloned.1.call-update) | async-done | bytes 294928 | tf_op jit(solution)/shard_map/reduce_scatter | solution.py:339
  1479.7 30.0 %all-gather.73.cloned.1.call-done = bf16[1152,1,1024]{2,0,1:T(8,128)(2,1)} async-done(((bf16[144,1,1024]{2,0,1:T(8,128)(2,1)}), bf16[1152,1,1024]{2,0,1:T(8,128)(2,1)}) %all-gather.73.cloned.1.call-update) | async-done | bytes 2359312 | tf_op jit(solution)/shard_map/all_gather | solution.py:262
  1523.1 35.5 %reduce-scatter.59.cloned.1.call-done = bf16[144,1,1024]{2,0,1:T(8,128)(2,1)} async-done(((bf16[1152,1,1024]{2,0,1:T(8,128)(2,1)}), bf16[144,1,1024]{2,0,1:T(8,128)(2,1)}) %reduce-scatter.59.cloned.1.call-update) | async-done | bytes 294928 | tf_op jit(solution)/shard_map/reduce_scatter | solution.py:274
  1566.4 27.0 %all-gather.75.cloned.1.call-done = bf16[1152,1,1024]{2,0,1:T(8,128)(2,1)} async-done(((bf16[144,1,1024]{2,0,1:T(8,128)(2,1)}), bf16[1152,1,1024]{2,0,1:T(8,128)(2,1)}) %all-gather.75.cloned.1.call-update) | async-done | bytes 2359312 | tf_op jit(solution)/shard_map/all_gather | solution.py:288
  1610.6 35.5 %reduce-scatter.61.cloned.1.call-done = bf16[144,1,1024]{2,0,1:T(8,128)(2,1)} async-done(((bf16[1152,1,1024]{2,0,1:T(8,128)(2,1)}), bf16[144,1,1024]{2,0,1:T(8,128)(2,1)}) %reduce-scatter.61.cloned.1.call-update) | async-done | bytes 294928 | tf_op jit(solution)/shard_map/reduce_scatter | solution.py:339
  1660.9 30.3 %all-gather.77.cloned.1.call-done = bf16[1152,1,1024]{2,0,1:T(8,128)(2,1)} async-done(((bf16[144,1,1024]{2,0,1:T(8,128)(2,1)}), bf16[1152,1,1024]{2,0,1:T(8,128)(2,1)}) %all-gather.77.cloned.1.call-update) | async-done | bytes 2359312 | tf_op jit(solution)/shard_map/all_gather | solution.py:262
  1713.1 26.3 %reduce-scatter.63.cloned.1.call-done = bf16[144,1,1024]{2,0,1:T(8,128)(2,1)} async-done(((bf16[1152,1,1024]{2,0,1:T(8,128)(2,1)}), bf16[144,1,1024]{2,0,1:T(8,128)(2,1)}) %reduce-scatter.63.cloned.1.call-update) | async-done | bytes 294928 | tf_op jit(solution)/shard_map/reduce_scatter | solution.py:274
  1753.9 18.1 all-gather.93.cloned.1.call-done
  1779.2 25.8 %all-gather.83.cloned.1.call-done = bf16[1,1152,1,1024]{3,1,2,0:T(8,128)(2,1)} async-done(((bf16[1,144,1,1024]{3,1,2,0:T(8,128)(2,1)}), bf16[1,1152,1,1024]{3,1,2,0:T(8,128)(2,1)}) %all-gather.83.cloned.1.call-update) | async-done | bytes 2359312 | tf_op jit(solution)/shard_map/all_gather | solution.py:289
  1813.7 23.7 %all-gather.95.cloned.1.call-done = bf16[1,1152,1,1024]{3,1,2,0:T(8,128)(2,1)} async-done(((bf16[1,144,1,1024]{3,1,2,0:T(8,128)(2,1)}), bf16[1,1152,1,1024]{3,1,2,0:T(8,128)(2,1)}) %all-gather.95.cloned.1.call-update) | async-done | bytes 2359312 | tf_op jit(solution)/shard_map/all_gather | solution.py:263
  1844.6 24.8 %all-gather.85.cloned.1.call-done = bf16[1,1152,1,1024]{3,1,2,0:T(8,128)(2,1)} async-done(((bf16[1,144,1,1024]{3,1,2,0:T(8,128)(2,1)}), bf16[1,1152,1,1024]{3,1,2,0:T(8,128)(2,1)}) %all-gather.85.cloned.1.call-update) | async-done | bytes 2359312 | tf_op jit(solution)/shard_map/all_gather | solution.py:289
  1907.1 27.6 %all-gather.87.cloned.1.call-done = bf16[1,1152,1,1024]{3,1,2,0:T(8,128)(2,1)} async-done(((bf16[1,144,1,1024]{3,1,2,0:T(8,128)(2,1)}), bf16[1,1152,1,1024]{3,1,2,0:T(8,128)(2,1)}) %all-gather.87.cloned.1.call-update) | async-done | bytes 2359312 | tf_op jit(solution)/shard_map/all_gather | solution.py:289
  1939.0 27.9 %all-gather.99.cloned.1.call-done = bf16[1,1152,1,1024]{3,1,2,0:T(8,128)(2,1)} async-done(((bf16[1,144,1,1024]{3,1,2,0:T(8,128)(2,1)}), bf16[1,1152,1,1024]{3,1,2,0:T(8,128)(2,1)}) %all-gather.99.cloned.1.call-update) | async-done | bytes 2359312 | tf_op jit(solution)/shard_map/all_gather | solution.py:263
  1971.8 27.4 %all-gather.91.cloned.1.call-done = bf16[1,1152,1,1024]{3,1,2,0:T(8,128)(2,1)} async-done(((bf16[1,144,1,1024]{3,1,2,0:T(8,128)(2,1)}), bf16[1,1152,1,1024]{3,1,2,0:T(8,128)(2,1)}) %all-gather.91.cloned.1.call-update) | async-done | bytes 2359312 | tf_op jit(solution)/shard_map/all_gather | solution.py:263
  2006.3 25.1 %all-gather.79.cloned.1.call-done = bf16[1152,1,1024]{2,0,1:T(8,128)(2,1)} async-done(((bf16[144,1,1024]{2,0,1:T(8,128)(2,1)}), bf16[1152,1,1024]{2,0,1:T(8,128)(2,1)}) %all-gather.79.cloned.1.call-update) | async-done | bytes 2359312 | tf_op jit(solution)/shard_map/all_gather | solution.py:288
  2068.1 27.8 %all-gather.81.cloned.1.call-done = bf16[1,1152,1,1024]{3,1,2,0:T(8,128)(2,1)} async-done(((bf16[1,144,1,1024]{3,1,2,0:T(8,128)(2,1)}), bf16[1,1152,1,1024]{3,1,2,0:T(8,128)(2,1)}) %all-gather.81.cloned.1.call-update) | async-done | bytes 2359312 | tf_op jit(solution)/shard_map/all_gather | solution.py:289
  2201.0 37.0 %reduce-scatter.65.cloned.1.call-done = bf16[144,1,1024]{2,0,1:T(8,128)(2,1)} async-done(((bf16[1152,1,1024]{2,0,1:T(8,128)(2,1)}), bf16[144,1,1024]{2,0,1:T(8,128)(2,1)}) %reduce-scatter.65.cloned.1.call-update) | async-done | bytes 294928 | tf_op jit(solution)/shard_map/reduce_scatter | solution.py:339
  2239.1 60.7 %all-reduce = (f32[1,1024]{1,0:T(1,128)}, f32[1,1024]{1,0:T(1,128)}, f32[1024]{0:T(1024)S(1)}, f32[1024]{0:T(1024)S(1)}, f32[1,1024]{1,0:T(1,128)}, /*index=5*/f...) all-reduce(f32[1,1024]{1,0:T(1,128)S(1)} %bitcast.1719, ...), channel_id=1, replica_groups=mesh['pipe'=2,'dp'=2,'tensor'=8] {'dp','tensor'}, use_global_device_ids=true, to_apply=%region_93.94 | all-reduce | flops 14339 | bytes 114712 | tf_op jit(solution)/shard_map/psum | solution.py:419
  (1081 shorter events, 819.3 us)
Async XLA Ops:
  20.1 85.3 %reduce-scatter.27.cloned.1.call-start = ((), (), s32[]{:S(2)}) async-start(), calls=%async_computation.27 | async-start | bytes 2654208 | tf_op jit(solution)/shard_map/reduce_scatter | solution.py:161
  69.9 74.0 %all-gather.43.cloned.1.call-start = ((), (), s32[]{:S(2)}) async-start(), calls=%async_computation.28 | async-start | bytes 2654208 | tf_op jit(solution)/shard_map/all_gather | solution.py:177
  112.9 80.4 %reduce-scatter.29.cloned.1.call-start = ((), (), s32[]{:S(2)}) async-start(), calls=%async_computation.29 | async-start | bytes 2654208 | tf_op jit(solution)/shard_map/reduce_scatter | solution.py:185
  157.8 84.4 %all-gather.45.cloned.1.call-start = ((), (), s32[]{:S(2)}) async-start(), calls=%async_computation.30 | async-start | bytes 2654208 | tf_op jit(solution)/shard_map/all_gather | solution.py:140
  209.0 82.0 %reduce-scatter.31.cloned.1.call-start = ((), (), s32[]{:S(2)}) async-start(), calls=%async_computation.31 | async-start | bytes 2654208 | tf_op jit(solution)/shard_map/reduce_scatter | solution.py:161
  255.4 72.7 %all-gather.47.cloned.1.call-start = ((), (), s32[]{:S(2)}) async-start(), calls=%async_computation.32 | async-start | bytes 2654208 | tf_op jit(solution)/shard_map/all_gather | solution.py:177
  297.2 79.2 %reduce-scatter.33.cloned.1.call-start = ((), (), s32[]{:S(2)}) async-start(), calls=%async_computation.33 | async-start | bytes 2654208 | tf_op jit(solution)/shard_map/reduce_scatter | solution.py:185
  341.0 83.6 %all-gather.49.cloned.1.call-start = ((), (), s32[]{:S(2)}) async-start(), calls=%async_computation.34 | async-start | bytes 2654208 | tf_op jit(solution)/shard_map/all_gather | solution.py:140
  391.1 82.1 %reduce-scatter.35.cloned.1.call-start = ((), (), s32[]{:S(2)}) async-start(), calls=%async_computation.35 | async-start | bytes 2654208 | tf_op jit(solution)/shard_map/reduce_scatter | solution.py:161
  437.7 72.6 %all-gather.51.cloned.1.call-start = ((), (), s32[]{:S(2)}) async-start(), calls=%async_computation.36 | async-start | bytes 2654208 | tf_op jit(solution)/shard_map/all_gather | solution.py:177
  479.3 79.3 %reduce-scatter.37.cloned.1.call-start = ((), (), s32[]{:S(2)}) async-start(), calls=%async_computation.37 | async-start | bytes 2654208 | tf_op jit(solution)/shard_map/reduce_scatter | solution.py:185
  523.0 83.6 %all-gather.53.cloned.1.call-start = ((), (), s32[]{:S(2)}) async-start(), calls=%async_computation.38 | async-start | bytes 2654208 | tf_op jit(solution)/shard_map/all_gather | solution.py:140
  573.4 81.9 %reduce-scatter.39.cloned.1.call-start = ((), (), s32[]{:S(2)}) async-start(), calls=%async_computation.39 | async-start | bytes 2654208 | tf_op jit(solution)/shard_map/reduce_scatter | solution.py:161
  661.4 79.3 %reduce-scatter.41.cloned.1.call-start = ((), (), s32[]{:S(2)}) async-start(), calls=%async_computation.41 | async-start | bytes 2654208 | tf_op jit(solution)/shard_map/reduce_scatter | solution.py:185
  705.1 83.6 %all-gather.57.cloned.1.call-start = ((), (), s32[]{:S(2)}) async-start(), calls=%async_computation.42 | async-start | bytes 2654208 | tf_op jit(solution)/shard_map/all_gather | solution.py:140
  755.3 81.9 %reduce-scatter.43.cloned.1.call-start = ((), (), s32[]{:S(2)}) async-start(), calls=%async_computation.43 | async-start | bytes 2654208 | tf_op jit(solution)/shard_map/reduce_scatter | solution.py:161
  843.4 79.2 %reduce-scatter.45.cloned.1.call-start = ((), (), s32[]{:S(2)}) async-start(), calls=%async_computation.45 | async-start | bytes 2654208 | tf_op jit(solution)/shard_map/reduce_scatter | solution.py:185
  886.8 74.5 %all-gather.61.cloned.1.call-start = ((), (), s32[]{:S(2)}) async-start(), calls=%async_computation.46 | async-start | bytes 2654208 | tf_op jit(solution)/shard_map/all_gather | solution.py:262
  930.8 78.3 %reduce-scatter.47.cloned.1.call-start = ((), (), s32[]{:S(2)}) async-start(), calls=%async_computation.47 | async-start | bytes 2654208 | tf_op jit(solution)/shard_map/reduce_scatter | solution.py:274
  1014.1 83.8 %reduce-scatter.49.cloned.1.call-start = ((), (), s32[]{:S(2)}) async-start(), calls=%async_computation.49 | async-start | bytes 2654208 | tf_op jit(solution)/shard_map/reduce_scatter | solution.py:339
  1062.1 80.1 %all-gather.65.cloned.1.call-start = ((), (), s32[]{:S(2)}) async-start(), calls=%async_computation.50 | async-start | bytes 2654208 | tf_op jit(solution)/shard_map/all_gather | solution.py:262
  1111.9 79.2 %reduce-scatter.51.cloned.1.call-start = ((), (), s32[]{:S(2)}) async-start(), calls=%async_computation.51 | async-start | bytes 2654208 | tf_op jit(solution)/shard_map/reduce_scatter | solution.py:274
  1196.1 83.6 %reduce-scatter.53.cloned.1.call-start = ((), (), s32[]{:S(2)}) async-start(), calls=%async_computation.53 | async-start | bytes 2654208 | tf_op jit(solution)/shard_map/reduce_scatter | solution.py:339
  1244.2 81.9 %all-gather.69.cloned.1.call-start = ((), (), s32[]{:S(2)}) async-start(), calls=%async_computation.54 | async-start | bytes 2654208 | tf_op jit(solution)/shard_map/all_gather | solution.py:262
  1295.5 79.3 %reduce-scatter.55.cloned.1.call-start = ((), (), s32[]{:S(2)}) async-start(), calls=%async_computation.55 | async-start | bytes 2654208 | tf_op jit(solution)/shard_map/reduce_scatter | solution.py:274
  1379.8 83.7 %reduce-scatter.57.cloned.1.call-start = ((), (), s32[]{:S(2)}) async-start(), calls=%async_computation.57 | async-start | bytes 2654208 | tf_op jit(solution)/shard_map/reduce_scatter | solution.py:339
  1428.0 81.7 %all-gather.73.cloned.1.call-start = ((), (), s32[]{:S(2)}) async-start(), calls=%async_computation.58 | async-start | bytes 2654208 | tf_op jit(solution)/shard_map/all_gather | solution.py:262
  1479.3 79.3 %reduce-scatter.59.cloned.1.call-start = ((), (), s32[]{:S(2)}) async-start(), calls=%async_computation.59 | async-start | bytes 2654208 | tf_op jit(solution)/shard_map/reduce_scatter | solution.py:274
  1562.4 83.7 %reduce-scatter.61.cloned.1.call-start = ((), (), s32[]{:S(2)}) async-start(), calls=%async_computation.61 | async-start | bytes 2654208 | tf_op jit(solution)/shard_map/reduce_scatter | solution.py:339
  1610.6 80.7 %all-gather.77.cloned.1.call-start = ((), (), s32[]{:S(2)}) async-start(), calls=%async_computation.62 | async-start | bytes 2654208 | tf_op jit(solution)/shard_map/all_gather | solution.py:262
  1660.7 78.7 %reduce-scatter.63.cloned.1.call-start = ((), (), s32[]{:S(2)}) async-start(), calls=%async_computation.63 | async-start | bytes 2654208 | tf_op jit(solution)/shard_map/reduce_scatter | solution.py:274
  1706.5 98.5 %all-gather.83.cloned.1.call-start = ((), (), s32[]{:S(2)}) async-start(), calls=%async_computation.73 | async-start | bytes 2654208 | tf_op jit(solution)/shard_map/all_gather | solution.py:289
  1709.0 128.4 %all-gather.95.cloned.1.call-start = ((), (), s32[]{:S(2)}) async-start(), calls=%async_computation.79 | async-start | bytes 2654208 | tf_op jit(solution)/shard_map/all_gather | solution.py:263
  1709.8 159.7 %all-gather.85.cloned.1.call-start = ((), (), s32[]{:S(2)}) async-start(), calls=%async_computation.74 | async-start | bytes 2654208 | tf_op jit(solution)/shard_map/all_gather | solution.py:289
  1710.5 191.7 %all-gather.97.cloned.1.call-start = ((), (), s32[]{:S(2)}) async-start(), calls=%async_computation.80 | async-start | bytes 2654208 | tf_op jit(solution)/shard_map/all_gather | solution.py:263
  1711.1 223.5 %all-gather.87.cloned.1.call-start = ((), (), s32[]{:S(2)}) async-start(), calls=%async_computation.75 | async-start | bytes 2654208 | tf_op jit(solution)/shard_map/all_gather | solution.py:289
  1711.9 255.0 %all-gather.99.cloned.1.call-start = ((), (), s32[]{:S(2)}) async-start(), calls=%async_computation.81 | async-start | bytes 2654208 | tf_op jit(solution)/shard_map/all_gather | solution.py:263
  1712.4 286.7 %all-gather.91.cloned.1.call-start = ((), (), s32[]{:S(2)}) async-start(), calls=%async_computation.77 | async-start | bytes 2654208 | tf_op jit(solution)/shard_map/all_gather | solution.py:263
  1713.0 318.4 %all-gather.79.cloned.1.call-start = ((), (), s32[]{:S(2)}) async-start(), calls=%async_computation.64 | async-start | bytes 2654208 | tf_op jit(solution)/shard_map/all_gather | solution.py:288
  1743.3 320.4 %all-gather.89.cloned.1.call-start = ((), (), s32[]{:S(2)}) async-start(), calls=%async_computation.76 | async-start | bytes 2654208 | tf_op jit(solution)/shard_map/all_gather | solution.py:289
  1743.9 352.1 %all-gather.81.cloned.1.call-start = ((), (), s32[]{:S(2)}) async-start(), calls=%async_computation.72 | async-start | bytes 2654208 | tf_op jit(solution)/shard_map/all_gather | solution.py:289
  1747.3 379.7 %reduce-scatter.77.cloned.1.call-start = ((), (), s32[]{:S(2)}) async-start(), calls=%async_computation.71 | async-start | bytes 1572864 | tf_op jit(solution)/shard_map/reduce_scatter | solution.py:404
  1884.4 256.9 %reduce-scatter.75.cloned.1.call-start = ((), (), s32[]{:S(2)}) async-start(), calls=%async_computation.70 | async-start | bytes 1572864 | tf_op jit(solution)/shard_map/reduce_scatter | solution.py:401
  2006.2 149.6 %reduce-scatter.73.cloned.1.call-start = ((), (), s32[]{:S(2)}) async-start(), calls=%async_computation.69 | async-start | bytes 393216 | tf_op jit(solution)/shard_map/reduce_scatter | solution.py:398
  2059.3 111.0 %reduce-scatter.71.cloned.1.call-start = ((), (), s32[]{:S(2)}) async-start(), calls=%async_computation.68 | async-start | bytes 393216 | tf_op jit(solution)/shard_map/reduce_scatter | solution.py:395
  2102.2 82.6 %reduce-scatter.69.cloned.1.call-start = ((), (), s32[]{:S(2)}) async-start(), calls=%async_computation.67 | async-start | bytes 393216 | tf_op jit(solution)/shard_map/reduce_scatter | solution.py:392
  2102.9 96.5 %reduce-scatter.67.cloned.1.call-start = ((), (), s32[]{:S(2)}) async-start(), calls=%async_computation.66 | async-start | bytes 393216 | tf_op jit(solution)/shard_map/reduce_scatter | solution.py:389
  2103.7 134.3 %reduce-scatter.65.cloned.1.call-start = ((), (), s32[]{:S(2)}) async-start(), calls=%async_computation.65 | async-start | bytes 2654208 | tf_op jit(solution)/shard_map/reduce_scatter | solution.py:339
  (307 other events, 6374.0 us)
Sparse Core Ops, SparseCore 0:
  20.2 34.3 all-gather.40
  70.0 35.3 reduce-scatter.26
  113.1 30.8 all-gather.42
  157.9 35.3 reduce-scatter.28
  209.1 33.0 all-gather.44
  255.5 35.4 reduce-scatter.30
  297.4 30.7 all-gather.46
  341.1 35.2 reduce-scatter.32
  391.2 33.3 all-gather.48
  437.8 35.3 reduce-scatter.34
  479.4 30.8 all-gather.50
  523.1 35.3 reduce-scatter.36
  573.5 33.0 all-gather.52
  619.8 35.3 reduce-scatter.38
  661.5 30.7 all-gather.54
  705.2 35.4 reduce-scatter.40
  755.4 33.1 all-gather.56
  801.8 35.3 reduce-scatter.42
  843.5 30.7 all-gather.58
  886.9 35.5 reduce-scatter.44
  930.9 30.3 all-gather.60
  973.3 35.7 reduce-scatter.46
  1014.2 30.7 all-gather.62
  1062.3 35.6 reduce-scatter.48
  1155.5 35.5 reduce-scatter.50
  1196.2 30.5 all-gather.66
  1244.3 35.3 reduce-scatter.52
  1295.6 30.3 all-gather.68
  1339.4 35.3 reduce-scatter.54
  1379.9 30.7 all-gather.70
  1428.1 35.3 reduce-scatter.56
  1523.2 35.3 reduce-scatter.58
  1562.5 30.8 all-gather.74
  1610.7 35.3 reduce-scatter.60
  1660.8 30.4 all-gather.76
  1704.0 35.3 reduce-scatter.62
  1740.9 31.1 all-gather.92
  1774.3 30.7 all-gather.82
  1806.7 30.7 all-gather.94
  1839.1 30.3 all-gather.84
  1870.9 31.2 all-gather.96
  1903.9 30.7 all-gather.86
  1936.1 30.7 all-gather.98
  1968.4 30.7 all-gather.90
  2000.7 30.7 all-gather.78
  2032.9 30.7 all-gather.88
  2065.2 30.7 all-gather.80
  2201.7 36.2 reduce-scatter.64
  (8 shorter events, 146.4 us)
where the time goes:
time: 2320 us; the launch traced here: 2310 us
  waiting for transfers between devices  1560 us (67%)
  matrix products  339 us (15%)
  other arithmetic  207 us (9%)
  local copies, waits for them, and re-layouts  106 us (5%)
  blocking collectives  60.7 us (3%)
  starting transfers between devices  25.8 us (1%)
    reduce_scatter x5, waiting for transfers between devices, per_device(): lax.psum_scatter(jnp.einsum('tsc,dc->tsd', grad_qkv, joined, preferred_el...  179 us
    reduce_scatter x5, waiting for transfers between devices, per_device(): lax.psum_scatter(jnp.einsum('tsh,hd->tsd', forward_mixed_low, out_weight,...  173 us
    reduce_scatter x5, waiting for transfers between devices, per_device(): lax.psum_scatter(jnp.einsum('tsf,df->tsd', grad_pre, ffn_in, preferred_el...  160 us
    reduce_scatter x5, waiting for transfers between devices, per_device(): lax.psum_scatter(jnp.einsum('tsf,fd->tsd', forward_hidden, ffn_out, prefe...  160 us
    all_gather x5, waiting for transfers between devices, per_device(): lax.all_gather(forward_rounded, 'tensor', axis=0, tiled=True)  147 us
    all_gather x5, waiting for transfers between devices, per_device(): lax.all_gather(forward_first_low, 'tensor', axis=0, tiled=True)  145 us
    all_gather x5, waiting for transfers between devices, per_device(): ffn_grad_all = lax.all_gather(grad_ffn, 'tensor', axis=0, tiled=True)  130 us
    all_gather x5, waiting for transfers between devices, per_device(): branch_all = lax.all_gather(grad_branch, 'tensor', axis=0, tiled=True)  127 us
  transfers between devices with their start and end apart: 64, of which 63 were waited for; matrix products, arithmetic and copies ran while one was open for 10% of the time, Pallas kernels for 0%

commit v1 on v0

v1 whole, which is shorter than its diff:
```python
import functools
import math

import jax
import jax.numpy as jnp
from jax import lax
from jax.experimental import pallas as pl
from jax.experimental.pallas import tpu as pltpu
from jax.sharding import Mesh
from jax.sharding import PartitionSpec as P

HDIM = 64
SEQ_LEN = 1152
STEPS = 5000
PAIR = 2 * HDIM
TILE = 128
WIDTHS = (2, 3, 4, 5, 6, 7, 9)
LOG2E = math.log2(math.e)
SCALE = 1.0 / math.sqrt(HDIM)
TENSOR = ("zs", "tp")

epsilon = 1e-05
f32 = jnp.float32
bf16 = jnp.bfloat16


def received(shard, axis, by):
    size = lax.axis_size(axis)
    by = by % size
    if by == 0:
        return shard
    return lax.ppermute(shard, axis, [((i + by) % size, i) for i in range(size)])


def passed_along(shard, axis, by):
    size = lax.axis_size(axis)
    pairs = [(i, i + by) for i in range(size) if 0 <= i + by < size]
    return lax.ppermute(shard, axis, pairs)


def summed_over(values, axis):
    total = values
    for by in range(1, lax.axis_size(axis)):
        total = total + received(values, axis, by)
    return total


def after(value, *others):
    return lax.optimization_barrier((value, *others))[0]


def norm_parts(summed):
    centered = summed - jnp.mean(summed, axis=-1, keepdims=True)
    inverse = lax.rsqrt(jnp.mean(centered * centered, axis=-1, keepdims=True) + epsilon)
    return (centered * inverse, inverse)


def norm_back(upstream, normed, inverse, gain):
    scaled = upstream * gain
    return inverse * (
        scaled
        - jnp.mean(scaled, axis=-1, keepdims=True)
        - normed * jnp.mean(scaled * normed, axis=-1, keepdims=True)
    )


def token_sum(values):
    return jnp.sum(values.astype(f32), axis=0)


def mm(a, b, dims=((1,), (0,))):
    return lax.dot_general(a, b, (dims, ((), ())), preferred_element_type=f32)


def key_spans(item_ends, length):
    tiles = length // TILE
    first = jnp.arange(tiles, dtype=jnp.int32)[:, None] * TILE
    ends = item_ends[None, :]
    start = jnp.max(jnp.where(ends <= first, ends, 0), axis=1) // TILE
    end = jnp.min(jnp.where(ends > first + TILE - 1, ends, length), axis=1)
    need = (end + TILE - 1) // TILE - start
    widths = jnp.array([min(w, tiles) for w in WIDTHS], jnp.int32)
    kind = jnp.sum((widths[None, :] < need[:, None]).astype(jnp.int32), axis=1)
    is_kind = jnp.arange(len(WIDTHS), dtype=jnp.int32)[None, :] == kind[:, None]
    width = jnp.sum(jnp.where(is_kind, widths[None, :], 0), axis=1)
    return jnp.stack([kind, jnp.minimum(start, tiles - width) * TILE]).astype(jnp.int32)


def place(order, source, target, rows, by_position):
    for block in range(source.shape[0] // rows):
        at = pl.ds(pl.multiple_of(order[block] * rows, 16), rows)
        if by_position:
            target[at, :] = source[block * rows : (block + 1) * rows, :]
        else:
            target[block * rows : (block + 1) * rows, :] = source[at, :]


def two_heads(pair):
    first = lax.broadcasted_iota(jnp.int32, pair.shape, 1) < HDIM
    zero = jnp.zeros_like(pair)
    return jnp.concatenate([jnp.where(first, pair, zero), jnp.where(first, zero, pair)], axis=0)


def one_pair(stacked):
    half = stacked.shape[0] // 2
    first = lax.broadcasted_iota(jnp.int32, (half, stacked.shape[1]), 1) < HDIM
    return jnp.where(first, stacked[:half], stacked[half:])


def each_tile(span, length, body):
    tiles = length // TILE

    def step(tile, carry):
        at = pl.ds(pl.multiple_of(tile * TILE, TILE), TILE)

        def branch(width):
            count = min(width, tiles) * TILE
            return lambda: body(at, pl.ds(pl.multiple_of(span[1, tile], TILE), count))

        lax.switch(span[0, tile], [branch(width) for width in WIDTHS])
        return carry

    lax.fori_loop(0, tiles, step, 0)


def attend_kernel(
    rows, order, span, seg_c, seg_r, q_ref, k_ref, v_ref, mixed_ref, lse_ref, q_s, k_s, v_s, mixed_s
):
    for source, target in ((q_ref, q_s), (k_ref, k_s), (v_ref, v_s)):
        place(order, source, target, rows, True)

    def body(at, to):
        same_item = seg_c[at, :] == seg_r[:, to]
        same_item = jnp.concatenate([same_item, same_item], axis=0)
        for pair in range(q_ref.shape[1] // PAIR):
            cols = slice(pair * PAIR, (pair + 1) * PAIR)
            scores = mm(two_heads(q_s[at, cols]), k_s[to, cols], ((1,), (1,))) * (SCALE * LOG2E)
            scores = jnp.where(same_item, scores, -1e30)
            top = jnp.max(scores, axis=1, keepdims=True)
            weights = jnp.exp2(scores - top)
            total = jnp.sum(weights, axis=1, keepdims=True)
            mixed = mm(weights.astype(bf16), v_s[to, cols]) * (1.0 / total)
            mixed_s[at, cols] = one_pair(mixed).astype(bf16)
            sums = top + jnp.log2(total)
            spread = one_pair(jnp.broadcast_to(sums, (2 * TILE, PAIR))).T
            lse_ref[pair, 0:1, at] = spread[0:1]
            lse_ref[pair, 1:2, at] = spread[HDIM : HDIM + 1]

    each_tile(span, q_ref.shape[0], body)
    place(order, mixed_s, mixed_ref, rows, False)


def attend(qkv, segment, span, order, rows):
    length, width = qkv.shape[0], qkv.shape[1] // 3
    pairs = width // PAIR
    small = pl.BlockSpec(memory_space=pltpu.SMEM)
    third = lambda i: pl.BlockSpec((length, width), lambda h: (0, i))
    return pl.pallas_call(
        functools.partial(attend_kernel, rows),
        grid=(1,),
        in_specs=[
            small,
            small,
            pl.BlockSpec((length, 1), lambda h: (0, 0)),
            pl.BlockSpec((1, length), lambda h: (0, 0)),
            third(0),
            third(1),
            third(2),
        ],
        out_specs=[third(0), pl.BlockSpec((pairs, 2, length), lambda h: (0, 0, 0))],
        out_shape=[
            jax.ShapeDtypeStruct((length, width), bf16),
            jax.ShapeDtypeStruct((pairs, 2, length), f32),
        ],
        scratch_shapes=[pltpu.VMEM((length, width), bf16)] * 4,
        compiler_params=pltpu.CompilerParams(vmem_limit_bytes=48 * 1024 * 1024),
        cost_estimate=pl.CostEstimate(
            flops=8 * length * length * width,
            bytes_accessed=8 * length * width,
            transcendentals=2 * pairs * length * length,
        ),
    )(order, span, segment[:, None], segment[None, :], qkv, qkv, qkv)


def attend_back_kernel(
    rows, order, span, seg_c, seg_r, q_ref, k_ref, v_ref, up_ref, lse_ref, dq_ref, dk_ref, dv_ref,
    q_s, k_s, v_s, up_s, dq_s, dk_s, dv_s,
):
    for source, target in ((q_ref, q_s), (k_ref, k_s), (v_ref, v_s), (up_ref, up_s)):
        place(order, source, target, rows, True)
    dk_s[...] = jnp.zeros_like(dk_s)
    dv_s[...] = jnp.zeros_like(dv_s)

    def body(at, to):
        same_item = seg_c[to, :] == seg_r[:, at]
        same_item = jnp.concatenate([same_item, same_item], axis=1)
        for pair in range(q_ref.shape[1] // PAIR):
            cols = slice(pair * PAIR, (pair + 1) * PAIR)
            keys_all = k_s[to, cols]
            queries, upstream = two_heads(q_s[at, cols]), two_heads(up_s[at, cols])
            lse = jnp.concatenate([lse_ref[pair, 0:1, at], lse_ref[pair, 1:2, at]], axis=1)
            scores = mm(keys_all, queries, ((1,), (1,))) * (SCALE * LOG2E)
            probs = jnp.where(same_item, jnp.exp2(scores - lse), 0.0)
            grad_probs = mm(v_s[to, cols], upstream, ((1,), (1,)))
            weighted = probs * grad_probs
            inner = jnp.sum(weighted, axis=0, keepdims=True)
            grad_scores = (weighted - probs * inner).astype(bf16)
            dv_s[to, cols] += mm(probs.astype(bf16), upstream)
            dk_s[to, cols] += mm(grad_scores, queries)
            dq_s[at, cols] = (one_pair(mm(grad_scores, keys_all, ((0,), (0,)))) * SCALE).astype(bf16)

    each_tile(span, q_ref.shape[0], body)
    q_s[...] = (dk_s[...] * SCALE).astype(bf16)
    v_s[...] = dv_s[...].astype(bf16)
    for source, target in ((dq_s, dq_ref), (q_s, dk_ref), (v_s, dv_ref)):
        place(order, source, target, rows, False)


def attend_back(qkv, segment, span, order, rows, grad_mixed, lse):
    length, width = grad_mixed.shape
    pairs = width // PAIR
    small = pl.BlockSpec(memory_space=pltpu.SMEM)
    third = lambda i: pl.BlockSpec((length, width), lambda h: (0, i))
    return pl.pallas_call(
        functools.partial(attend_back_kernel, rows),
        grid=(1,),
        in_specs=[
            small,
            small,
            pl.BlockSpec((length, 1), lambda h: (0, 0)),
            pl.BlockSpec((1, length), lambda h: (0, 0)),
            third(0),
            third(1),
            third(2),
            third(0),
            pl.BlockSpec((pairs, 2, length), lambda h: (0, 0, 0)),
        ],
        out_specs=[third(0)] * 3,
        out_shape=[jax.ShapeDtypeStruct((length, width), bf16)] * 3,
        scratch_shapes=[pltpu.VMEM((length, width), bf16)] * 5 + [pltpu.VMEM((length, width), f32)] * 2,
        compiler_params=pltpu.CompilerParams(vmem_limit_bytes=48 * 1024 * 1024),
        cost_estimate=pl.CostEstimate(
            flops=20 * length * length * width,
            bytes_accessed=16 * length * width,
            transcendentals=2 * pairs * length * length,
        ),
    )(order, span, segment[:, None], segment[None, :], qkv, qkv, qkv, grad_mixed, lse)


def gelu_parts(pre):
    size = jnp.abs(pre)
    t = 1.0 / (1.0 + (0.3275911 * math.sqrt(0.5)) * size)
    bell = jnp.exp2((-0.5 * LOG2E) * (pre * pre))
    poly = t * (0.127414796 + t * (-0.142248368 + t * (0.7107068705 + t * (-0.7265760135 + t * 0.5307027145))))
    below = poly * bell
    below = jnp.where(pre >= 0, 1.0 - below, below)
    return pre * below, below + (pre * bell) * (1.0 / math.sqrt(2.0 * math.pi))


def widen_kernel(chunk, x_ref, w_ref, bias_ref, hidden_ref, slope_ref):
    for at in range(0, x_ref.shape[0], chunk):
        rows = slice(at, at + chunk)
        hidden, slope = gelu_parts(mm(x_ref[rows, :], w_ref[...]) + bias_ref[...])
        hidden_ref[rows, :] = hidden.astype(bf16)
        slope_ref[rows, :] = slope.astype(bf16)


def widen(x, weight, bias):
    count, width = x.shape
    units = weight.shape[1]
    step = 256
    return pl.pallas_call(
        functools.partial(widen_kernel, 144),
        grid=(units // step,),
        in_specs=[
            pl.BlockSpec((count, width), lambda i: (0, 0)),
            pl.BlockSpec((width, step), lambda i: (0, i)),
            pl.BlockSpec((1, step), lambda i: (0, i)),
        ],
        out_specs=[pl.BlockSpec((count, step), lambda i: (0, i))] * 2,
        out_shape=[jax.ShapeDtypeStruct((count, units), bf16)] * 2,
        compiler_params=pltpu.CompilerParams(vmem_limit_bytes=48 * 1024 * 1024),
        cost_estimate=pl.CostEstimate(
            flops=2 * count * width * units,
            bytes_accessed=2 * (width * units + 2 * count * units),
            transcendentals=2 * count * units,
        ),
    )(x, weight, bias[None])


def per_device(
    states,
    cotangent,
    lengths,
    timesteps,
    time_weight,
    time_bias,
    query_weight,
    query_bias,
    key_weight,
    value_weight,
    value_bias,
    out_weight,
    out_bias,
    attn_gain,
    attn_shift,
    ffn_in,
    ffn_in_bias,
    ffn_out,
    ffn_out_bias,
    ffn_gain,
    ffn_shift,
):
    rows, seqs, width = states.shape
    own_count = seqs * rows
    sections, section_at = lax.axis_size("pipe"), lax.axis_index("pipe")
    dp_size, dp_at = lax.axis_size("dp"), lax.axis_index("dp")
    zs_at = lax.axis_index("zs")
    tp_size, tp_at = lax.axis_size("tp"), lax.axis_index("tp")
    length = own_count * tp_size
    part = width // dp_size
    head_cols, unit_cols = query_weight.shape[2], ffn_in.shape[2]
    heads_all, units_all = head_cols * seqs, unit_cols * seqs

    def rotated(array, axis=-1):
        axis = axis % array.ndim
        twice = jnp.concatenate([array, array], axis=axis)
        return lax.dynamic_slice_in_dim(twice, dp_at * part, width, axis)

    def straightened(array):
        twice = jnp.concatenate([array, array], axis=-1)
        back = (dp_size - dp_at) % dp_size
        return lax.dynamic_slice_in_dim(twice, back * part, width, array.ndim - 1)

    vectors = rotated(
        jnp.concatenate(
            [time_weight, time_bias, out_bias, attn_gain, attn_shift, ffn_out_bias, ffn_gain, ffn_shift]
        )
    )
    time_weight, time_bias, out_bias, attn_gain = vectors[0], vectors[1], vectors[2], vectors[3]
    attn_shift, ffn_out_bias, ffn_gain, ffn_shift = vectors[4], vectors[5], vectors[6], vectors[7]


    def to_sequence(array):
        by_seq = rotated(jnp.transpose(array, (1, 0, 2)))
        got = []
        for by in range(seqs):
            block = lax.dynamic_index_in_dim(by_seq, (zs_at - by) % seqs, 0, keepdims=False)
            got.append(received(block, "zs", by))
        return got

    def to_positions(array):
        by_block = straightened(array).reshape(seqs, rows, width)
        got = [received(by_block[(seqs - by) % seqs], "zs", by)[None] for by in range(seqs)]
        twice = jnp.concatenate(got + got)
        by_seq = lax.dynamic_slice_in_dim(twice, (seqs - zs_at) % seqs, seqs, 0)
        return jnp.transpose(by_seq, (1, 0, 2))

    item_ends = jnp.cumsum(lax.dynamic_index_in_dim(lengths, zs_at, 0, keepdims=False))
    own_times = lax.dynamic_index_in_dim(timesteps, zs_at, 0, keepdims=False).astype(f32)
    member = (tp_at + jnp.arange(tp_size, dtype=jnp.int32)) % tp_size
    chips = (zs_at + jnp.arange(seqs, dtype=jnp.int32)) % seqs
    order = (chips[None, :] * tp_size + member[:, None]).reshape(seqs * tp_size).astype(jnp.int32)

    def segment_at(places):
        return jnp.sum((item_ends[None, :] <= places[:, None]).astype(jnp.int32), axis=1)

    segment = segment_at(jnp.arange(length, dtype=jnp.int32))
    span = key_spans(item_ends, length)
    own_places = order[:seqs, None] * rows + jnp.arange(rows, dtype=jnp.int32)[None, :]
    own_segment = segment_at(own_places.reshape(own_count))
    own_pick = own_segment[:, None] == jnp.arange(lengths.shape[1], dtype=jnp.int32)[None, :]
    time_rows = (jnp.sum(jnp.where(own_pick, own_times[None, :], 0.0), axis=1) / STEPS)[:, None]
    aligned = rows % 16 == 0
    kernel_rows = rows if aligned else length
    kernel_order = order if aligned else jnp.zeros((1,), jnp.int32)

    def by_position(array):
        if aligned:
            return array
        blocks = array.reshape(seqs * tp_size, rows, array.shape[1])
        return jnp.take(blocks, jnp.argsort(order), axis=0).reshape(array.shape)

    def by_distance(array):
        if aligned:
            return array
        blocks = array.reshape(seqs * tp_size, rows, array.shape[1])
        return jnp.take(blocks, order, axis=0).reshape(array.shape)


    def over_zs(block, axis, *before):
        mine = lax.dynamic_slice_in_dim(block, dp_at * part, part, axis)
        mine = after(mine, *before)
        return [received(mine, "zs", by) for by in range(1, seqs)]

    def over_dp(pieces):
        return [[received(piece, "dp", other) for other in range(dp_size)] for piece in pieces]

    def assembled(block, axis, pieces, thirds):
        across = 1 - axis
        each = block.shape[across] // thirds
        shape = [0, 0]
        shape[axis], shape[across] = width, block.shape[across] * seqs
        whole = jnp.zeros(shape, block.dtype)

        def put(whole, piece, slot, at):
            for third in range(thirds):
                start = [0, 0]
                start[axis], start[across] = at, (third * seqs + slot) * each
                cut = lax.slice_in_dim(piece, third * each, (third + 1) * each, axis=across)
                whole = lax.dynamic_update_slice(whole, cut, start)
            return whole

        whole = put(whole, rotated(block, axis), 0, 0)
        for slot, row in enumerate(pieces):
            for other, piece in enumerate(row):
                whole = put(whole, piece, slot + 1, other * part)
        return whole

    joined_block = jnp.concatenate([query_weight[0], key_weight[0], value_weight[0]], axis=1)
    biases = jnp.concatenate([query_bias[0], value_bias[0], ffn_in_bias[0].astype(f32)])[None]
    start_pieces = to_sequence(states)
    bias_slots = [received(biases, "zs", by)[0] for by in range(seqs)]
    joined_zs = over_zs(joined_block, 0)
    out_zs = over_zs(out_weight[0], 1, *joined_zs, *start_pieces)
    in_zs = over_zs(ffn_in[0], 0, *out_zs)
    ffn_out_zs = over_zs(ffn_out[0], 1, *in_zs)
    joined = assembled(joined_block, 0, over_dp(joined_zs), 3)
    out_all = assembled(out_weight[0], 1, over_dp(out_zs), 1)
    in_all = assembled(ffn_in[0], 0, over_dp(in_zs), 1)
    ffn_out_all = assembled(ffn_out[0], 1, over_dp(ffn_out_zs), 1)
    query_bias_all = jnp.concatenate([b[:head_cols] for b in bias_slots])
    value_bias_all = jnp.concatenate([b[head_cols : 2 * head_cols] for b in bias_slots])
    in_bias_all = jnp.concatenate([b[2 * head_cols :] for b in bias_slots])
    joined_bias = jnp.concatenate([query_bias_all, jnp.zeros_like(query_bias_all), value_bias_all])

    def everyone(own):
        return jnp.concatenate([received(own, "tp", by) for by in range(tp_size)])

    def returned(full, weight, dims):
        total = 0.0
        for by in range(1, tp_size):
            theirs = mm(full[by * own_count : (by + 1) * own_count], weight, dims).astype(bf16)
            total = total + received(theirs, "tp", -by).astype(f32)
        return total + mm(full[:own_count], weight, dims)

    kept = []
    layer_rows, stat_terms = None, None
    inputs = jnp.concatenate(start_pieces)
    for tick in range(sections):
        residual = inputs.astype(f32) + time_rows * time_weight + time_bias
        rounded_all = everyone(residual.astype(bf16))
        qkv = by_position((mm(rounded_all, joined) + joined_bias).astype(bf16))
        mixed, lse = attend(qkv, segment, span, kernel_order, kernel_rows)
        mixed = by_distance(mixed)
        branch = returned(mixed, out_all, ((1,), (0,))) + out_bias
        first_normed, first_inverse = norm_parts(residual + branch)
        first_out = first_normed * attn_gain + attn_shift
        first_all = everyone(first_out.astype(bf16))
        hidden, slope = widen(first_all, in_all, in_bias_all)
        ffn_branch = returned(hidden, ffn_out_all, ((1,), (0,))) + ffn_out_bias
        second_normed, second_inverse = norm_parts(first_out + ffn_branch)
        layer_y = (second_normed * ffn_gain + ffn_shift).astype(bf16)
        terms = jnp.stack(
            [jnp.sum(residual * residual), jnp.sum(branch * branch), jnp.sum(ffn_branch * ffn_branch)]
        )
        kept.append(
            (
                rounded_all,
                qkv,
                mixed,
                lse,
                first_normed,
                first_inverse,
                first_all,
                hidden,
                slope,
                second_normed,
                second_inverse,
            )
        )
        if tick == 0:
            layer_rows, stat_terms = layer_y, terms
            upstream_pieces = to_sequence(after(cotangent, layer_y))
        else:
            here = section_at == tick
            layer_rows = jnp.where(here, layer_y, layer_rows)
            stat_terms = jnp.where(here, terms, stat_terms)
        if tick + 1 < sections:
            inputs = passed_along(layer_y, "pipe", 1)
    layer_out = to_positions(layer_rows)


    def parts_of(left, right, side):
        found = []
        for other in range(dp_size):
            cut = slice(other * part, (other + 1) * part)
            if side == 0:
                found.append(mm(left[:, cut], right, ((0,), (0,))).astype(bf16))
            else:
                found.append(mm(left, right[:, cut], ((0,), (0,))).astype(bf16))
        return found

    def chosen(found_at, operands):
        if sections == 1:
            return found_at(*operands[0])
        return lax.switch(
            sections - 1 - section_at, [functools.partial(found_at, *each) for each in operands]
        )

    def owned(parts, axis, thirds):
        total = parts[0].astype(f32)
        for other in range(1, dp_size):
            total = total + received(parts[other], "dp", -other).astype(f32)
        each = total.shape[axis] // (seqs * thirds)
        blocks = [
            jnp.concatenate(
                [
                    lax.slice_in_dim(total, (third * seqs + k) * each, (third * seqs + k + 1) * each, axis=axis)
                    for third in range(thirds)
                ],
                axis=axis,
            )
            for k in range(seqs)
        ]
        mine = blocks[0]
        for by in range(1, seqs):
            mine = mine + received(blocks[by].astype(bf16), "zs", -by).astype(f32)
        return mine

    results = None
    upstream_rows = jnp.concatenate(upstream_pieces)
    for_ffn, for_out, for_joined = [], [], []
    for step in range(sections):
        (
            rounded_all,
            qkv,
            mixed,
            lse,
            first_normed,
            first_inverse,
            first_all,
            hidden,
            slope,
            second_normed,
            second_inverse,
        ) = kept[sections - 1 - step]
        last = step + 1 == sections
        upstream = upstream_rows.astype(f32)
        gain_two, shift_two = token_sum(upstream * second_normed), token_sum(upstream)
        grad_second = norm_back(upstream, second_normed, second_inverse, ffn_gain)
        grad_ffn = grad_second.astype(bf16)
        ffn_out_bias_grad = token_sum(grad_ffn)
        grad_ffn_all = everyone(grad_ffn)
        grad_pre = (mm(grad_ffn_all, ffn_out_all, ((1,), (1,))) * slope.astype(f32)).astype(bf16)
        in_bias_sum = token_sum(grad_pre)
        for_ffn.append((hidden, grad_ffn_all, first_all, grad_pre))
        if last:
            ffn_out_parts = chosen(lambda a, b, c, d: parts_of(a, b, 1), for_ffn)
            ffn_in_parts = chosen(lambda a, b, c, d: parts_of(c, d, 0), for_ffn)
            grad_second = after(grad_second, *ffn_out_parts, *ffn_in_parts)
        grad_first = grad_second + returned(grad_pre, in_all, ((1,), (1,)))
        gain_one, shift_one = token_sum(grad_first * first_normed), token_sum(grad_first)
        grad_resid = norm_back(grad_first, first_normed, first_inverse, attn_gain)
        grad_branch = grad_resid.astype(bf16)
        out_bias_grad = token_sum(grad_branch)
        branch_all = everyone(grad_branch)
        grad_mixed = by_position(mm(branch_all, out_all, ((1,), (1,))).astype(bf16))
        for_out.append((mixed, branch_all))
        if last:
            out_parts = chosen(lambda a, b: parts_of(a, b, 1), for_out)
            grad_mixed = after(grad_mixed, *out_parts)
        grads = attend_back(qkv, segment, span, kernel_order, kernel_rows, grad_mixed, lse)
        grad_qkv = jnp.concatenate([by_distance(grad) for grad in grads], axis=1)
        bias_sums = token_sum(grad_qkv)
        for_joined.append((rounded_all, grad_qkv))
        if last:
            joined_parts = chosen(lambda a, b: parts_of(a, b, 0), for_joined)
            grad_resid = after(grad_resid, *joined_parts)
        grad_input = grad_resid + returned(grad_qkv, joined, ((1,), (1,)))
        tw_grad, tb_grad = token_sum(grad_input * time_rows), token_sum(grad_input)
        grad_in = grad_input.astype(bf16)
        slot_sums = jnp.concatenate(
            [
                bias_sums[:heads_all].reshape(seqs, head_cols),
                bias_sums[2 * heads_all :].reshape(seqs, head_cols),
                in_bias_sum.reshape(seqs, unit_cols),
            ],
            axis=1,
        )
        vector_sums = jnp.stack(
            [tw_grad, tb_grad, out_bias_grad, gain_one, shift_one, ffn_out_bias_grad, gain_two, shift_two]
        )
        these = (vector_sums, slot_sums, grad_in)
        if step == 0:
            results = these
        else:
            here = section_at == sections - 1 - step
            results = jax.tree.map(lambda a, b: jnp.where(here, a, b), these, results)
        if not last:
            upstream_rows = passed_along(grad_in, "pipe", -1)
    ffn_out_grad = owned(ffn_out_parts, 0, 1)
    ffn_in_grad = owned(ffn_in_parts, 1, 1)
    out_grad = owned(out_parts, 0, 1)
    joined_grad = owned(joined_parts, 1, 3)
    vector_sums, slot_sums, grad_in = results
    input_grad = to_positions(grad_in)

    stat_row = jnp.concatenate([stat_terms, jnp.zeros((width - 3,), f32)])[None]
    shared = jnp.concatenate([straightened(vector_sums), stat_row])
    shared = summed_over(summed_over(summed_over(shared, "tp"), "zs"), "dp")
    own_slot = slot_sums[0:1]
    for by in range(1, seqs):
        own_slot = own_slot + received(slot_sums[by : by + 1], "zs", -by)
    own_slot = summed_over(own_slot, "dp")
    element_count = float(SEQ_LEN * seqs * dp_size * width)
    stats = jnp.sqrt(shared[8:9, :3] / element_count)
    return (
        layer_out[None],
        input_grad[None],
        shared[0:1],
        shared[1:2],
        joined_grad[None, :, :head_cols],
        own_slot[:, :head_cols],
        joined_grad[None, :, head_cols : 2 * head_cols],
        joined_grad[None, :, 2 * head_cols :],
        own_slot[:, head_cols : 2 * head_cols],
        out_grad[None],
        shared[2:3],
        shared[3:4],
        shared[4:5],
        ffn_in_grad[None],
        own_slot[:, 2 * head_cols :],
        ffn_out_grad[None],
        shared[5:6],
        shared[6:7],
        shared[7:8],
        stats,
    )


def solution(mesh):
    def run(states, *rest):
        sizes = mesh.shape
        seqs = states.shape[1] // sizes["dp"]
        grouped = Mesh(
            mesh.devices.reshape(sizes["pipe"], sizes["dp"], seqs, sizes["tensor"] // seqs),
            ("pipe", "dp", "zs", "tp"),
        )
        return jax.shard_map(
            per_device,
            mesh=grouped,
            in_specs=(
                P(TENSOR, "dp", None),
                P(TENSOR, "dp", None),
                P("dp", None),
                P("dp", None),
                P("pipe", None),
                P("pipe", None),
                P("pipe", None, TENSOR),
                P("pipe", TENSOR),
                P("pipe", None, TENSOR),
                P("pipe", None, TENSOR),
                P("pipe", TENSOR),
                P("pipe", TENSOR, None),
                P("pipe", None),
                P("pipe", None),
                P("pipe", None),
                P("pipe", None, TENSOR),
                P("pipe", TENSOR),
                P("pipe", TENSOR, None),
                P("pipe", None),
                P("pipe", None),
                P("pipe", None),
            ),
            out_specs=(
                P("pipe", TENSOR, "dp", None),
                P("pipe", TENSOR, "dp", None),
                P("pipe", None),
                P("pipe", None),
                P("pipe", "dp", TENSOR),
                P("pipe", TENSOR),
                P("pipe", "dp", TENSOR),
                P("pipe", "dp", TENSOR),
                P("pipe", TENSOR),
                P("pipe", TENSOR, "dp"),
                P("pipe", None),
                P("pipe", None),
                P("pipe", None),
                P("pipe", "dp", TENSOR),
                P("pipe", TENSOR),
                P("pipe", TENSOR, "dp"),
                P("pipe", None),
                P("pipe", None),
                P("pipe", None),
                P("pipe", None),
            ),
            check_vma=False,
        )(states, *rest)

    return run
```

time: 2320 us -> 855 us (0.37)
  waiting for transfers between devices: 1560 us -> 410 us
  matrix products: 339 us -> 112 us
  other arithmetic: 207 us -> 65.3 us
  Pallas kernels: 0 us -> 122 us
  local copies, waits for them, and re-layouts: 106 us -> 36.9 us
  starting transfers between devices: 25.8 us -> 94 us
  blocking collectives: 60.7 us -> 0 us
    all_gather x30 -> x0, waiting for transfers between devices: 771 us -> none  [the longest x5 147 us: per_device(): lax.all_gather(forward_rounded, 'tensor', axis=0, tiled=True)]
    reduce_scatter x26 -> x0, waiting for transfers between devices: 735 us -> none  [the longest x5 179 us: per_device(): lax.psum_scatter(jnp.einsum('tsc,dc->tsd', grad_qkv, joined, preferred_el...]
    ppermute x0 -> x80, waiting for transfers between devices: none -> 382 us  [received(): lax.ppermute(shard, axis, [((i + by) % size, i) for i in range(size)])]
    dot_general x95 -> x30, matrix products: 339 us -> 112 us  [mm(): return lax.dot_general(a, b, (dims, ((), ())), preferred_element_type=f32)]
    pallas_call x0 -> x6, Pallas kernels: none -> 122 us  [the longest x2 54.2 us: attend_back(): pl.pallas_call(functools.partial(attend_back_kernel, rows), grid=(1,), in...]
    ppermute x0 -> x80, starting transfers between devices: none -> 88.2 us  [received(): lax.ppermute(shard, axis, [((i + by) % size, i) for i in range(size)])]
    reduce_sum x52 -> x14, other arithmetic: 79.1 us -> 16.2 us  [the longest x9 15.8 us: token_sum(): return jnp.sum(values.astype(f32), axis=0)]
    psum x1 -> x0, blocking collectives: 60.7 us -> none  [per_device(): lax.psum((grad_time_weight, grad_time_bias, grad_attn_bias, grad_gain_one...]
  transfers between devices with their start and end apart: 64 -> 82, of which waited for: 63 -> 45; matrix products, arithmetic and copies ran while one was open for 10% -> 16% of each run, Pallas kernels for 0% -> 5%
where the time goes in v1:
time: 855 us; the launch traced here: 843 us
  waiting for transfers between devices  410 us (48%)
  Pallas kernels  122 us (14%)
  matrix products  112 us (13%)
  starting transfers between devices  94 us (11%)
  other arithmetic  65.3 us (8%)
  local copies, waits for them, and re-layouts  36.9 us (4%)
    ppermute x80, waiting for transfers between devices, received(): lax.ppermute(shard, axis, [((i + by) % size, i) for i in range(size)])  382 us
    dot_general x30, matrix products, mm(): return lax.dot_general(a, b, (dims, ((), ())), preferred_element_type=f32)  112 us
    ppermute x80, starting transfers between devices, received(): lax.ppermute(shard, axis, [((i + by) % size, i) for i in range(size)])  88.2 us
    pallas_call x2, Pallas kernels, attend_back(): pl.pallas_call(functools.partial(attend_back_kernel, rows), grid=(1,), in...  54.2 us
    pallas_call x2, Pallas kernels, attend(): pl.pallas_call(functools.partial(attend_kernel, rows), grid=(1,), in_spec...  34.9 us
    pallas_call x2, Pallas kernels, widen(): pl.pallas_call(functools.partial(widen_kernel, 144), grid=(units // step,...  32.9 us
    ppermute x2, waiting for transfers between devices, passed_along(): return lax.ppermute(shard, axis, pairs)  27.9 us
    unnamed x277, local copies, waits for them, and re-layouts  20.9 us
  transfers between devices with their start and end apart: 82, of which 45 were waited for; matrix products, arithmetic and copies ran while one was open for 16% of the time, Pallas kernels for 5%

profile of v1, /device:TPU:0, one launch (start us, length us, event | category | flops | bytes accessed | tf_op | source)
XLA Modules:
  0.0 843.4 jit_solution(14237268822136195490)
XLA Ops:
  26.1 13.9 %collective-permute-done.2 = bf16[144,1024]{1,0:T(8,128)(2,1)S(1)} collective-permute-done((bf16[144,1024]{1,0:T(8,128)(2,1)}, bf16[144,1024]{1,0:T(8,128)(2,1)S(1)}, u32[]{:S(2)}, u32[]{:S(2)}) %collective-permute-start.2) | collective-permute-done | bytes 294944 | tf_op jit(solution)/shard_map/ppermute | solution.py:32
  42.9 22.0 %collective-permute-done.1 = bf16[144,1024]{1,0:T(8,128)(2,1)S(1)} collective-permute-done((bf16[144,1024]{1,0:T(8,128)(2,1)}, bf16[144,1024]{1,0:T(8,128)(2,1)S(1)}, u32[]{:S(2)}, u32[]{:S(2)}) %collective-permute-start.1) | collective-permute-done | bytes 294944 | tf_op jit(solution)/shard_map/ppermute | solution.py:32
  65.4 7.8 collective-permute-done.4
  86.2 6.8 collective-permute-done.14
  95.5 14.2 %collective-permute-done.16 = bf16[128,512]{1,0:T(8,128)(2,1)S(1)} collective-permute-done((bf16[128,512]{1,0:T(8,128)(2,1)S(1)}, bf16[128,512]{1,0:T(8,128)(2,1)S(1)}, u32[]{:S(2)}, u32[]{:S(2)}) %collective-permute-start.16) | collective-permute-done | bytes 131104 | tf_op jit(solution)/shard_map/ppermute | solution.py:32
  123.0 5.0 fusion.32.q_ref.k_ref.v_ref
  128.1 17.1 %shard_map.365 = (bf16[1152,512]{1,0:T(8,128)(2,1)S(1)}, f32[4,2,1152]{2,1,0:T(2,128)S(1)}) custom-call(s32[8]{0:T(128)S(1)} %add.505.order, s32[2,9]{1,0:T(2,128)S(1)} %pad_add_fusion.span, s32[1152,1]{1,0:T(8,128)S(1)} %broadcast_in_dim.174.seg_c, s32[1,1152]{1,0:T(1,128)S(1)} %broadcast_in_dim.87.seg_r, bf16[1152,1536]{1,0:T(8,128)(2,1)S(1)} %fusion.32.q_ref.k_ref.v_ref, ...), custom_call_target="tpu_custom_call" | custom-call | flops 5435817984 | bytes 4718592 | tf_op jit(solution)/shard_map/pallas_call | solution.py:158
  151.1 11.9 %collective-permute-done.25 = bf16[512,512]{1,0:T(8,128)(2,1)S(1)} collective-permute-done((bf16[512,512]{1,0:T(8,128)(2,1)S(1)}, bf16[512,512]{1,0:T(8,128)(2,1)S(1)}, u32[]{:S(2)}, u32[]{:S(2)}) %collective-permute-start.25) | collective-permute-done | bytes 524320 | tf_op jit(solution)/shard_map/ppermute | solution.py:32
  163.0 21.9 %collective-permute-done.23 = bf16[512,512]{1,0:T(8,128)(2,1)S(1)} collective-permute-done((bf16[512,512]{1,0:T(8,128)(2,1)S(1)}, bf16[512,512]{1,0:T(8,128)(2,1)S(1)}, u32[]{:S(2)}, u32[]{:S(2)}) %collective-permute-start.23) | collective-permute-done | bytes 524320 | tf_op jit(solution)/shard_map/ppermute | solution.py:32
  193.0 18.7 %collective-permute-done.27 = bf16[512,512]{1,0:T(8,128)(2,1)S(1)} collective-permute-done((bf16[512,512]{1,0:T(8,128)(2,1)S(1)}, bf16[512,512]{1,0:T(8,128)(2,1)S(1)}, u32[]{:S(2)}, u32[]{:S(2)}) %collective-permute-start.27) | collective-permute-done | bytes 524320 | tf_op jit(solution)/shard_map/ppermute | solution.py:32
  216.6 10.0 %collective-permute-done.24 = bf16[512,512]{1,0:T(8,128)(2,1)S(1)} collective-permute-done((bf16[512,512]{1,0:T(8,128)(2,1)S(1)}, bf16[512,512]{1,0:T(8,128)(2,1)S(1)}, u32[]{:S(2)}, u32[]{:S(2)}) %collective-permute-start.24) | collective-permute-done | bytes 524320 | tf_op jit(solution)/shard_map/ppermute | solution.py:32
  232.7 5.1 collective-permute-done.28
  237.9 20.0 %collective-permute-done.30 = bf16[512,512]{1,0:T(8,128)(2,1)S(1)} collective-permute-done((bf16[512,512]{1,0:T(8,128)(2,1)S(1)}, bf16[512,512]{1,0:T(8,128)(2,1)S(1)}, u32[]{:S(2)}, u32[]{:S(2)}) %collective-permute-start.30) | collective-permute-done | bytes 524320 | tf_op jit(solution)/shard_map/ppermute | solution.py:32
  258.4 15.7 %shard_map.366 = (bf16[1152,2048]{1,0:T(8,128)(2,1)}, bf16[1152,2048]{1,0:T(8,128)(2,1)}) custom-call(bf16[1152,1024]{1,0:T(8,128)(2,1)S(1)} %pad_maximum_fusion.1.x_ref, bf16[1024,2048]{1,0:T(8,128)(2,1)S(1)} %constant_dynamic-update-slice_fusion.21.w_ref, f32[1,2048]{1,0:T(1,128)S(1)} %bitcast.216), custom_call_target="tpu_custom_call" | custom-call | flops 4831838208 | bytes 13631488 | tf_op jit(solution)/shard_map/pallas_call | solution.py:272
  274.0 4.5 fusion.88
  281.4 4.4 fusion.185
  286.7 4.4 collective-permute-start.34
  291.0 25.0 %collective-permute-done.34 = bf16[576,1024]{1,0:T(8,128)(2,1)S(1)} collective-permute-done((bf16[576,1024]{1,0:T(8,128)(2,1)S(1)}, bf16[576,1024]{1,0:T(8,128)(2,1)S(1)}, u32[]{:S(2)}, u32[]{:S(2)}) %collective-permute-start.34) | collective-permute-done | bytes 1179680 | tf_op jit(solution)/shard_map/ppermute | solution.py:38
  320.4 5.0 fusion.33.q_ref.k_ref.v_ref
  325.5 17.8 %shard_map.367 = (bf16[1152,512]{1,0:T(8,128)(2,1)}, f32[4,2,1152]{2,1,0:T(2,128)S(1)}) custom-call(s32[8]{0:T(128)S(1)} %add.505.order, s32[2,9]{1,0:T(2,128)S(1)} %pad_add_fusion.span, s32[1152,1]{1,0:T(8,128)S(1)} %broadcast_in_dim.174.seg_c, s32[1,1152]{1,0:T(1,128)S(1)} %broadcast_in_dim.87.seg_r, bf16[1152,1536]{1,0:T(8,128)(2,1)S(1)} %fusion.33.q_ref.k_ref.v_ref, ...), custom_call_target="tpu_custom_call" | custom-call | flops 5435817984 | bytes 4718592 | tf_op jit(solution)/shard_map/pallas_call | solution.py:158
  355.6 17.2 %shard_map.368 = (bf16[1152,2048]{1,0:T(8,128)(2,1)}, bf16[1152,2048]{1,0:T(8,128)(2,1)}) custom-call(bf16[1152,1024]{1,0:T(8,128)(2,1)} %pad_maximum_fusion.3.x_ref, bf16[1024,2048]{1,0:T(8,128)(2,1)S(1)} %constant_dynamic-update-slice_fusion.21.w_ref, f32[1,2048]{1,0:T(1,128)S(1)} %bitcast.217), custom_call_target="tpu_custom_call" | custom-call | flops 4831838208 | bytes 13631488 | tf_op jit(solution)/shard_map/pallas_call | solution.py:272
  372.9 4.5 fusion.91
  390.8 7.2 collective-permute-done.42
  398.0 8.2 collective-permute-done.43
  412.3 7.7 convert_reduce_fusion
  436.0 27.2 %shard_map.369 = (bf16[1152,512]{1,0:T(8,128)(2,1)S(1)}, bf16[1152,512]{1,0:T(8,128)(2,1)S(1)}, bf16[1152,512]{1,0:T(8,128)(2,1)S(1)}) custom-call(s32[8]{0:T(128)S(1)} %add.505.order, s32[2,9]{1,0:T(2,128)S(1)} %pad_add_fusion.span, s32[1152,1]{1,0:T(8,128)S(1)} %broadcast_in_dim.174.seg_c, s32[1,1152]{1,0:T(1,128)S(1)} %broadcast_in_dim.87.seg_r, ...), custom_call_target="tpu_custom_call" | custom-call | flops 13589544960 | bytes 9437184 | tf_op jit(solution)/shard_map/pallas_call | solution.py:224
  483.6 7.3 collective-permute-done.39
  490.9 14.9 %collective-permute-done.40 = bf16[144,1024]{1,0:T(8,128)(2,1)S(1)} collective-permute-done((bf16[144,1024]{1,0:T(8,128)(2,1)S(1)}, bf16[144,1024]{1,0:T(8,128)(2,1)S(1)}, u32[]{:S(2)}, u32[]{:S(2)}) %collective-permute-start.40) | collective-permute-done | bytes 294944 | tf_op jit(solution)/shard_map/ppermute | solution.py:32
  515.6 5.8 convert_reduce_fusion.1
  531.4 10.6 %conditional.9 = (bf16[512,2048]{1,0:T(8,128)(2,1)S(1)}, bf16[512,2048]{1,0:T(8,128)(2,1)}) conditional(s32[]{:T(128)} %clamp.54, (bf16[1152,1024]{1,0:T(8,128)(2,1)}, bf16[1152,2048]{1,0:T(8,128)(2,1)}) %tuple.189, (bf16[1152,1024]{1,0:T(8,128)(2,1)}, bf16[1152,2048]{1,0:T(8,128)(2,1)}) %tuple.190), branch_computations={%region_24.25_spmd, %region_25.26_spmd} | conditional | flops 4831838208 | bytes 44302408 | solution.py:650
  531.5 7.1 fusion.12
  545.1 10.0 %conditional.8 = (bf16[2048,512]{1,0:T(8,128)(2,1)S(1)}, bf16[2048,512]{1,0:T(8,128)(2,1)}) conditional(s32[]{:T(128)} %clamp.54, (bf16[1152,1024]{1,0:T(8,128)(2,1)S(1)}, bf16[1152,2048]{1,0:T(8,128)(2,1)}) %tuple.186, (bf16[1152,1024]{1,0:T(8,128)(2,1)S(1)}, bf16[1152,2048]{1,0:T(8,128)(2,1)}) %tuple.64), branch_computations={%region_22.23_spmd, %region_23.24_spmd} | conditional | flops 4831838208 | bytes 34865196 | solution.py:650
  545.1 6.8 fusion.4
  556.4 7.9 multiply_reduce_fusion.8
  566.5 25.7 %collective-permute-done.74 = bf16[512,2048]{1,0:T(8,128)(2,1)} collective-permute-done((bf16[512,2048]{1,0:T(8,128)(2,1)}, bf16[512,2048]{1,0:T(8,128)(2,1)}, u32[]{:S(2)}, u32[]{:S(2)}) %collective-permute-start.74) | collective-permute-done | bytes 2097184 | tf_op jit(solution)/shard_map/ppermute | solution.py:32
  592.2 4.5 fusion.174
  601.8 34.3 %collective-permute-done.78 = bf16[2048,512]{1,0:T(8,128)(2,1)S(1)} collective-permute-done((bf16[2048,512]{1,0:T(8,128)(2,1)}, bf16[2048,512]{1,0:T(8,128)(2,1)S(1)}, u32[]{:S(2)}, u32[]{:S(2)}) %collective-permute-start.78) | collective-permute-done | bytes 2097184 | tf_op jit(solution)/shard_map/ppermute | solution.py:32
  648.5 27.0 %shard_map.370 = (bf16[1152,512]{1,0:T(8,128)(2,1)S(1)}, bf16[1152,512]{1,0:T(8,128)(2,1)S(1)}, bf16[1152,512]{1,0:T(8,128)(2,1)S(1)}) custom-call(s32[8]{0:T(128)S(1)} %add.505.order, s32[2,9]{1,0:T(2,128)S(1)} %pad_add_fusion.span, s32[1152,1]{1,0:T(8,128)S(1)} %broadcast_in_dim.174.seg_c, s32[1,1152]{1,0:T(1,128)S(1)} %broadcast_in_dim.87.seg_r, ...), custom_call_target="tpu_custom_call" | custom-call | flops 13589544960 | bytes 9437184 | tf_op jit(solution)/shard_map/pallas_call | solution.py:224
  684.6 19.9 %collective-permute-done.67 = f32[1,768]{1,0:T(1,128)S(1)} collective-permute-done((f32[1,768]{1,0:T(1,128)S(1)}, f32[1,768]{1,0:T(1,128)S(1)}, u32[]{:S(2)}, u32[]{:S(2)}) %collective-permute-start.67) | collective-permute-done | bytes 3104 | tf_op jit(solution)/shard_map/ppermute | solution.py:32
  708.4 5.7 conditional.11
  716.6 12.5 %collective-permute-done.76 = bf16[512,512]{1,0:T(8,128)(2,1)S(1)} collective-permute-done((bf16[512,512]{1,0:T(8,128)(2,1)}, bf16[512,512]{1,0:T(8,128)(2,1)S(1)}, u32[]{:S(2)}, u32[]{:S(2)}) %collective-permute-start.76) | collective-permute-done | bytes 524320 | tf_op jit(solution)/shard_map/ppermute | solution.py:32
  733.4 8.5 %collective-permute-start.71 = (bf16[128,512]{1,0:T(8,128)(2,1)S(1)}, bf16[128,512]{1,0:T(8,128)(2,1)S(1)}, u32[]{:S(2)}, u32[]{:S(2)}) collective-permute-start(bf16[128,512]{1,0:T(8,128)(2,1)S(1)} %get-tuple-element.297), channel_id=1, source_target_pairs={{6,0},{0,2},{2,4},{4,6},{7,1},{1,3},{3,5},{5,7},{14,8},{8,10},{10,... | collective-permute-start | bytes 393224 | tf_op jit(solution)/shard_map/ppermute | solution.py:32
  742.1 13.8 %collective-permute-done.80 = bf16[512,512]{1,0:T(8,128)(2,1)S(1)} collective-permute-done((bf16[512,512]{1,0:T(8,128)(2,1)}, bf16[512,512]{1,0:T(8,128)(2,1)S(1)}, u32[]{:S(2)}, u32[]{:S(2)}) %collective-permute-start.80) | collective-permute-done | bytes 524320 | tf_op jit(solution)/shard_map/ppermute | solution.py:32
  758.5 4.3 collective-permute-done.72
  789.1 14.7 %collective-permute-done.54 = bf16[144,1024]{1,0:T(8,128)(2,1)S(1)} collective-permute-done((bf16[144,1024]{1,0:T(8,128)(2,1)S(1)}, bf16[144,1024]{1,0:T(8,128)(2,1)S(1)}, u32[]{:S(2)}, u32[]{:S(2)}) %collective-permute-start.54) | collective-permute-done | bytes 294944 | tf_op jit(solution)/shard_map/ppermute | solution.py:32
  806.9 5.9 collective-permute-start.64
  818.5 12.6 %collective-permute-done.64 = bf16[512,384]{1,0:T(8,128)(2,1)S(1)} collective-permute-done((bf16[512,384]{1,0:T(8,128)(2,1)S(1)}, bf16[512,384]{1,0:T(8,128)(2,1)S(1)}, u32[]{:S(2)}, u32[]{:S(2)}) %collective-permute-start.64) | collective-permute-done | bytes 393248 | tf_op jit(solution)/shard_map/ppermute | solution.py:32
  831.1 11.0 %collective-permute-done.63 = bf16[512,384]{1,0:T(8,128)(2,1)S(1)} collective-permute-done((bf16[512,384]{1,0:T(8,128)(2,1)S(1)}, bf16[512,384]{1,0:T(8,128)(2,1)S(1)}, u32[]{:S(2)}, u32[]{:S(2)}) %collective-permute-start.63) | collective-permute-done | bytes 393248 | tf_op jit(solution)/shard_map/ppermute | solution.py:32
  (622 shorter events, 275.7 us)
Async XLA Ops:
  2.3 22.6 %collective-permute-start.12 = (f32[1,768]{1,0:T(1,128)S(1)}, f32[1,768]{1,0:T(1,128)S(1)}, u32[]{:S(2)}, u32[]{:S(2)}) collective-permute-start(f32[1,768]{1,0:T(1,128)S(1)} %broadcast_in_dim.88), channel_id=1, source_target_pairs={{6,0},{0,2},{2,4},{4,6},{7,1},{1,3},{3,5},{5,7},{14,8},{8,10},{10,... | collective-permute-start | bytes 9224 | tf_op jit(solution)/shard_map/ppermute | solution.py:32
  5.4 19.0 %collective-permute-start.11 = (f32[1,768]{1,0:T(1,128)S(1)}, f32[1,768]{1,0:T(1,128)S(1)}, u32[]{:S(2)}, u32[]{:S(2)}) collective-permute-start(f32[1,768]{1,0:T(1,128)S(1)} %broadcast_in_dim.88), channel_id=1, source_target_pairs={{4,0},{6,2},{0,4},{2,6},{5,1},{7,3},{1,5},{3,7},{12,8},{14,10},{8,... | collective-permute-start | bytes 9224 | tf_op jit(solution)/shard_map/ppermute | solution.py:32
  11.1 54.3 %collective-permute-start.8 = (bf16[512,384]{1,0:T(8,128)(2,1)}, bf16[512,384]{1,0:T(8,128)(2,1)}, u32[]{:S(2)}, u32[]{:S(2)}) collective-permute-start(bf16[512,384]{1,0:T(8,128)(2,1)} %fusion.133), channel_id=1, source_target_pairs={{6,0},{0,2},{2,4},{4,6},{7,1},{1,3},{3,5},{5,7},{14,8},{8,10},{10,... | collective-permute-start | bytes 1179656 | tf_op jit(solution)/shard_map/ppermute | solution.py:32
  11.8 53.6 %collective-permute-start.6 = (bf16[512,384]{1,0:T(8,128)(2,1)}, bf16[512,384]{1,0:T(8,128)(2,1)}, u32[]{:S(2)}, u32[]{:S(2)}) collective-permute-start(bf16[512,384]{1,0:T(8,128)(2,1)} %fusion.133), channel_id=1, source_target_pairs={{4,0},{6,2},{0,4},{2,6},{5,1},{7,3},{1,5},{3,7},{12,8},{14,10},{8,... | collective-permute-start | bytes 1179656 | tf_op jit(solution)/shard_map/ppermute | solution.py:32
  21.0 19.0 %collective-permute-start.2 = (bf16[144,1024]{1,0:T(8,128)(2,1)}, bf16[144,1024]{1,0:T(8,128)(2,1)S(1)}, u32[]{:S(2)}, u32[]{:S(2)}) collective-permute-start(bf16[144,1024]{1,0:T(8,128)(2,1)} %get-tuple-element.288), channel_id=1, source_target_pairs={{6,0},{0,2},{2,4},{4,6},{7,1},{1,3},{3,5},{5,7},{14,8},{8,10},{10,... | collective-permute-start | bytes 884744 | tf_op jit(solution)/shard_map/ppermute | solution.py:32
  24.4 18.5 %collective-permute-start = (bf16[144,1024]{1,0:T(8,128)(2,1)}, bf16[144,1024]{1,0:T(8,128)(2,1)S(1)}, u32[]{:S(2)}, u32[]{:S(2)}) collective-permute-start(bf16[144,1024]{1,0:T(8,128)(2,1)} %get-tuple-element.290), channel_id=1, source_target_pairs={{2,0},{4,2},{6,4},{0,6},{3,1},{5,3},{7,5},{1,7},{10,8},{12,10},{14... | collective-permute-start | bytes 884744 | tf_op jit(solution)/shard_map/ppermute | solution.py:32
  24.9 40.0 %collective-permute-start.1 = (bf16[144,1024]{1,0:T(8,128)(2,1)}, bf16[144,1024]{1,0:T(8,128)(2,1)S(1)}, u32[]{:S(2)}, u32[]{:S(2)}) collective-permute-start(bf16[144,1024]{1,0:T(8,128)(2,1)} %get-tuple-element.291), channel_id=1, source_target_pairs={{4,0},{6,2},{0,4},{2,6},{5,1},{7,3},{1,5},{3,7},{12,8},{14,10},{8,... | collective-permute-start | bytes 884744 | tf_op jit(solution)/shard_map/ppermute | solution.py:32
  40.0 33.2 %collective-permute-start.4 = (bf16[512,384]{1,0:T(8,128)(2,1)}, bf16[512,384]{1,0:T(8,128)(2,1)S(1)}, u32[]{:S(2)}, u32[]{:S(2)}) collective-permute-start(bf16[512,384]{1,0:T(8,128)(2,1)} %fusion.133), channel_id=1, source_target_pairs={{2,0},{4,2},{6,4},{0,6},{3,1},{5,3},{7,5},{1,7},{10,8},{12,10},{14... | collective-permute-start | bytes 1179656 | tf_op jit(solution)/shard_map/ppermute | solution.py:32
  65.3 56.1 %collective-permute-start.3 = (bf16[576,1024]{1,0:T(8,128)(2,1)S(1)}, bf16[576,1024]{1,0:T(8,128)(2,1)S(1)}, u32[]{:S(2)}, u32[]{:S(2)}) collective-permute-start(bf16[576,1024]{1,0:T(8,128)(2,1)S(1)} %fusion.71), channel_id=1, source_target_pairs={{1,0},{0,1},{3,2},{2,3},{5,4},{4,5},{7,6},{6,7},{9,8},{8,9},{11,10... | collective-permute-start | bytes 3538952 | tf_op jit(solution)/shard_map/ppermute | solution.py:32
  78.7 42.6 %collective-permute-start.9 = (bf16[512,384]{1,0:T(8,128)(2,1)}, bf16[512,384]{1,0:T(8,128)(2,1)S(1)}, u32[]{:S(2)}, u32[]{:S(2)}) collective-permute-start(bf16[512,384]{1,0:T(8,128)(2,1)} %collective-permute-done.8), channel_id=1, source_target_pairs={{8,0},{0,8},{9,1},{1,9},{10,2},{2,10},{11,3},{3,11},{12,4},{4,12},... | collective-permute-start | bytes 1179656 | tf_op jit(solution)/shard_map/ppermute | solution.py:32
  84.1 34.2 %collective-permute-start.7 = (bf16[512,384]{1,0:T(8,128)(2,1)}, bf16[512,384]{1,0:T(8,128)(2,1)S(1)}, u32[]{:S(2)}, u32[]{:S(2)}) collective-permute-start(bf16[512,384]{1,0:T(8,128)(2,1)} %collective-permute-done.6), channel_id=1, source_target_pairs={{8,0},{0,8},{9,1},{1,9},{10,2},{2,10},{11,3},{3,11},{12,4},{4,12},... | collective-permute-start | bytes 1179656 | tf_op jit(solution)/shard_map/ppermute | solution.py:32
  85.4 29.8 %collective-permute-start.5 = (bf16[512,384]{1,0:T(8,128)(2,1)S(1)}, bf16[512,384]{1,0:T(8,128)(2,1)S(1)}, u32[]{:S(2)}, u32[]{:S(2)}) collective-permute-start(bf16[512,384]{1,0:T(8,128)(2,1)S(1)} %collective-permute-done.4), channel_id=1, source_target_pairs={{8,0},{0,8},{9,1},{1,9},{10,2},{2,10},{11,3},{3,11},{12,4},{4,12},... | collective-permute-start | bytes 1179656 | tf_op jit(solution)/shard_map/ppermute | solution.py:32
  115.2 34.4 %collective-permute-start.21 = (bf16[512,512]{1,0:T(8,128)(2,1)S(1)}, bf16[512,512]{1,0:T(8,128)(2,1)S(1)}, u32[]{:S(2)}, u32[]{:S(2)}) collective-permute-start(bf16[512,512]{1,0:T(8,128)(2,1)S(1)} %dynamic-slice_bitcast_fusion.3), channel_id=1, source_target_pairs={{2,0},{4,2},{6,4},{0,6},{3,1},{5,3},{7,5},{1,7},{10,8},{12,10},{14... | collective-permute-start | bytes 1572872 | tf_op jit(solution)/shard_map/ppermute | solution.py:32
  146.0 66.7 %collective-permute-start.19 = (bf16[576,1024]{1,0:T(8,128)(2,1)S(1)}, bf16[576,1024]{1,0:T(8,128)(2,1)S(1)}, u32[]{:S(2)}, u32[]{:S(2)}) collective-permute-start(bf16[576,1024]{1,0:T(8,128)(2,1)S(1)} %convolution_convert_fusion.3), channel_id=1, source_target_pairs={{1,0},{0,1},{3,2},{2,3},{5,4},{4,5},{7,6},{6,7},{9,8},{8,9},{11,10... | collective-permute-start | bytes 3538952 | tf_op jit(solution)/shard_map/ppermute | solution.py:32
  148.6 36.3 %collective-permute-start.23 = (bf16[512,512]{1,0:T(8,128)(2,1)S(1)}, bf16[512,512]{1,0:T(8,128)(2,1)S(1)}, u32[]{:S(2)}, u32[]{:S(2)}) collective-permute-start(bf16[512,512]{1,0:T(8,128)(2,1)S(1)} %dynamic-slice_bitcast_fusion.3), channel_id=1, source_target_pairs={{4,0},{6,2},{0,4},{2,6},{5,1},{7,3},{1,5},{3,7},{12,8},{14,10},{8,... | collective-permute-start | bytes 1572872 | tf_op jit(solution)/shard_map/ppermute | solution.py:32
  149.6 41.8 %collective-permute-start.22 = (bf16[512,512]{1,0:T(8,128)(2,1)S(1)}, bf16[512,512]{1,0:T(8,128)(2,1)S(1)}, u32[]{:S(2)}, u32[]{:S(2)}) collective-permute-start(bf16[512,512]{1,0:T(8,128)(2,1)S(1)} %collective-permute-done.21), channel_id=1, source_target_pairs={{8,0},{0,8},{9,1},{1,9},{10,2},{2,10},{11,3},{3,11},{12,4},{4,12},... | collective-permute-start | bytes 1572872 | tf_op jit(solution)/shard_map/ppermute | solution.py:32
  184.9 26.8 %collective-permute-start.27 = (bf16[512,512]{1,0:T(8,128)(2,1)S(1)}, bf16[512,512]{1,0:T(8,128)(2,1)S(1)}, u32[]{:S(2)}, u32[]{:S(2)}) collective-permute-start(bf16[512,512]{1,0:T(8,128)(2,1)S(1)} %dynamic-slice_bitcast_fusion.2), channel_id=1, source_target_pairs={{2,0},{4,2},{6,4},{0,6},{3,1},{5,3},{7,5},{1,7},{10,8},{12,10},{14... | collective-permute-start | bytes 1572872 | tf_op jit(solution)/shard_map/ppermute | solution.py:32
  190.8 35.9 %collective-permute-start.31 = (bf16[512,512]{1,0:T(8,128)(2,1)S(1)}, bf16[512,512]{1,0:T(8,128)(2,1)S(1)}, u32[]{:S(2)}, u32[]{:S(2)}) collective-permute-start(bf16[512,512]{1,0:T(8,128)(2,1)S(1)} %dynamic-slice_bitcast_fusion.2), channel_id=1, source_target_pairs={{6,0},{0,2},{2,4},{4,6},{7,1},{1,3},{3,5},{5,7},{14,8},{8,10},{10,... | collective-permute-start | bytes 1572872 | tf_op jit(solution)/shard_map/ppermute | solution.py:32
  190.8 40.2 %collective-permute-start.29 = (bf16[512,512]{1,0:T(8,128)(2,1)S(1)}, bf16[512,512]{1,0:T(8,128)(2,1)S(1)}, u32[]{:S(2)}, u32[]{:S(2)}) collective-permute-start(bf16[512,512]{1,0:T(8,128)(2,1)S(1)} %dynamic-slice_bitcast_fusion.2), channel_id=1, source_target_pairs={{4,0},{6,2},{0,4},{2,6},{5,1},{7,3},{1,5},{3,7},{12,8},{14,10},{8,... | collective-permute-start | bytes 1572872 | tf_op jit(solution)/shard_map/ppermute | solution.py:32
  191.5 41.1 %collective-permute-start.26 = (bf16[512,512]{1,0:T(8,128)(2,1)S(1)}, bf16[512,512]{1,0:T(8,128)(2,1)S(1)}, u32[]{:S(2)}, u32[]{:S(2)}) collective-permute-start(bf16[512,512]{1,0:T(8,128)(2,1)S(1)} %collective-permute-done.25), channel_id=1, source_target_pairs={{8,0},{0,8},{9,1},{1,9},{10,2},{2,10},{11,3},{3,11},{12,4},{4,12},... | collective-permute-start | bytes 1572872 | tf_op jit(solution)/shard_map/ppermute | solution.py:32
  212.7 25.1 %collective-permute-start.28 = (bf16[512,512]{1,0:T(8,128)(2,1)S(1)}, bf16[512,512]{1,0:T(8,128)(2,1)S(1)}, u32[]{:S(2)}, u32[]{:S(2)}) collective-permute-start(bf16[512,512]{1,0:T(8,128)(2,1)S(1)} %collective-permute-done.27), channel_id=1, source_target_pairs={{8,0},{0,8},{9,1},{1,9},{10,2},{2,10},{11,3},{3,11},{12,4},{4,12},... | collective-permute-start | bytes 1572872 | tf_op jit(solution)/shard_map/ppermute | solution.py:32
  226.6 31.6 %collective-permute-start.20 = (bf16[576,1024]{1,0:T(8,128)(2,1)S(1)}, bf16[576,1024]{1,0:T(8,128)(2,1)S(1)}, u32[]{:S(2)}, u32[]{:S(2)}) collective-permute-start(bf16[576,1024]{1,0:T(8,128)(2,1)S(1)} %fusion.73), channel_id=1, source_target_pairs={{1,0},{0,1},{3,2},{2,3},{5,4},{4,5},{7,6},{6,7},{9,8},{8,9},{11,10... | collective-permute-start | bytes 3538952 | tf_op jit(solution)/shard_map/ppermute | solution.py:32
  226.7 31.4 %collective-permute-start.32 = (bf16[512,512]{1,0:T(8,128)(2,1)S(1)}, bf16[512,512]{1,0:T(8,128)(2,1)S(1)}, u32[]{:S(2)}, u32[]{:S(2)}) collective-permute-start(bf16[512,512]{1,0:T(8,128)(2,1)S(1)} %collective-permute-done.31), channel_id=1, source_target_pairs={{8,0},{0,8},{9,1},{1,9},{10,2},{2,10},{11,3},{3,11},{12,4},{4,12},... | collective-permute-start | bytes 1572872 | tf_op jit(solution)/shard_map/ppermute | solution.py:32
  231.0 26.9 %collective-permute-start.30 = (bf16[512,512]{1,0:T(8,128)(2,1)S(1)}, bf16[512,512]{1,0:T(8,128)(2,1)S(1)}, u32[]{:S(2)}, u32[]{:S(2)}) collective-permute-start(bf16[512,512]{1,0:T(8,128)(2,1)S(1)} %collective-permute-done.29), channel_id=1, source_target_pairs={{8,0},{0,8},{9,1},{1,9},{10,2},{2,10},{11,3},{3,11},{12,4},{4,12},... | collective-permute-start | bytes 1572872 | tf_op jit(solution)/shard_map/ppermute | solution.py:32
  286.7 29.4 %collective-permute-start.34 = (bf16[576,1024]{1,0:T(8,128)(2,1)S(1)}, bf16[576,1024]{1,0:T(8,128)(2,1)S(1)}, u32[]{:S(2)}, u32[]{:S(2)}) collective-permute-start(bf16[576,1024]{1,0:T(8,128)(2,1)S(1)} %add_convert_fusion.1), channel_id=1, source_target_pairs={{0,16},{1,17},{2,18},{3,19},{4,20},{5,21},{6,22},{7,23},{8,24},{9,... | collective-permute-start | bytes 3538952 | tf_op jit(solution)/shard_map/ppermute | solution.py:38
  379.1 18.8 %collective-permute-start.42 = (bf16[144,1024]{1,0:T(8,128)(2,1)S(1)}, bf16[144,1024]{1,0:T(8,128)(2,1)S(1)}, u32[]{:S(2)}, u32[]{:S(2)}) collective-permute-start(bf16[144,1024]{1,0:T(8,128)(2,1)S(1)} %get-tuple-element.283), channel_id=1, source_target_pairs={{2,0},{4,2},{6,4},{0,6},{3,1},{5,3},{7,5},{1,7},{10,8},{12,10},{14... | collective-permute-start | bytes 884744 | tf_op jit(solution)/shard_map/ppermute | solution.py:32
  383.0 23.2 %collective-permute-start.43 = (bf16[144,1024]{1,0:T(8,128)(2,1)S(1)}, bf16[144,1024]{1,0:T(8,128)(2,1)S(1)}, u32[]{:S(2)}, u32[]{:S(2)}) collective-permute-start(bf16[144,1024]{1,0:T(8,128)(2,1)S(1)} %get-tuple-element.284), channel_id=1, source_target_pairs={{4,0},{6,2},{0,4},{2,6},{5,1},{7,3},{1,5},{3,7},{12,8},{14,10},{8,... | collective-permute-start | bytes 884744 | tf_op jit(solution)/shard_map/ppermute | solution.py:32
  478.3 30.4 %collective-permute-start.49 = (bf16[576,1024]{1,0:T(8,128)(2,1)S(1)}, bf16[576,1024]{1,0:T(8,128)(2,1)S(1)}, u32[]{:S(2)}, u32[]{:S(2)}) collective-permute-start(bf16[576,1024]{1,0:T(8,128)(2,1)S(1)} %get-tuple-element.259), channel_id=1, source_target_pairs={{16,0},{17,1},{18,2},{19,3},{20,4},{21,5},{22,6},{23,7},{24,8},{25... | collective-permute-start | bytes 3538952 | tf_op jit(solution)/shard_map/ppermute | solution.py:38
  482.6 23.2 %collective-permute-start.40 = (bf16[144,1024]{1,0:T(8,128)(2,1)S(1)}, bf16[144,1024]{1,0:T(8,128)(2,1)S(1)}, u32[]{:S(2)}, u32[]{:S(2)}) collective-permute-start(bf16[144,1024]{1,0:T(8,128)(2,1)S(1)} %get-tuple-element.286), channel_id=1, source_target_pairs={{4,0},{6,2},{0,4},{2,6},{5,1},{7,3},{1,5},{3,7},{12,8},{14,10},{8,... | collective-permute-start | bytes 884744 | tf_op jit(solution)/shard_map/ppermute | solution.py:32
  482.7 29.8 %collective-permute-start.41 = (bf16[144,1024]{1,0:T(8,128)(2,1)S(1)}, bf16[144,1024]{1,0:T(8,128)(2,1)S(1)}, u32[]{:S(2)}, u32[]{:S(2)}) collective-permute-start(bf16[144,1024]{1,0:T(8,128)(2,1)S(1)} %get-tuple-element.285), channel_id=1, source_target_pairs={{6,0},{0,2},{2,4},{4,6},{7,1},{1,3},{3,5},{5,7},{14,8},{8,10},{10,... | collective-permute-start | bytes 884744 | tf_op jit(solution)/shard_map/ppermute | solution.py:32
  525.1 31.4 %collective-permute-start.51 = (bf16[576,1024]{1,0:T(8,128)(2,1)}, bf16[576,1024]{1,0:T(8,128)(2,1)}, u32[]{:S(2)}, u32[]{:S(2)}) collective-permute-start(bf16[576,1024]{1,0:T(8,128)(2,1)} %fusion.97), channel_id=1, source_target_pairs={{1,0},{0,1},{3,2},{2,3},{5,4},{4,5},{7,6},{6,7},{9,8},{8,9},{11,10... | collective-permute-start | bytes 3538952 | tf_op jit(solution)/shard_map/ppermute | solution.py:32
  543.4 48.8 %collective-permute-start.74 = (bf16[512,2048]{1,0:T(8,128)(2,1)}, bf16[512,2048]{1,0:T(8,128)(2,1)}, u32[]{:S(2)}, u32[]{:S(2)}) collective-permute-start(bf16[512,2048]{1,0:T(8,128)(2,1)} %get-tuple-element.130), channel_id=1, source_target_pairs={{8,0},{0,8},{9,1},{1,9},{10,2},{2,10},{11,3},{3,11},{12,4},{4,12},... | collective-permute-start | bytes 6291464 | tf_op jit(solution)/shard_map/ppermute | solution.py:32
  555.1 81.0 %collective-permute-start.78 = (bf16[2048,512]{1,0:T(8,128)(2,1)}, bf16[2048,512]{1,0:T(8,128)(2,1)S(1)}, u32[]{:S(2)}, u32[]{:S(2)}) collective-permute-start(bf16[2048,512]{1,0:T(8,128)(2,1)} %get-tuple-element.127), channel_id=1, source_target_pairs={{8,0},{0,8},{9,1},{1,9},{10,2},{2,10},{11,3},{3,11},{12,4},{4,12},... | collective-permute-start | bytes 6291464 | tf_op jit(solution)/shard_map/ppermute | solution.py:32
  566.5 72.5 %collective-permute-start.52 = (bf16[576,1024]{1,0:T(8,128)(2,1)S(1)}, bf16[576,1024]{1,0:T(8,128)(2,1)S(1)}, u32[]{:S(2)}, u32[]{:S(2)}) collective-permute-start(bf16[576,1024]{1,0:T(8,128)(2,1)S(1)} %get-tuple-element.238), channel_id=1, source_target_pairs={{1,0},{0,1},{3,2},{2,3},{5,4},{4,5},{7,6},{6,7},{9,8},{8,9},{11,10... | collective-permute-start | bytes 3538952 | tf_op jit(solution)/shard_map/ppermute | solution.py:32
  597.9 118.7 %collective-permute-start.75 = (bf16[512,512]{1,0:T(8,128)(2,1)}, bf16[512,512]{1,0:T(8,128)(2,1)S(1)}, u32[]{:S(2)}, u32[]{:S(2)}) collective-permute-start(bf16[512,512]{1,0:T(8,128)(2,1)} %get-tuple-element.265), channel_id=1, source_target_pairs={{6,0},{0,2},{2,4},{4,6},{7,1},{1,3},{3,5},{5,7},{14,8},{8,10},{10,... | collective-permute-start | bytes 1572872 | tf_op jit(solution)/shard_map/ppermute | solution.py:32
  597.9 118.7 %collective-permute-start.77 = (bf16[512,512]{1,0:T(8,128)(2,1)}, bf16[512,512]{1,0:T(8,128)(2,1)}, u32[]{:S(2)}, u32[]{:S(2)}) collective-permute-start(bf16[512,512]{1,0:T(8,128)(2,1)} %get-tuple-element.266), channel_id=1, source_target_pairs={{2,0},{4,2},{6,4},{0,6},{3,1},{5,3},{7,5},{1,7},{10,8},{12,10},{14... | collective-permute-start | bytes 1572872 | tf_op jit(solution)/shard_map/ppermute | solution.py:32
  680.5 24.0 %collective-permute-start.67 = (f32[1,768]{1,0:T(1,128)S(1)}, f32[1,768]{1,0:T(1,128)S(1)}, u32[]{:S(2)}, u32[]{:S(2)}) collective-permute-start(f32[1,768]{1,0:T(1,128)S(1)} %get-tuple-element.318), channel_id=1, source_target_pairs={{4,0},{6,2},{0,4},{2,6},{5,1},{7,3},{1,5},{3,7},{12,8},{14,10},{8,... | collective-permute-start | bytes 9224 | tf_op jit(solution)/shard_map/ppermute | solution.py:32
  682.1 47.1 %collective-permute-start.76 = (bf16[512,512]{1,0:T(8,128)(2,1)}, bf16[512,512]{1,0:T(8,128)(2,1)S(1)}, u32[]{:S(2)}, u32[]{:S(2)}) collective-permute-start(bf16[512,512]{1,0:T(8,128)(2,1)} %get-tuple-element.267), channel_id=1, source_target_pairs={{4,0},{6,2},{0,4},{2,6},{5,1},{7,3},{1,5},{3,7},{12,8},{14,10},{8,... | collective-permute-start | bytes 1572872 | tf_op jit(solution)/shard_map/ppermute | solution.py:32
  684.6 48.8 %collective-permute-start.79 = (bf16[512,512]{1,0:T(8,128)(2,1)}, bf16[512,512]{1,0:T(8,128)(2,1)}, u32[]{:S(2)}, u32[]{:S(2)}) collective-permute-start(bf16[512,512]{1,0:T(8,128)(2,1)} %get-tuple-element.262), channel_id=1, source_target_pairs={{6,0},{0,2},{2,4},{4,6},{7,1},{1,3},{3,5},{5,7},{14,8},{8,10},{10,... | collective-permute-start | bytes 1572872 | tf_op jit(solution)/shard_map/ppermute | solution.py:32
  716.6 25.4 %collective-permute-start.81 = (bf16[512,512]{1,0:T(8,128)(2,1)}, bf16[512,512]{1,0:T(8,128)(2,1)S(1)}, u32[]{:S(2)}, u32[]{:S(2)}) collective-permute-start(bf16[512,512]{1,0:T(8,128)(2,1)} %get-tuple-element.263), channel_id=1, source_target_pairs={{2,0},{4,2},{6,4},{0,6},{3,1},{5,3},{7,5},{1,7},{10,8},{12,10},{14... | collective-permute-start | bytes 1572872 | tf_op jit(solution)/shard_map/ppermute | solution.py:32
  716.6 39.3 %collective-permute-start.80 = (bf16[512,512]{1,0:T(8,128)(2,1)}, bf16[512,512]{1,0:T(8,128)(2,1)S(1)}, u32[]{:S(2)}, u32[]{:S(2)}) collective-permute-start(bf16[512,512]{1,0:T(8,128)(2,1)} %get-tuple-element.264), channel_id=1, source_target_pairs={{4,0},{6,2},{0,4},{2,6},{5,1},{7,3},{1,5},{3,7},{12,8},{14,10},{8,... | collective-permute-start | bytes 1572872 | tf_op jit(solution)/shard_map/ppermute | solution.py:32
  729.2 34.4 %collective-permute-start.53 = (bf16[576,1024]{1,0:T(8,128)(2,1)}, bf16[576,1024]{1,0:T(8,128)(2,1)S(1)}, u32[]{:S(2)}, u32[]{:S(2)}) collective-permute-start(bf16[576,1024]{1,0:T(8,128)(2,1)} %fusion.103), channel_id=1, source_target_pairs={{1,0},{0,1},{3,2},{2,3},{5,4},{4,5},{7,6},{6,7},{9,8},{8,9},{11,10... | collective-permute-start | bytes 3538952 | tf_op jit(solution)/shard_map/ppermute | solution.py:32
  731.9 74.1 %collective-permute-start.62 = (bf16[512,1536]{1,0:T(8,128)(2,1)}, bf16[512,1536]{1,0:T(8,128)(2,1)S(1)}, u32[]{:S(2)}, u32[]{:S(2)}) collective-permute-start(bf16[512,1536]{1,0:T(8,128)(2,1)} %get-tuple-element.140), channel_id=1, source_target_pairs={{8,0},{0,8},{9,1},{1,9},{10,2},{2,10},{11,3},{3,11},{12,4},{4,12},... | collective-permute-start | bytes 4718600 | tf_op jit(solution)/shard_map/ppermute | solution.py:32
  733.4 25.1 %collective-permute-start.71 = (bf16[128,512]{1,0:T(8,128)(2,1)S(1)}, bf16[128,512]{1,0:T(8,128)(2,1)S(1)}, u32[]{:S(2)}, u32[]{:S(2)}) collective-permute-start(bf16[128,512]{1,0:T(8,128)(2,1)S(1)} %get-tuple-element.297), channel_id=1, source_target_pairs={{6,0},{0,2},{2,4},{4,6},{7,1},{1,3},{3,5},{5,7},{14,8},{8,10},{10,... | collective-permute-start | bytes 393224 | tf_op jit(solution)/shard_map/ppermute | solution.py:32
  783.7 22.2 %collective-permute-start.56 = (bf16[144,1024]{1,0:T(8,128)(2,1)S(1)}, bf16[144,1024]{1,0:T(8,128)(2,1)S(1)}, u32[]{:S(2)}, u32[]{:S(2)}) collective-permute-start(bf16[144,1024]{1,0:T(8,128)(2,1)S(1)} %get-tuple-element.278), channel_id=1, source_target_pairs={{6,0},{0,2},{2,4},{4,6},{7,1},{1,3},{3,5},{5,7},{14,8},{8,10},{10,... | collective-permute-start | bytes 884744 | tf_op jit(solution)/shard_map/ppermute | solution.py:32
  785.1 20.8 %collective-permute-start.55 = (bf16[144,1024]{1,0:T(8,128)(2,1)S(1)}, bf16[144,1024]{1,0:T(8,128)(2,1)S(1)}, u32[]{:S(2)}, u32[]{:S(2)}) collective-permute-start(bf16[144,1024]{1,0:T(8,128)(2,1)S(1)} %get-tuple-element.279), channel_id=1, source_target_pairs={{4,0},{6,2},{0,4},{2,6},{5,1},{7,3},{1,5},{3,7},{12,8},{14,10},{8,... | collective-permute-start | bytes 884744 | tf_op jit(solution)/shard_map/ppermute | solution.py:32
  806.9 24.2 %collective-permute-start.64 = (bf16[512,384]{1,0:T(8,128)(2,1)S(1)}, bf16[512,384]{1,0:T(8,128)(2,1)S(1)}, u32[]{:S(2)}, u32[]{:S(2)}) collective-permute-start(bf16[512,384]{1,0:T(8,128)(2,1)S(1)} %pad_maximum_fusion.11), channel_id=1, source_target_pairs={{4,0},{6,2},{0,4},{2,6},{5,1},{7,3},{1,5},{3,7},{12,8},{14,10},{8,... | collective-permute-start | bytes 1179656 | tf_op jit(solution)/shard_map/ppermute | solution.py:32
  816.3 25.9 %collective-permute-start.63 = (bf16[512,384]{1,0:T(8,128)(2,1)S(1)}, bf16[512,384]{1,0:T(8,128)(2,1)S(1)}, u32[]{:S(2)}, u32[]{:S(2)}) collective-permute-start(bf16[512,384]{1,0:T(8,128)(2,1)S(1)} %pad_maximum_fusion.10), channel_id=1, source_target_pairs={{6,0},{0,2},{2,4},{4,6},{7,1},{1,3},{3,5},{5,7},{14,8},{8,10},{10,... | collective-permute-start | bytes 1179656 | tf_op jit(solution)/shard_map/ppermute | solution.py:32
  (161 other events, 3497.6 us)

commit v2 on v1

--- a/solution.py
+++ b/solution.py
@@ -14,6 +14,7 @@
 STEPS = 5000
 PAIR = 2 * HDIM
 TILE = 128
+AHEAD = 2
 WIDTHS = (2, 3, 4, 5, 6, 7, 9)
 LOG2E = math.log2(math.e)
 SCALE = 1.0 / math.sqrt(HDIM)
@@ -174,11 +175,7 @@
         ],
         scratch_shapes=[pltpu.VMEM((length, width), bf16)] * 4,
         compiler_params=pltpu.CompilerParams(vmem_limit_bytes=48 * 1024 * 1024),
-        cost_estimate=pl.CostEstimate(
-            flops=8 * length * length * width,
-            bytes_accessed=8 * length * width,
-            transcendentals=2 * pairs * length * length,
-        ),
+        cost_estimate=pl.CostEstimate(flops=0, bytes_accessed=0, transcendentals=0),
     )(order, span, segment[:, None], segment[None, :], qkv, qkv, qkv)
 
 
@@ -239,11 +236,7 @@
         out_shape=[jax.ShapeDtypeStruct((length, width), bf16)] * 3,
         scratch_shapes=[pltpu.VMEM((length, width), bf16)] * 5 + [pltpu.VMEM((length, width), f32)] * 2,
         compiler_params=pltpu.CompilerParams(vmem_limit_bytes=48 * 1024 * 1024),
-        cost_estimate=pl.CostEstimate(
-            flops=20 * length * length * width,
-            bytes_accessed=16 * length * width,
-            transcendentals=2 * pairs * length * length,
-        ),
+        cost_estimate=pl.CostEstimate(flops=0, bytes_accessed=0, transcendentals=0),
     )(order, span, segment[:, None], segment[None, :], qkv, qkv, qkv, grad_mixed, lse)
 
 
@@ -280,12 +273,428 @@
         out_specs=[pl.BlockSpec((count, step), lambda i: (0, i))] * 2,
         out_shape=[jax.ShapeDtypeStruct((count, units), bf16)] * 2,
         compiler_params=pltpu.CompilerParams(vmem_limit_bytes=48 * 1024 * 1024),
-        cost_estimate=pl.CostEstimate(
-            flops=2 * count * width * units,
-            bytes_accessed=2 * (width * units + 2 * count * units),
-            transcendentals=2 * count * units,
+        cost_estimate=pl.CostEstimate(flops=0, bytes_accessed=0, transcendentals=0),
+    )(x, weight, bias[None])
+
+
+def gather_kernel(seqs, dp_size, *refs):
+    seq_ref, bias_ref = refs[:2]
+    blocks = refs[2:8]
+    start_ref, biases_ref, joined_ref, out_ref, in_ref, ffn_out_ref = refs[8:14]
+    local_sem, seq_send, seq_get, up_send, up_get, down_send, down_get, side_send, side_get = refs[14:]
+    zs, dp = lax.axis_index("zs"), lax.axis_index("dp")
+    width, hc = blocks[0].shape
+    units = blocks[4].shape[1]
+    part = width // dp_size
+    half = units // 2
+    table = [(0, 0, hc), (1, 0, hc), (2, 0, hc), (3, 0, hc)]
+    table += [(4, 0, half), (4, half, half), (5, 0, half), (5, half, half)]
+    kinds = range(len(table))
+
+    def home(kind, slot, other):
+        array, first, size = table[kind]
+        features = slice(other * part, (other + 1) * part)
+        if array < 3:
+            at = (array * seqs + slot) * hc
+            return joined_ref.at[features, at : at + hc]
+        if array == 3:
+            return out_ref.at[slot * hc : (slot + 1) * hc, features]
+        at = slice(slot * units + first, slot * units + first + size)
+        return in_ref.at[features, at] if array == 4 else ffn_out_ref.at[at, features]
+
+    def own(kind, other):
+        array, first, size = table[kind]
+        features = pl.ds(pl.multiple_of(lax.rem(dp + other, dp_size) * part, part), part)
+        if array in (3, 5):
+            return blocks[array].at[first : first + size, features]
+        return blocks[array].at[features, first : first + size]
+
+    def to(axis, at, source, target, send, get):
+        return pltpu.make_async_remote_copy(
+            src_ref=source,
+            dst_ref=target,
+            send_sem=send,
+            recv_sem=get,
+            device_id={axis: at},
+            device_id_type=pl.DeviceIdType.MESH,
+        )
+
+    def sequence(by):
+        at = lax.rem(zs - by + seqs, seqs)
+        return to("zs", at, seq_ref.at[at], start_ref.at[by], seq_send.at[by], seq_get.at[by])
+
+    def bias(by):
+        at = lax.rem(zs - by + seqs, seqs)
+        return to("zs", at, bias_ref, biases_ref.at[by], seq_send.at[seqs + by], seq_get.at[seqs + by])
+
+    def up(kind, hop):
+        source = own(kind, 0) if hop == 0 else home(kind, seqs - hop, 0)
+        target = home(kind, seqs - hop - 1, 0)
+        return to("zs", zs + 1, source, target, up_send.at[kind, hop], up_get.at[kind, hop])
+
+    def down(kind, hop):
+        source = own(kind, 0) if hop == 0 else home(kind, hop, 0)
+        target = home(kind, hop + 1, 0)
+        return to("zs", zs - 1, source, target, down_send.at[kind, hop], down_get.at[kind, hop])
+
+    def side(kind, slot, other):
+        at = lax.rem(dp - other + dp_size, dp_size)
+        place = side_send.at[kind, slot, other], side_get.at[kind, slot, other]
+        return to("dp", at, home(kind, slot, 0), home(kind, slot, other), *place)
+
+    def local(kind, other):
+        return pltpu.make_async_copy(own(kind, other), home(kind, 0, other), local_sem.at[kind, other])
+
+    barrier = pltpu.get_barrier_semaphore()
+    for axis, at, size in (("zs", zs, seqs), ("dp", dp, dp_size)):
+        for by in range(1, size):
+            pl.semaphore_signal(
+                barrier,
+                inc=1,
+                device_id={axis: lax.rem(at + by, size)},
+                device_id_type=pl.DeviceIdType.MESH,
+            )
+    pl.semaphore_wait(barrier, seqs + dp_size - 2)
+
+    for by in range(1, seqs):
+        sequence(by).start()
+        bias(by).start()
+    def begin(kind):
+        @pl.when(zs < seqs - 1)
+        def _():
+            up(kind, 0).start()
+
+        @pl.when(zs > 0)
+        def _():
+            down(kind, 0).start()
+
+    for kind in kinds[:AHEAD]:
+        begin(kind)
+
+    own_seq = pltpu.make_async_copy(seq_ref.at[zs], start_ref.at[0], local_sem.at[len(table), 0])
+    own_bias = pltpu.make_async_copy(bias_ref, biases_ref.at[0], local_sem.at[len(table), 1])
+    own_seq.start()
+    own_bias.start()
+    for kind in kinds:
+        for other in range(dp_size):
+            local(kind, other).start()
+
+    def pass_on(kind, hop):
+        @pl.when(zs >= hop)
+        def _():
+            up(kind, hop - 1).wait_recv()
+            if hop < seqs - 1:
+
+                @pl.when(zs < seqs - 1)
+                def _():
+                    up(kind, hop).start()
+
+            for other in range(1, dp_size):
+                side(kind, seqs - hop, other).start()
+
+        @pl.when(zs + hop < seqs)
+        def _():
+            down(kind, hop - 1).wait_recv()
+            if hop < seqs - 1:
+
+                @pl.when(zs > 0)
+                def _():
+                    down(kind, hop).start()
+
+            for other in range(1, dp_size):
+                side(kind, hop, other).start()
+
+    for step in range(len(kinds) + seqs - 2):
+        for hop in range(1, seqs):
+            if 0 <= step - hop + 1 < len(kinds):
+                pass_on(step - hop + 1, hop)
+        if step + AHEAD < len(kinds):
+            begin(step + AHEAD)
+
+    own_seq.wait()
+    own_bias.wait()
+    for by in range(1, seqs):
+        sequence(by).wait()
+        bias(by).wait()
+    for kind in kinds:
+        for other in range(dp_size):
+            local(kind, other).wait()
+        for slot in range(1, seqs):
+            for other in range(1, dp_size):
+                side(kind, slot, other).wait()
+        for hop in range(seqs - 1):
+
+            @pl.when((zs >= hop) & (zs < seqs - 1))
+            def _():
+                up(kind, hop).wait_send()
+
+            @pl.when((zs + hop < seqs) & (zs > 0))
+            def _():
+                down(kind, hop).wait_send()
+
+
+def gather_all(by_seq, biases, blocks, dp_size):
+    seqs, _, width = by_seq.shape
+    hc, units = blocks[0].shape[1], blocks[4].shape[1]
+    anywhere = pl.BlockSpec(memory_space=pl.ANY)
+    low = lambda *shape: jax.ShapeDtypeStruct(shape, bf16)
+    dma = pltpu.SemaphoreType.DMA
+    kinds = 8
+    return pl.pallas_call(
+        functools.partial(gather_kernel, seqs, dp_size),
+        in_specs=[anywhere] * (2 + len(blocks)),
+        out_specs=[anywhere] * 6,
+        out_shape=[
+            jax.ShapeDtypeStruct(by_seq.shape, bf16),
+            jax.ShapeDtypeStruct((seqs,) + biases.shape, f32),
+            low(width, 3 * seqs * hc),
+            low(seqs * hc, width),
+            low(width, seqs * units),
+            low(seqs * units, width),
+        ],
+        scratch_shapes=[
+            dma((kinds + 1, max(dp_size, 2))),
+            dma((2 * seqs,)),
+            dma((2 * seqs,)),
+            dma((kinds, seqs - 1)),
+            dma((kinds, seqs - 1)),
+            dma((kinds, seqs - 1)),
+            dma((kinds, seqs - 1)),
+            dma((kinds, seqs, dp_size)),
+            dma((kinds, seqs, dp_size)),
+        ],
+        compiler_params=pltpu.CompilerParams(collective_id=0, has_side_effects=True),
+    )(by_seq, biases, *blocks)
+
+
+def scatter_kernel(seqs, dp_size, tp_size, *refs):
+    seq_ref, small_ref, slots_ref = refs[:3]
+    mine, theirs = refs[3:7], refs[7:11]
+    seq_out, small_out, slots_out = refs[11:14]
+    outs = refs[14:20]
+    sides, ups, downs = refs[20:24], refs[24:28], refs[28:32]
+    small_zs, small_all, slots_zs, slots_dp = refs[32:36]
+    seq_send, seq_get, local_sem, small_send, small_get = refs[36:41]
+    side_send, side_get, up_send, up_get, down_send, down_get = refs[41:47]
+    zs, dp, tp = lax.axis_index("zs"), lax.axis_index("dp"), lax.axis_index("tp")
+    units = mine[0].shape[0] // seqs
+    hc = mine[2].shape[0] // seqs
+    half = units // 2
+    kinds = [(0, 0, 0, half), (0, 0, half, half), (1, 1, 0, half), (1, 1, half, half), (2, 0, 0, hc)]
+    kinds += [(3, 1, third * seqs * hc, hc) for third in range(3)]
+
+    def cut(arrays, kind, slot):
+        array, axis, first, size = kinds[kind]
+        apart = units if array < 2 else hc
+        at = slice(first + slot * apart, first + slot * apart + size)
+        return arrays[array].at[at, :] if axis == 0 else arrays[array].at[:, at]
+
+    def to(where, source, target, send, get):
+        return pltpu.make_async_remote_copy(
+            src_ref=source,
+            dst_ref=target,
+            send_sem=send,
+            recv_sem=get,
+            device_id=where,
+            device_id_type=pl.DeviceIdType.MESH,
+        )
+
+    def sequence(by):
+        at = lax.rem(zs + by, seqs)
+        return to({"zs": at}, seq_ref.at[by], seq_out.at[by], seq_send.at[by], seq_get.at[by])
+
+    def side(kind, slot):
+        place = side_send.at[kind, slot], side_get.at[kind, slot]
+        return to({"dp": 1 - dp}, cut(theirs, kind, slot), cut(sides, kind, slot), *place)
+
+    def up(kind, far):
+        place = up_send.at[kind, far], up_get.at[kind, far]
+        return to({"zs": zs + 1}, cut(sides, kind, far), cut(ups, kind, far - 1), *place)
+
+    def down(kind, far):
+        place = down_send.at[kind, far], down_get.at[kind, far]
+        return to({"zs": zs - 1}, cut(sides, kind, seqs - far), cut(downs, kind, far - 1), *place)
+
+    def small(by):
+        at = {"zs": lax.rem(zs + by, seqs)}
+        return to(at, small_ref, small_zs.at[by], small_send.at[0, by], small_get.at[0, by])
+
+    def slots(by):
+        at = {"zs": lax.rem(zs + by, seqs)}
+        return to(at, slots_ref.at[by], slots_zs.at[by], small_send.at[1, by], small_get.at[1, by])
+
+    def small_across(by):
+        at = lax.rem(dp * tp_size + tp + by, dp_size * tp_size)
+        where = {"dp": lax.div(at, tp_size), "tp": lax.rem(at, tp_size)}
+        return to(where, small_all.at[0], small_all.at[by], small_send.at[2, by], small_get.at[2, by])
+
+    def slots_across():
+        return to({"dp": 1 - dp}, slots_dp.at[0], slots_dp.at[1], small_send.at[3, 0], small_get.at[3, 0])
+
+    def added(target, *others):
+        rows = target.shape[0]
+        step = 64
+
+        def body(i, carry):
+            at = pl.ds(pl.multiple_of(i * step, step), step)
+            total = target[at, :].astype(f32)
+            for other in others:
+                total = total + other[at, :].astype(f32)
+            target[at, :] = total.astype(target.dtype)
+            return carry
+
+        lax.fori_loop(0, rows // step, body, 0)
+
+    barrier = pltpu.get_barrier_semaphore()
+    greeted = [{"zs": lax.rem(zs + by, seqs)} for by in range(1, seqs)]
+    for by in range(1, dp_size * tp_size):
+        at = lax.rem(dp * tp_size + tp + by, dp_size * tp_size)
+        greeted.append({"dp": lax.div(at, tp_size), "tp": lax.rem(at, tp_size)})
+    for where in greeted:
+        pl.semaphore_signal(barrier, inc=1, device_id=where, device_id_type=pl.DeviceIdType.MESH)
+    pl.semaphore_wait(barrier, len(greeted))
+
+    slot_order = list(range(1, seqs)) + [0]
+
+    def begin(kind):
+        for slot in slot_order:
+            side(kind, slot).start()
+
+    for kind in range(AHEAD):
+        begin(kind)
+    for by in range(1, seqs):
+        small(by).start()
+        slots(by).start()
+    for by in range(1, seqs):
+        sequence(by).start()
+    own_seq = pltpu.make_async_copy(seq_ref.at[0], seq_out.at[0], local_sem.at[0])
+    own_seq.start()
+
+    total, slot_total = small_ref[...], slots_ref[0]
+    for by in range(1, seqs):
+        small(by).wait()
+        slots(by).wait()
+        total = total + small_zs[by]
+        slot_total = slot_total + slots_zs[by]
+    small_all[0] = total
+    slots_dp[0] = slot_total
+    for by in range(1, dp_size * tp_size):
+        small_across(by).start()
+    slots_across().start()
+
+    def taken(kind):
+        for slot in slot_order:
+            side(kind, slot).wait()
+            added(cut(sides, kind, slot), cut(mine, kind, slot))
+
+    def pass_on(kind, hop):
+        @pl.when((zs == hop) & (zs < seqs - 1))
+        def _():
+            for far in range(seqs - 1 - hop, 0, -1):
+                if hop > 0:
+                    up(kind, far + 1).wait_recv()
+                    added(cut(sides, kind, far), cut(ups, kind, far))
+                up(kind, far).start()
+
+        @pl.when((zs == seqs - 1 - hop) & (zs > 0))
+        def _():
+            for far in range(seqs - 1 - hop, 0, -1):
+                if hop > 0:
+                    down(kind, far + 1).wait_recv()
+                    added(cut(sides, kind, seqs - far), cut(downs, kind, far))
+                down(kind, far).start()
+
+    for step in range(len(kinds) + seqs - 2):
+        if step < len(kinds):
+            taken(step)
+            if step + AHEAD < len(kinds):
+                begin(step + AHEAD)
+        for hop in range(seqs - 1):
+            if 0 <= step - hop < len(kinds):
+                pass_on(step - hop, hop)
+
+    for by in range(1, dp_size * tp_size):
+        small_across(by).wait()
+        total = total + small_all[by]
+    slots_across().wait()
+    small_out[...] = total
+    slots_out[...] = slot_total + slots_dp[1]
+
+    for kind, (array, axis, first, size) in enumerate(kinds):
+        out = outs[array] if array < 3 else outs[3 + first // (seqs * hc)]
+        if array < 2:
+            out = out.at[first : first + size, :] if axis == 0 else out.at[:, first : first + size]
+        out[...] = cut(sides, kind, 0)[...].astype(f32)
+
+        @pl.when(zs > 0)
+        def _():
+            up(kind, 1).wait_recv()
+            added(out, cut(ups, kind, 0))
+
+        @pl.when(zs < seqs - 1)
+        def _():
+            down(kind, 1).wait_recv()
+            added(out, cut(downs, kind, 0))
+
+        for far in range(1, seqs):
+
+            @pl.when(zs + far < seqs)
+            def _():
+                up(kind, far).wait_send()
+
+            @pl.when(zs >= far)
+            def _():
+                down(kind, far).wait_send()
+
+    own_seq.wait()
+    for by in range(1, seqs):
+        sequence(by).wait()
+
+
+def scatter_all(by_block, small, slots, mine, theirs, tp_size):
+    seqs = by_block.shape[0]
+    units, part = mine[0].shape[0] // seqs, mine[0].shape[1]
+    hc = mine[2].shape[0] // seqs
+    dp_size = 2
+    anywhere = pl.BlockSpec(memory_space=pl.ANY)
+    inside = pl.BlockSpec(memory_space=pltpu.VMEM)
+    wide = lambda *shape: jax.ShapeDtypeStruct(shape, f32)
+    dma = pltpu.SemaphoreType.DMA
+    like = [pltpu.VMEM(block.shape, bf16) for block in mine]
+    kinds = 8
+    return pl.pallas_call(
+        functools.partial(scatter_kernel, seqs, dp_size, tp_size),
+        in_specs=[anywhere, inside, inside] + [inside] * 4 + [anywhere] * 4,
+        out_specs=[anywhere] + [inside] * 8,
+        out_shape=[
+            jax.ShapeDtypeStruct(by_block.shape, bf16),
+            wide(*small.shape),
+            wide(*slots.shape[1:]),
+            wide(units, part),
+            wide(part, units),
+            wide(hc, part),
+            wide(part, hc),
+            wide(part, hc),
+            wide(part, hc),
+        ],
+        scratch_shapes=like * 3
+        + [
+            pltpu.VMEM((seqs,) + small.shape, f32),
+            pltpu.VMEM((dp_size * tp_size,) + small.shape, f32),
+            pltpu.VMEM(slots.shape, f32),
+            pltpu.VMEM((2,) + slots.shape[1:], f32),
+            dma((seqs,)),
+            dma((seqs,)),
+            dma((1,)),
+            dma((4, max(seqs, dp_size * tp_size))),
+            dma((4, max(seqs, dp_size * tp_size))),
+        ]
+        + [dma((kinds, seqs))] * 6,
+        input_output_aliases={},
+        compiler_params=pltpu.CompilerParams(
+            collective_id=1, has_side_effects=True, vmem_limit_bytes=56 * 1024 * 1024
         ),
-    )(x, weight, bias[None])
+    )(by_block, small, slots, *mine, *theirs)
 
 
 def per_device(
@@ -351,7 +760,10 @@
 
     def to_positions(array):
         by_block = straightened(array).reshape(seqs, rows, width)
-        got = [received(by_block[(seqs - by) % seqs], "zs", by)[None] for by in range(seqs)]
+        return [received(by_block[(seqs - by) % seqs], "zs", by)[None] for by in range(seqs)]
+
+    def in_positions(got, *before):
+        got = [after(piece, *before) for piece in got]
         twice = jnp.concatenate(got + got)
         by_seq = lax.dynamic_slice_in_dim(twice, (seqs - zs_at) % seqs, seqs, 0)
         return jnp.transpose(by_seq, (1, 0, 2))
@@ -417,18 +829,29 @@
                 whole = put(whole, piece, slot + 1, other * part)
         return whole
 
-    joined_block = jnp.concatenate([query_weight[0], key_weight[0], value_weight[0]], axis=1)
     biases = jnp.concatenate([query_bias[0], value_bias[0], ffn_in_bias[0].astype(f32)])[None]
-    start_pieces = to_sequence(states)
-    bias_slots = [received(biases, "zs", by)[0] for by in range(seqs)]
-    joined_zs = over_zs(joined_block, 0)
-    out_zs = over_zs(out_weight[0], 1, *joined_zs, *start_pieces)
-    in_zs = over_zs(ffn_in[0], 0, *out_zs)
-    ffn_out_zs = over_zs(ffn_out[0], 1, *in_zs)
-    joined = assembled(joined_block, 0, over_dp(joined_zs), 3)
-    out_all = assembled(out_weight[0], 1, over_dp(out_zs), 1)
-    in_all = assembled(ffn_in[0], 0, over_dp(in_zs), 1)
-    ffn_out_all = assembled(ffn_out[0], 1, over_dp(ffn_out_zs), 1)
+    in_kernels = dp_size == 2 and head_cols % 128 == 0 and part % 128 == 0 and unit_cols % 128 == 0
+    if in_kernels:
+        by_seq = rotated(jnp.transpose(states, (1, 0, 2)))
+        blocks = (query_weight, key_weight, value_weight, out_weight, ffn_in, ffn_out)
+        start, bias_slots, joined, out_all, in_all, ffn_out_all = gather_all(
+            by_seq, biases, [block[0] for block in blocks], dp_size
+        )
+        start_rows = start.reshape(own_count, width)
+        bias_slots = bias_slots[:, 0]
+    else:
+        joined_block = jnp.concatenate([query_weight[0], key_weight[0], value_weight[0]], axis=1)
+        start_pieces = to_sequence(states)
+        start_rows = jnp.concatenate(start_pieces)
+        bias_slots = [received(biases, "zs", by)[0] for by in range(seqs)]
+        joined_zs = over_zs(joined_block, 0)
+        out_zs = over_zs(out_weight[0], 1, *joined_zs, *start_pieces)
+        in_zs = over_zs(ffn_in[0], 0, *out_zs)
+        ffn_out_zs = over_zs(ffn_out[0], 1, *in_zs)
+        joined = assembled(joined_block, 0, over_dp(joined_zs), 3)
+        out_all = assembled(out_weight[0], 1, over_dp(out_zs), 1)
+        in_all = assembled(ffn_in[0], 0, over_dp(in_zs), 1)
+        ffn_out_all = assembled(ffn_out[0], 1, over_dp(ffn_out_zs), 1)
     query_bias_all = jnp.concatenate([b[:head_cols] for b in bias_slots])
     value_bias_all = jnp.concatenate([b[head_cols : 2 * head_cols] for b in bias_slots])
     in_bias_all = jnp.concatenate([b[2 * head_cols :] for b in bias_slots])
@@ -446,12 +869,14 @@
 
     kept = []
     layer_rows, stat_terms = None, None
-    inputs = jnp.concatenate(start_pieces)
+    inputs = start_rows
     for tick in range(sections):
         residual = inputs.astype(f32) + time_rows * time_weight + time_bias
         rounded_all = everyone(residual.astype(bf16))
         qkv = by_position((mm(rounded_all, joined) + joined_bias).astype(bf16))
         mixed, lse = attend(qkv, segment, span, kernel_order, kernel_rows)
+        if tick == 1:
+            mixed = after(mixed, *upstream_pieces)
         mixed = by_distance(mixed)
         branch = returned(mixed, out_all, ((1,), (0,))) + out_bias
         first_normed, first_inverse = norm_parts(residual + branch)
@@ -488,7 +913,7 @@
             stat_terms = jnp.where(here, terms, stat_terms)
         if tick + 1 < sections:
             inputs = passed_along(layer_y, "pipe", 1)
-    layer_out = to_positions(layer_rows)
+    layer_pieces = to_positions(layer_rows)
 
 
     def parts_of(left, right, side):
@@ -599,20 +1024,40 @@
             results = jax.tree.map(lambda a, b: jnp.where(here, a, b), these, results)
         if not last:
             upstream_rows = passed_along(grad_in, "pipe", -1)
-    ffn_out_grad = owned(ffn_out_parts, 0, 1)
-    ffn_in_grad = owned(ffn_in_parts, 1, 1)
-    out_grad = owned(out_parts, 0, 1)
-    joined_grad = owned(joined_parts, 1, 3)
     vector_sums, slot_sums, grad_in = results
-    input_grad = to_positions(grad_in)
-
     stat_row = jnp.concatenate([stat_terms, jnp.zeros((width - 3,), f32)])[None]
     shared = jnp.concatenate([straightened(vector_sums), stat_row])
-    shared = summed_over(summed_over(summed_over(shared, "tp"), "zs"), "dp")
-    own_slot = slot_sums[0:1]
-    for by in range(1, seqs):
-        own_slot = own_slot + received(slot_sums[by : by + 1], "zs", -by)
-    own_slot = summed_over(own_slot, "dp")
+    if in_kernels:
+        small = jnp.concatenate([shared, jnp.zeros((7, width), f32)])
+        padded = -(-slot_sums.shape[1] // 1024) * 1024
+        slots = jnp.pad(slot_sums, ((0, 0), (0, padded - slot_sums.shape[1])))
+        all_parts = (ffn_out_parts, ffn_in_parts, out_parts, joined_parts)
+        by_block = straightened(grad_in).reshape(seqs, rows, width)
+        input_pieces, small, slots, *gradients = scatter_all(
+            by_block,
+            small,
+            slots.reshape(seqs, 8, padded // 8),
+            [parts[0] for parts in all_parts],
+            [parts[1] for parts in all_parts],
+            tp_size,
+        )
+        input_grad = in_positions([input_pieces[(seqs - by) % seqs][None] for by in range(seqs)])
+        shared, own_slot = small[:9], slots.reshape(1, padded)[:, : slot_sums.shape[1]]
+        ffn_out_grad, ffn_in_grad, out_grad = gradients[:3]
+        triple = gradients[3:]
+    else:
+        input_grad = in_positions(to_positions(grad_in))
+        shared = summed_over(summed_over(summed_over(shared, "tp"), "zs"), "dp")
+        own_slot = slot_sums[0:1]
+        for by in range(1, seqs):
+            own_slot = own_slot + received(slot_sums[by : by + 1], "zs", -by)
+        own_slot = summed_over(own_slot, "dp")
+        ffn_out_grad = owned(ffn_out_parts, 0, 1)
+        ffn_in_grad = owned(ffn_in_parts, 1, 1)
+        out_grad = owned(out_parts, 0, 1)
+        joined_grad = owned(joined_parts, 1, 3)
+        triple = [joined_grad[:, i * head_cols : (i + 1) * head_cols] for i in range(3)]
+    layer_out = in_positions(layer_pieces, grads[0])
     element_count = float(SEQ_LEN * seqs * dp_size * width)
     stats = jnp.sqrt(shared[8:9, :3] / element_count)
     return (
@@ -620,10 +1065,10 @@
         input_grad[None],
         shared[0:1],
         shared[1:2],
-        joined_grad[None, :, :head_cols],
+        triple[0][None],
         own_slot[:, :head_cols],
-        joined_grad[None, :, head_cols : 2 * head_cols],
-        joined_grad[None, :, 2 * head_cols :],
+        triple[1][None],
+        triple[2][None],
         own_slot[:, head_cols : 2 * head_cols],
         out_grad[None],
         shared[2:3],

time: 855 us -> 745 us (0.87)
  waiting for transfers between devices: 410 us -> 87.1 us
  Pallas kernels: 122 us -> 423 us
  starting transfers between devices: 94 us -> 16.9 us
  other arithmetic: 65.3 us -> 51.5 us
    ppermute x80 -> x22, waiting for transfers between devices: 382 us -> 32.8 us  [received(): lax.ppermute(shard, axis, [((i + by) % size, i) for i in range(size)])]
    pallas_call x0 -> x2, Pallas kernels: none -> 306 us  [the longest x1 165 us: scatter_all(): pl.pallas_call(functools.partial(scatter_kernel, seqs, dp_size, tp_size),...]
    ppermute x80 -> x22, starting transfers between devices: 88.2 us -> 12.1 us  [received(): lax.ppermute(shard, axis, [((i + by) % size, i) for i in range(size)])]
    ppermute x2, waiting for transfers between devices: 27.9 us -> 54.3 us  [passed_along(): return lax.ppermute(shard, axis, pairs)]
    another operation x5 -> x1, other arithmetic: 9.49 us -> 0.18 us  [run(): jax.shard_map(per_device, mesh=grouped, in_specs=(P(TENSOR, 'dp', None),...]
    unnamed x277 -> x225, local copies, waits for them, and re-layouts: 20.9 us -> 28.4 us
  transfers between devices with their start and end apart: 82 -> 24, of which waited for: 45 -> 14; matrix products, arithmetic and copies ran while one was open for 16% -> 9% of each run, Pallas kernels for 5% -> 6%
where the time goes in v2:
time: 745 us; the launch traced here: 738 us
  Pallas kernels  423 us (57%)
  matrix products  118 us (16%)
  waiting for transfers between devices  87.1 us (12%)
  other arithmetic  51.5 us (7%)
  local copies, waits for them, and re-layouts  38.8 us (5%)
  starting transfers between devices  16.9 us (2%)
    pallas_call x1, Pallas kernels, scatter_all(): pl.pallas_call(functools.partial(scatter_kernel, seqs, dp_size, tp_size),...  165 us
    pallas_call x1, Pallas kernels, gather_all(): pl.pallas_call(functools.partial(gather_kernel, seqs, dp_size), in_specs=...  142 us
    dot_general x30, matrix products, mm(): return lax.dot_general(a, b, (dims, ((), ())), preferred_element_type=f32)  118 us
    ppermute x2, waiting for transfers between devices, passed_along(): return lax.ppermute(shard, axis, pairs)  54.3 us
    pallas_call x2, Pallas kernels, attend_back(): pl.pallas_call(functools.partial(attend_back_kernel, rows), grid=(1,), in...  51.8 us
    pallas_call x2, Pallas kernels, attend(): pl.pallas_call(functools.partial(attend_kernel, rows), grid=(1,), in_spec...  33.6 us
    ppermute x22, waiting for transfers between devices, received(): lax.ppermute(shard, axis, [((i + by) % size, i) for i in range(size)])  32.8 us
    pallas_call x2, Pallas kernels, widen(): pl.pallas_call(functools.partial(widen_kernel, 144), grid=(units // step,...  31 us
  transfers between devices with their start and end apart: 24, of which 14 were waited for; matrix products, arithmetic and copies ran while one was open for 9% of the time, Pallas kernels for 6%

profile of v2, /device:TPU:0, one launch (start us, length us, event | category | flops | bytes accessed | tf_op | source)
XLA Modules:
  0.0 737.6 jit_solution(15384283835944575404)
XLA Ops:
  8.8 141.6 %shard_map.365 = (bf16[4,144,1024]{2,1,0:T(8,128)(2,1)}, f32[4,1,768]{2,1,0:T(1,128)}, bf16[1024,1536]{1,0:T(8,128)(2,1)}, bf16[512,1024]{1,0:T(8,128)(2,1)}, bf...) custom-call(bf16[4,144,1024]{2,1,0:T(8,128)(2,1)} %fusion.106.refs_0_, f32[1,768]{1,0:T(1,128)} %broadcast_in_dim.76.refs_1_, ...), custom_call_target="tpu_custom_call" | custom-call | tf_op jit(solution)/shard_map/pallas_call | solution.py:443
  155.0 7.3 fusion.32.q_ref.k_ref.v_ref
  162.3 16.8 %shard_map.366 = (bf16[1152,512]{1,0:T(8,128)(2,1)S(1)}, f32[4,2,1152]{2,1,0:T(2,128)S(1)}) custom-call(s32[8]{0:T(128)S(1)} %add.394.order, s32[2,9]{1,0:T(2,128)S(1)} %pad_add_fusion.span, s32[1152,1]{1,0:T(8,128)S(1)} %broadcast_in_dim.162.seg_c, s32[1,1152]{1,0:T(1,128)S(1)} %broadcast_in_dim.84.seg_r, bf16[1152,1536]{1,0:T(8,128)(2,1)S(1)} %fusion.32.q_ref.k_ref.v_ref, ...), custom_call_target="tpu_custom_call" | custom-call | tf_op jit(solution)/shard_map/pallas_call | solution.py:159
  180.2 2.7 collective-permute-done.1
  189.5 15.4 %shard_map.367 = (bf16[1152,2048]{1,0:T(8,128)(2,1)}, bf16[1152,2048]{1,0:T(8,128)(2,1)}) custom-call(bf16[1152,1024]{1,0:T(8,128)(2,1)S(1)} %pad_maximum_fusion.1.x_ref, bf16[1024,2048]{1,0:T(8,128)(2,1)S(1)} %copy-done.4, f32[1,2048]{1,0:T(1,128)S(1)} %bitcast.175), custom_call_target="tpu_custom_call" | custom-call | tf_op jit(solution)/shard_map/pallas_call | solution.py:265
  204.9 4.5 fusion.82
  209.6 2.7 collective-permute-done.3
  212.3 4.4 fusion.141
  218.2 3.5 collective-permute-start.4
  221.7 25.4 %collective-permute-done.4 = bf16[576,1024]{1,0:T(8,128)(2,1)S(1)} collective-permute-done((bf16[576,1024]{1,0:T(8,128)(2,1)S(1)}, bf16[576,1024]{1,0:T(8,128)(2,1)S(1)}, u32[]{:S(2)}, u32[]{:S(2)}) %collective-permute-start.4) | collective-permute-done | bytes 1179680 | tf_op jit(solution)/shard_map/ppermute | solution.py:39
  250.2 4.0 collective-permute-start.6
  254.7 5.3 fusion.33.q_ref.k_ref.v_ref
  260.1 16.7 %shard_map.368 = (bf16[1152,512]{1,0:T(8,128)(2,1)S(1)}, f32[4,2,1152]{2,1,0:T(2,128)S(1)}) custom-call(s32[8]{0:T(128)S(1)} %add.394.order, s32[2,9]{1,0:T(2,128)S(1)} %pad_add_fusion.span, s32[1152,1]{1,0:T(8,128)S(1)} %broadcast_in_dim.162.seg_c, s32[1,1152]{1,0:T(1,128)S(1)} %broadcast_in_dim.84.seg_r, bf16[1152,1536]{1,0:T(8,128)(2,1)S(1)} %fusion.33.q_ref.k_ref.v_ref, ...), custom_call_target="tpu_custom_call" | custom-call | tf_op jit(solution)/shard_map/pallas_call | solution.py:159
  276.9 3.7 collective-permute-done.7
  281.6 2.8 collective-permute-done.9
  287.9 2.7 collective-permute-done.10
  290.9 15.6 %shard_map.369 = (bf16[1152,2048]{1,0:T(8,128)(2,1)}, bf16[1152,2048]{1,0:T(8,128)(2,1)}) custom-call(bf16[1152,1024]{1,0:T(8,128)(2,1)S(1)} %pad_maximum_fusion.3.x_ref, bf16[1024,2048]{1,0:T(8,128)(2,1)S(1)} %copy-done.5, f32[1,2048]{1,0:T(1,128)S(1)} %bitcast.176), custom_call_target="tpu_custom_call" | custom-call | tf_op jit(solution)/shard_map/pallas_call | solution.py:265
  306.6 5.6 fusion.85
  315.2 3.9 multiply_reduce_fusion
  322.9 2.7 collective-permute-done.12
  325.6 10.4 %convert_reduce_fusion = (f32[2048]{0:T(1024)S(1)}, bf16[1152,2048]{1,0:T(8,128)(2,1)}) fusion(bf16[1152,2048]{1,0:T(8,128)(2,1)S(1)} %bitcast.265, bf16[2048,1024]{1,0:T(8,128)(2,1)} %get-tuple-element.137, bf16[576,1024]{1,0:T(8,128)(2,1)S(1)} %collective-permute-done.12, bf16[576,1024]{1,0:T(8,128)(2,1)S(1)} %get-tuple-element.263), kind=kOutput, calls=%fused_computation.34 | convolution fusion | flops 4848351232 | bytes 15998976 | tf_op jit(solution)/shard_map/dot_general | solution.py:73
  336.0 4.3 fusion.88
  343.3 5.6 multiply_reduce_fusion.6
  354.1 25.7 %shard_map.370 = (bf16[1152,512]{1,0:T(8,128)(2,1)S(1)}, bf16[1152,512]{1,0:T(8,128)(2,1)S(1)}, bf16[1152,512]{1,0:T(8,128)(2,1)S(1)}) custom-call(s32[8]{0:T(128)S(1)} %add.394.order, s32[2,9]{1,0:T(2,128)S(1)} %pad_add_fusion.span, s32[1152,1]{1,0:T(8,128)S(1)} %broadcast_in_dim.162.seg_c, s32[1,1152]{1,0:T(1,128)S(1)} %broadcast_in_dim.84.seg_r, ...), custom_call_target="tpu_custom_call" | custom-call | tf_op jit(solution)/shard_map/pallas_call | solution.py:221
  386.7 3.2 fusion.133
  391.4 28.9 %collective-permute-done.16 = bf16[576,1024]{1,0:T(8,128)(2,1)} collective-permute-done((bf16[576,1024]{1,0:T(8,128)(2,1)}, bf16[576,1024]{1,0:T(8,128)(2,1)}, u32[]{:S(2)}, u32[]{:S(2)}) %collective-permute-start.16) | collective-permute-done | bytes 1179680 | tf_op jit(solution)/shard_map/ppermute | solution.py:39
  422.7 3.7 convert_reduce_fusion.8
  429.5 3.2 pad_maximum_fusion.2
  434.6 8.4 %convert_reduce_fusion.1 = (f32[2048]{0:T(1024)S(1)}, bf16[1152,2048]{1,0:T(8,128)(2,1)S(1)}) fusion(bf16[1152,2048]{1,0:T(8,128)(2,1)} %get-tuple-element.149, bf16[2048,1024]{1,0:T(8,128)(2,1)S(1)} %copy-done.70, bf16[576,1024]{1,0:T(8,128)(2,1)S(1)} %collective-permute-done.17, bf16[576,1024]{1,0:T(8,128)(2,1)S(1)} %get-tuple-element.268), kind=kOutput, calls=%fused_computation.35 | convolution fusion | flops 4848351232 | bytes 15998976 | tf_op jit(solution)/shard_map/dot_general | solution.py:73
  443.1 3.7 fusion.91
  449.4 6.7 conditional.8
  449.4 3.3 fusion.4
  452.7 3.3 fusion.6
  458.1 9.2 %conditional.9 = (bf16[512,2048]{1,0:T(8,128)(2,1)S(1)}, bf16[512,2048]{1,0:T(8,128)(2,1)S(1)}) conditional(s32[]{:T(128)} %clamp.30, (bf16[1152,1024]{1,0:T(8,128)(2,1)}, bf16[1152,2048]{1,0:T(8,128)(2,1)}) %tuple.166, (bf16[1152,1024]{1,0:T(8,128)(2,1)S(1)}, bf16[1152,2048]{1,0:T(8,128)(2,1)}) %tuple.175), branch_computations={%region_24.25_spmd, %region_25.26_spmd} | conditional | flops 4831838208 | bytes 44302408 | solution.py:1095
  458.5 5.6 fusion.12
  464.2 3.1 fusion.14
  468.7 5.3 fusion.52
  485.4 3.3 pad_maximum_fusion.5
  489.4 3.0 convolution_convert_fusion.up_ref
  496.9 26.1 %shard_map.371 = (bf16[1152,512]{1,0:T(8,128)(2,1)S(1)}, bf16[1152,512]{1,0:T(8,128)(2,1)S(1)}, bf16[1152,512]{1,0:T(8,128)(2,1)S(1)}) custom-call(s32[8]{0:T(128)S(1)} %add.394.order, s32[2,9]{1,0:T(2,128)S(1)} %pad_add_fusion.span, s32[1152,1]{1,0:T(8,128)S(1)} %broadcast_in_dim.162.seg_c, s32[1,1152]{1,0:T(1,128)S(1)} %broadcast_in_dim.84.seg_r, ...), custom_call_target="tpu_custom_call" | custom-call | tf_op jit(solution)/shard_map/pallas_call | solution.py:221
  528.0 3.0 fusion.97
  536.3 7.1 conditional.11
  536.3 3.4 fusion.28
  539.7 3.5 fusion.30
  543.4 2.7 convert_reduce_fusion.3
  546.7 5.6 fusion.134
  554.3 4.0 broadcast_select_fusion.1
  559.0 164.6 %shard_map.372 = (bf16[4,144,1024]{2,1,0:T(8,128)(2,1)}, f32[16,1024]{1,0:T(8,128)}, f32[8,128]{1,0:T(8,128)}, f32[512,512]{1,0:T(8,128)}, f32[512,512]{1,0:T(8,...) custom-call(bf16[4,144,1024]{2,1,0:T(8,128)(2,1)} %bitcast.179, ...), custom_call_target="tpu_custom_call" | custom-call | tf_op jit(solution)/shard_map/pallas_call | solution.py:665
  (383 shorter events, 111.6 us)
Async XLA Ops:
  152.0 10.3 %copy-start.28 = (bf16[576,1024]{1,0:T(8,128)(2,1)}, bf16[576,1024]{1,0:T(8,128)(2,1)S(1)}, u32[]{:S(2)}) copy-start(bf16[576,1024]{1,0:T(8,128)(2,1)S(1)} %fusion.107) | copy-start | bytes 3538948
  152.1 2.9 collective-permute-start
  162.3 16.8 %copy-start.2 = (bf16[1152,1536]{1,0:T(8,128)(2,1)}, bf16[1152,1536]{1,0:T(8,128)(2,1)S(1)}, u32[]{:S(2)}) copy-start(bf16[1152,1536]{1,0:T(8,128)(2,1)S(1)} %fusion.32.q_ref.k_ref.v_ref) | copy-start | bytes 10616836
  162.3 16.9 %copy-start.82 = (bf16[512,1024]{1,0:T(8,128)(2,1)S(1)}, bf16[512,1024]{1,0:T(8,128)(2,1)}, u32[]{:S(2)}) copy-start(bf16[512,1024]{1,0:T(8,128)(2,1)} %get-tuple-element.134) | copy-start | bytes 3145732
  180.0 2.9 collective-permute-start.1
  185.3 27.0 %copy-start.7 = (f32[576,1024]{1,0:T(8,128)}, f32[576,1024]{1,0:T(8,128)S(1)}, u32[]{:S(2)}) copy-start(f32[576,1024]{1,0:T(8,128)S(1)} %get-tuple-element.326) | copy-start | bytes 7077892
  185.5 26.8 %copy-start.61 = (f32[576]{0:T(1024)}, f32[576]{0:T(1024)S(1)}, u32[]{:S(2)}) copy-start(f32[576]{0:T(1024)S(1)} %broadcast_multiply_fusion.11) | copy-start | bytes 6916
  185.9 26.4 %copy-start.63 = (f32[576]{0:T(1024)}, f32[576]{0:T(1024)S(1)}, u32[]{:S(2)}) copy-start(f32[576]{0:T(1024)S(1)} %add_rsqrt_fusion.3) | copy-start | bytes 6916
  186.4 2.9 collective-permute-start.2
  189.5 15.4 %copy-start.13 = (bf16[1152,1024]{1,0:T(8,128)(2,1)}, bf16[1152,1024]{1,0:T(8,128)(2,1)S(1)}, u32[]{:S(2)}) copy-start(bf16[1152,1024]{1,0:T(8,128)(2,1)S(1)} %pad_maximum_fusion.1.x_ref) | copy-start | bytes 7077892
  189.5 15.4 %copy-start.68 = (bf16[2048,1024]{1,0:T(8,128)(2,1)S(1)}, bf16[2048,1024]{1,0:T(8,128)(2,1)}, u32[]{:S(2)}) copy-start(bf16[2048,1024]{1,0:T(8,128)(2,1)} %get-tuple-element.137) | copy-start | bytes 12582916
  209.4 2.9 collective-permute-start.3
  217.1 31.6 %copy-start.43 = (bf16[144,4,1024]{2,1,0:T(4,128)(2,1)S(1)}, bf16[144,4,1024]{2,1,0:T(4,128)(2,1)}, u32[]{:S(2)}) copy-start(bf16[144,4,1024]{2,1,0:T(4,128)(2,1)} %param.31) | copy-start | bytes 3538948
  218.2 28.9 %collective-permute-start.4 = (bf16[576,1024]{1,0:T(8,128)(2,1)S(1)}, bf16[576,1024]{1,0:T(8,128)(2,1)S(1)}, u32[]{:S(2)}, u32[]{:S(2)}) collective-permute-start(bf16[576,1024]{1,0:T(8,128)(2,1)S(1)} %add_convert_fusion.1), channel_id=1, source_target_pairs={{0,16},{1,17},{2,18},{3,19},{4,20},{5,21},{6,22},{7,23},{8,24},{9,... | collective-permute-start | bytes 3538952 | tf_op jit(solution)/shard_map/ppermute | solution.py:39
  248.5 6.2 collective-permute-start.5
  250.2 26.7 %collective-permute-start.8 = (bf16[144,1024]{1,0:T(8,128)(2,1)S(1)}, bf16[144,1024]{1,0:T(8,128)(2,1)S(1)}, u32[]{:S(2)}, u32[]{:S(2)}) collective-permute-start(bf16[144,1024]{1,0:T(8,128)(2,1)S(1)} %get-tuple-element.296), channel_id=1, source_target_pairs={{6,0},{0,2},{2,4},{4,6},{7,1},{1,3},{3,5},{5,7},{14,8},{8,10},{10,... | collective-permute-start | bytes 884744 | tf_op jit(solution)/shard_map/ppermute | solution.py:33
  250.2 26.7 %collective-permute-start.6 = (bf16[144,1024]{1,0:T(8,128)(2,1)S(1)}, bf16[144,1024]{1,0:T(8,128)(2,1)S(1)}, u32[]{:S(2)}, u32[]{:S(2)}) collective-permute-start(bf16[144,1024]{1,0:T(8,128)(2,1)S(1)} %get-tuple-element.298), channel_id=1, source_target_pairs={{2,0},{4,2},{6,4},{0,6},{3,1},{5,3},{7,5},{1,7},{10,8},{12,10},{14... | collective-permute-start | bytes 884744 | tf_op jit(solution)/shard_map/ppermute | solution.py:33
  254.2 26.4 %collective-permute-start.7 = (bf16[144,1024]{1,0:T(8,128)(2,1)S(1)}, bf16[144,1024]{1,0:T(8,128)(2,1)S(1)}, u32[]{:S(2)}, u32[]{:S(2)}) collective-permute-start(bf16[144,1024]{1,0:T(8,128)(2,1)S(1)} %get-tuple-element.299), channel_id=1, source_target_pairs={{4,0},{6,2},{0,4},{2,6},{5,1},{7,3},{1,5},{3,7},{12,8},{14,10},{8,... | collective-permute-start | bytes 884744 | tf_op jit(solution)/shard_map/ppermute | solution.py:33
  260.1 16.8 %copy-start.3 = (bf16[1152,1536]{1,0:T(8,128)(2,1)}, bf16[1152,1536]{1,0:T(8,128)(2,1)S(1)}, u32[]{:S(2)}) copy-start(bf16[1152,1536]{1,0:T(8,128)(2,1)S(1)} %fusion.33.q_ref.k_ref.v_ref) | copy-start | bytes 10616836
  260.1 20.6 %copy-start.83 = (bf16[512,1024]{1,0:T(8,128)(2,1)S(1)}, bf16[512,1024]{1,0:T(8,128)(2,1)}, u32[]{:S(2)}) copy-start(bf16[512,1024]{1,0:T(8,128)(2,1)} %get-tuple-element.134) | copy-start | bytes 3145732
  260.1 24.3 %copy-start.86 = (f32[576,1024]{1,0:T(8,128)S(1)}, f32[576,1024]{1,0:T(8,128)}, u32[]{:S(2)}) copy-start(f32[576,1024]{1,0:T(8,128)} %get-tuple-element.327) | copy-start | bytes 7077892
  281.4 2.9 collective-permute-start.9
  287.7 2.9 collective-permute-start.10
  290.9 15.7 %copy-start.15 = (bf16[1152,1024]{1,0:T(8,128)(2,1)}, bf16[1152,1024]{1,0:T(8,128)(2,1)S(1)}, u32[]{:S(2)}) copy-start(bf16[1152,1024]{1,0:T(8,128)(2,1)S(1)} %pad_maximum_fusion.3.x_ref) | copy-start | bytes 7077892
  312.2 2.9 collective-permute-start.11
  319.1 24.2 %copy-start.11 = (f32[576,1024]{1,0:T(8,128)}, f32[576,1024]{1,0:T(8,128)S(1)}, u32[]{:S(2)}) copy-start(f32[576,1024]{1,0:T(8,128)S(1)} %get-tuple-element.285) | copy-start | bytes 7077892
  322.7 13.4 %copy-start.32 = (bf16[576,1024]{1,0:T(8,128)(2,1)}, bf16[576,1024]{1,0:T(8,128)(2,1)S(1)}, u32[]{:S(2)}) copy-start(bf16[576,1024]{1,0:T(8,128)(2,1)S(1)} %get-tuple-element.263) | copy-start | bytes 3538948
  322.7 2.9 collective-permute-start.12
  325.6 10.4 %copy-start.49 = (bf16[576,1024]{1,0:T(8,128)(2,1)}, bf16[576,1024]{1,0:T(8,128)(2,1)S(1)}, u32[]{:S(2)}) copy-start(bf16[576,1024]{1,0:T(8,128)(2,1)S(1)} %collective-permute-done.12) | copy-start | bytes 3538948
  340.3 2.9 collective-permute-start.13
  349.7 2.9 collective-permute-start.14
  383.8 2.9 collective-permute-start.15
  386.7 33.6 %copy-start.10 = (f32[576,1024]{1,0:T(8,128)S(1)}, f32[576,1024]{1,0:T(8,128)}, u32[]{:S(2)}) copy-start(f32[576,1024]{1,0:T(8,128)} %copy-done.9) | copy-start | bytes 7077892
  389.9 30.3 %collective-permute-start.16 = (bf16[576,1024]{1,0:T(8,128)(2,1)}, bf16[576,1024]{1,0:T(8,128)(2,1)}, u32[]{:S(2)}, u32[]{:S(2)}) collective-permute-start(bf16[576,1024]{1,0:T(8,128)(2,1)} %get-tuple-element.286), channel_id=1, source_target_pairs={{16,0},{17,1},{18,2},{19,3},{20,4},{21,5},{22,6},{23,7},{24,8},{25... | collective-permute-start | bytes 3538952 | tf_op jit(solution)/shard_map/ppermute | solution.py:39
  426.4 8.2 %collective-permute-start.17 = (bf16[576,1024]{1,0:T(8,128)(2,1)S(1)}, bf16[576,1024]{1,0:T(8,128)(2,1)S(1)}, u32[]{:S(2)}, u32[]{:S(2)}) collective-permute-start(bf16[576,1024]{1,0:T(8,128)(2,1)S(1)} %get-tuple-element.268), channel_id=1, source_target_pairs={{1,0},{0,1},{3,2},{2,3},{5,4},{4,5},{7,6},{6,7},{9,8},{8,9},{11,10... | collective-permute-start | bytes 3538952 | tf_op jit(solution)/shard_map/ppermute | solution.py:33
  432.7 14.9 %slice-start = ((s8[4718592]{0:T(1024)(128)(4,1)}), s8[4194304]{0:T(1024)(128)(4,1)S(1)}, s32[]{:S(2)}) async-start(s8[4718592]{0:T(1024)(128)(4,1)} %bitcast.260), calls=%async_computation | async-start | bytes 8388608
  432.7 15.0 %slice-start.2 = ((s8[4718592]{0:T(1024)(128)(4,1)}), s8[4194304]{0:T(1024)(128)(4,1)S(1)}, s32[]{:S(2)}) async-start(s8[4718592]{0:T(1024)(128)(4,1)} %bitcast.262), calls=%async_computation.2 | async-start | bytes 8388608
  434.6 13.1 %slice-start.1 = ((s8[4718592]{0:T(1024)(128)(4,1)}), s8[524288]{0:T(1024)(128)(4,1)S(1)}, s32[]{:S(2)}) async-start(s8[4718592]{0:T(1024)(128)(4,1)} %bitcast.260), calls=%async_computation.1 | async-start | bytes 1048576
  434.6 13.1 %slice-start.3 = ((s8[4718592]{0:T(1024)(128)(4,1)}), s8[524288]{0:T(1024)(128)(4,1)S(1)}, s32[]{:S(2)}) async-start(s8[4718592]{0:T(1024)(128)(4,1)} %bitcast.262), calls=%async_computation.3 | async-start | bytes 1048576
  446.7 27.3 %collective-permute-start.18 = (bf16[576,1024]{1,0:T(8,128)(2,1)}, bf16[576,1024]{1,0:T(8,128)(2,1)}, u32[]{:S(2)}, u32[]{:S(2)}) collective-permute-start(bf16[576,1024]{1,0:T(8,128)(2,1)} %fusion.91), channel_id=1, source_target_pairs={{1,0},{0,1},{3,2},{2,3},{5,4},{4,5},{7,6},{6,7},{9,8},{8,9},{11,10... | collective-permute-start | bytes 3538952 | tf_op jit(solution)/shard_map/ppermute | solution.py:33
  478.9 10.5 %collective-permute-start.19 = (bf16[576,1024]{1,0:T(8,128)(2,1)S(1)}, bf16[576,1024]{1,0:T(8,128)(2,1)}, u32[]{:S(2)}, u32[]{:S(2)}) collective-permute-start(bf16[576,1024]{1,0:T(8,128)(2,1)S(1)} %get-tuple-element.271), channel_id=1, source_target_pairs={{1,0},{0,1},{3,2},{2,3},{5,4},{4,5},{7,6},{6,7},{9,8},{8,9},{11,10... | collective-permute-start | bytes 3538952 | tf_op jit(solution)/shard_map/ppermute | solution.py:33
  480.5 42.5 %collective-permute-start.22 = (bf16[144,1024]{1,0:T(8,128)(2,1)}, bf16[144,1024]{1,0:T(8,128)(2,1)}, u32[]{:S(2)}, u32[]{:S(2)}) collective-permute-start(bf16[144,1024]{1,0:T(8,128)(2,1)} %get-tuple-element.292), channel_id=1, source_target_pairs={{6,0},{0,2},{2,4},{4,6},{7,1},{1,3},{3,5},{5,7},{14,8},{8,10},{10,... | collective-permute-start | bytes 884744 | tf_op jit(solution)/shard_map/ppermute | solution.py:33
  482.4 40.7 %collective-permute-start.21 = (bf16[144,1024]{1,0:T(8,128)(2,1)}, bf16[144,1024]{1,0:T(8,128)(2,1)}, u32[]{:S(2)}, u32[]{:S(2)}) collective-permute-start(bf16[144,1024]{1,0:T(8,128)(2,1)} %get-tuple-element.293), channel_id=1, source_target_pairs={{4,0},{6,2},{0,4},{2,6},{5,1},{7,3},{1,5},{3,7},{12,8},{14,10},{8,... | collective-permute-start | bytes 884744 | tf_op jit(solution)/shard_map/ppermute | solution.py:33
  483.0 40.1 %collective-permute-start.20 = (bf16[144,1024]{1,0:T(8,128)(2,1)}, bf16[144,1024]{1,0:T(8,128)(2,1)}, u32[]{:S(2)}, u32[]{:S(2)}) collective-permute-start(bf16[144,1024]{1,0:T(8,128)(2,1)} %get-tuple-element.294), channel_id=1, source_target_pairs={{2,0},{4,2},{6,4},{0,6},{3,1},{5,3},{7,5},{1,7},{10,8},{12,10},{14... | collective-permute-start | bytes 884744 | tf_op jit(solution)/shard_map/ppermute | solution.py:33
  496.9 26.1 %copy-start.53 = (bf16[512,512]{1,0:T(8,128)(2,1)}, bf16[512,512]{1,0:T(8,128)(2,1)S(1)}, u32[]{:S(2)}) copy-start(bf16[512,512]{1,0:T(8,128)(2,1)S(1)} %get-tuple-element.154.refs_9_) | copy-start | bytes 1572868
  496.9 26.1 %copy-start.55 = (bf16[512,512]{1,0:T(8,128)(2,1)}, bf16[512,512]{1,0:T(8,128)(2,1)S(1)}, u32[]{:S(2)}) copy-start(bf16[512,512]{1,0:T(8,128)(2,1)S(1)} %get-tuple-element.153.refs_5_) | copy-start | bytes 1572868
  531.1 15.7 %collective-permute-start.23 = (bf16[576,1024]{1,0:T(8,128)(2,1)}, bf16[576,1024]{1,0:T(8,128)(2,1)}, u32[]{:S(2)}, u32[]{:S(2)}) collective-permute-start(bf16[576,1024]{1,0:T(8,128)(2,1)} %fusion.97), channel_id=1, source_target_pairs={{1,0},{0,1},{3,2},{2,3},{5,4},{4,5},{7,6},{6,7},{9,8},{8,9},{11,10... | collective-permute-start | bytes 3538952 | tf_op jit(solution)/shard_map/ppermute | solution.py:33
  536.3 10.5 %copy-start.34 = (f32[576,1024]{1,0:T(8,128)S(1)}, f32[576,1024]{1,0:T(8,128)}, u32[]{:S(2)}) copy-start(f32[576,1024]{1,0:T(8,128)} %get-tuple-element.166) | copy-start | bytes 7077892
  (71 other events, 322.1 us)

commit v3 on v2

--- a/solution.py
+++ b/solution.py
@@ -12,6 +12,7 @@
 HDIM = 64
 SEQ_LEN = 1152
 STEPS = 5000
+ITEM_MOST = 525
 PAIR = 2 * HDIM
 TILE = 128
 AHEAD = 2
@@ -179,6 +180,25 @@
     )(order, span, segment[:, None], segment[None, :], qkv, qkv, qkv)
 
 
+def back_tile(at, to, seg_c, seg_r, lse_ref, q_s, k_s, v_s, up_s, dq_s, dk_s, dv_s):
+    same_item = seg_c[to, :] == seg_r[:, at]
+    same_item = jnp.concatenate([same_item, same_item], axis=1)
+    for pair in range(q_s.shape[1] // PAIR):
+        cols = slice(pair * PAIR, (pair + 1) * PAIR)
+        keys_all = k_s[to, cols]
+        queries, upstream = two_heads(q_s[at, cols]), two_heads(up_s[at, cols])
+        lse = jnp.concatenate([lse_ref[pair, 0:1, at], lse_ref[pair, 1:2, at]], axis=1)
+        scores = mm(keys_all, queries, ((1,), (1,))) * (SCALE * LOG2E)
+        probs = jnp.where(same_item, jnp.exp2(scores - lse), 0.0)
+        grad_probs = mm(v_s[to, cols], upstream, ((1,), (1,)))
+        weighted = probs * grad_probs
+        inner = jnp.sum(weighted, axis=0, keepdims=True)
+        grad_scores = (weighted - probs * inner).astype(bf16)
+        dv_s[to, cols] += mm(probs.astype(bf16), upstream)
+        dk_s[to, cols] += mm(grad_scores, queries)
+        dq_s[at, cols] = (one_pair(mm(grad_scores, keys_all, ((0,), (0,)))) * SCALE).astype(bf16)
+
+
 def attend_back_kernel(
     rows, order, span, seg_c, seg_r, q_ref, k_ref, v_ref, up_ref, lse_ref, dq_ref, dk_ref, dv_ref,
     q_s, k_s, v_s, up_s, dq_s, dk_s, dv_s,
@@ -189,22 +209,7 @@
     dv_s[...] = jnp.zeros_like(dv_s)
 
     def body(at, to):
-        same_item = seg_c[to, :] == seg_r[:, at]
-        same_item = jnp.concatenate([same_item, same_item], axis=1)
-        for pair in range(q_ref.shape[1] // PAIR):
-            cols = slice(pair * PAIR, (pair + 1) * PAIR)
-            keys_all = k_s[to, cols]
-            queries, upstream = two_heads(q_s[at, cols]), two_heads(up_s[at, cols])
-            lse = jnp.concatenate([lse_ref[pair, 0:1, at], lse_ref[pair, 1:2, at]], axis=1)
-            scores = mm(keys_all, queries, ((1,), (1,))) * (SCALE * LOG2E)
-            probs = jnp.where(same_item, jnp.exp2(scores - lse), 0.0)
-            grad_probs = mm(v_s[to, cols], upstream, ((1,), (1,)))
-            weighted = probs * grad_probs
-            inner = jnp.sum(weighted, axis=0, keepdims=True)
-            grad_scores = (weighted - probs * inner).astype(bf16)
-            dv_s[to, cols] += mm(probs.astype(bf16), upstream)
-            dk_s[to, cols] += mm(grad_scores, queries)
-            dq_s[at, cols] = (one_pair(mm(grad_scores, keys_all, ((0,), (0,)))) * SCALE).astype(bf16)
+        back_tile(at, to, seg_c, seg_r, lse_ref, q_s, k_s, v_s, up_s, dq_s, dk_s, dv_s)
 
     each_tile(span, q_ref.shape[0], body)
     q_s[...] = (dk_s[...] * SCALE).astype(bf16)
@@ -467,19 +472,30 @@
     )(by_seq, biases, *blocks)
 
 
-def scatter_kernel(seqs, dp_size, tp_size, *refs):
+def scatter_kernel(rows, seqs, dp_size, tp_size, *refs):
     seq_ref, small_ref, slots_ref = refs[:3]
-    mine, theirs = refs[3:7], refs[7:11]
-    seq_out, small_out, slots_out = refs[11:14]
-    outs = refs[14:20]
-    sides, ups, downs = refs[20:24], refs[24:28], refs[28:32]
-    small_zs, small_all, slots_zs, slots_dp = refs[32:36]
-    seq_send, seq_get, local_sem, small_send, small_get = refs[36:41]
-    side_send, side_get, up_send, up_get, down_send, down_get = refs[41:47]
+    mine, theirs = list(refs[3:6]), list(refs[6:9])
+    qkv_ref, up_ref, lse_ref, seg_c, seg_r, joined_ref, resid_ref, time_ref = refs[9:17]
+    tokens_last, tokens_before, gq_before = refs[17:20]
+    seq_out, small_out, slots_out = refs[20:23]
+    outs = refs[23:29]
+    sides, ups, downs = refs[29:33], refs[33:37], refs[37:41]
+    small_zs, small_all, slots_zs, slots_dp = refs[41:45]
+    seq_send, seq_get, local_sem, small_send, small_get = refs[45:50]
+    side_send, side_get, up_send, up_get, down_send, down_get = refs[50:56]
+    q_s, k_s, v_s, up_s, dq_s, dk_s, dv_s, gq_s, tokens_s = refs[56:65]
+    x_send, x_get, seq_s, small_s, slots_s, joined_mine, joined_theirs = refs[65:72]
+    place_sem, x_sem = refs[72:74]
+    mine.append(joined_mine)
+    theirs.append(joined_theirs)
+    first_stage = lax.axis_index("pipe") == 0
     zs, dp, tp = lax.axis_index("zs"), lax.axis_index("dp"), lax.axis_index("tp")
     units = mine[0].shape[0] // seqs
     hc = mine[2].shape[0] // seqs
     half = units // 2
+    length, heads_all = q_s.shape
+    own_count, width = resid_ref.shape
+    part = width // dp_size
     kinds = [(0, 0, 0, half), (0, 0, half, half), (1, 1, 0, half), (1, 1, half, half), (2, 0, 0, hc)]
     kinds += [(3, 1, third * seqs * hc, hc) for third in range(3)]
 
@@ -501,7 +517,7 @@
 
     def sequence(by):
         at = lax.rem(zs + by, seqs)
-        return to({"zs": at}, seq_ref.at[by], seq_out.at[by], seq_send.at[by], seq_get.at[by])
+        return to({"zs": at}, seq_s.at[by], seq_out.at[by], seq_send.at[by], seq_get.at[by])
 
     def side(kind, slot):
         place = side_send.at[kind, slot], side_get.at[kind, slot]
@@ -517,11 +533,11 @@
 
     def small(by):
         at = {"zs": lax.rem(zs + by, seqs)}
-        return to(at, small_ref, small_zs.at[by], small_send.at[0, by], small_get.at[0, by])
+        return to(at, small_s, small_zs.at[by], small_send.at[0, by], small_get.at[0, by])
 
     def slots(by):
         at = {"zs": lax.rem(zs + by, seqs)}
-        return to(at, slots_ref.at[by], slots_zs.at[by], small_send.at[1, by], small_get.at[1, by])
+        return to(at, slots_s.at[by], slots_zs.at[by], small_send.at[1, by], small_get.at[1, by])
 
     def small_across(by):
         at = lax.rem(dp * tp_size + tp + by, dp_size * tp_size)
@@ -560,27 +576,165 @@
         for slot in slot_order:
             side(kind, slot).start()
 
+    def placed(block, array):
+        member, chip = divmod(block, seqs)
+        at = lax.rem(zs + chip, seqs) * tp_size + lax.rem(tp + member, tp_size)
+        at = pl.ds(pl.multiple_of(at * rows, 16), rows)
+        here = slice(block * rows, (block + 1) * rows)
+        if array < 3:
+            source = qkv_ref.at[here, array * heads_all : (array + 1) * heads_all]
+        else:
+            source = up_ref.at[here, :]
+        target = (q_s, k_s, v_s, up_s)[array].at[at, :]
+        return pltpu.make_async_copy(source, target, place_sem.at[array, block])
+
+    def each_placed(act):
+        for array in range(4):
+            for block in range(length // rows):
+                act(placed(block, array))
+
+    own_tokens = pltpu.make_async_copy(tokens_last, tokens_s, local_sem.at[1])
+    old_tokens = pltpu.make_async_copy(tokens_before, tokens_s, local_sem.at[1])
+    old_grads = pltpu.make_async_copy(gq_before, gq_s, local_sem.at[2])
+    old_seq = pltpu.make_async_copy(seq_ref, seq_s, local_sem.at[3])
+
+    def attention(tiles):
+        reach = ITEM_MOST - 1
+        for tile in tiles:
+            low = max(0, (tile * TILE - reach) // TILE)
+            high = min(length, -(-((tile + 1) * TILE + reach) // TILE) * TILE)
+            back_tile(
+                slice(tile * TILE, (tile + 1) * TILE),
+                slice(low * TILE, high),
+                seg_c,
+                seg_r,
+                lse_ref,
+                q_s,
+                k_s,
+                v_s,
+                up_s,
+                dq_s,
+                dk_s,
+                dv_s,
+            )
+
+    def attention_start():
+        @pl.when(first_stage)
+        def _():
+            own_tokens.start()
+            each_placed(lambda copy: copy.start())
+            dk_s[...] = jnp.zeros_like(dk_s)
+            dv_s[...] = jnp.zeros_like(dv_s)
+            each_placed(lambda copy: copy.wait())
+            attention(range(length // TILE // 2))
+
+        @pl.when(jnp.logical_not(first_stage))
+        def _():
+            old_tokens.start()
+            old_grads.start()
+            old_seq.start()
+
+    def attention_end():
+        @pl.when(first_stage)
+        def _():
+            attention(range(length // TILE // 2, length // TILE))
+            q_s[...] = (dk_s[...] * SCALE).astype(bf16)
+            v_s[...] = dv_s[...].astype(bf16)
+            for third, source in enumerate((dq_s, q_s, v_s)):
+                cols = slice(third * heads_all, (third + 1) * heads_all)
+                for block in range(length // rows):
+                    member, chip = divmod(block, seqs)
+                    at = lax.rem(zs + chip, seqs) * tp_size + lax.rem(tp + member, tp_size)
+                    at = pl.ds(pl.multiple_of(at * rows, 16), rows)
+                    gq_s[block * rows : (block + 1) * rows, cols] = source[at, :]
+            own_tokens.wait()
+
+        @pl.when(jnp.logical_not(first_stage))
+        def _():
+            old_tokens.wait()
+            old_grads.wait()
+            old_seq.wait()
+
+    def joined_parts():
+        step = 256
+        for other in reversed(range(dp_size)):
+            target = joined_mine if other == 0 else joined_theirs
+            for third in range(3):
+                cols = slice(third * heads_all, (third + 1) * heads_all)
+                for at in range(0, part, step):
+                    left = tokens_s[:, other * part + at : other * part + at + step]
+                    target[at : at + step, cols] = mm(left, gq_s[:, cols], ((0,), (0,))).astype(bf16)
+
+    def exchange():
+        return to({"tp": 1 - tp}, x_send, x_get, x_sem.at[0], x_sem.at[1])
+
+    def input_grads():
+        @pl.when(first_stage)
+        def _():
+            def theirs_rows(i, carry):
+                at = pl.multiple_of(i * rows, 16)
+                x_send[pl.ds(at, rows), :] = mm(
+                    gq_s[pl.ds(own_count + at, rows), :], joined_ref[...], ((1,), (1,))
+                ).astype(bf16)
+                return carry
+
+            lax.fori_loop(0, seqs, theirs_rows, 0)
+            exchange().start()
+            for slot in range(seqs):
+                cols = slice(slot * hc, (slot + 1) * hc)
+                slots_s[slot, 0:1, :] = jnp.sum(gq_s[:, cols].astype(f32), axis=0, keepdims=True)
+                cols = slice(2 * heads_all + slot * hc, 2 * heads_all + (slot + 1) * hc)
+                slots_s[slot, 1:2, :] = jnp.sum(gq_s[:, cols].astype(f32), axis=0, keepdims=True)
+            exchange().wait()
+
+            def own_rows(i, carry):
+                at = pl.ds(pl.multiple_of(i * rows, 16), rows)
+                total = mm(gq_s[at, :], joined_ref[...], ((1,), (1,)))
+                total = total + x_get[at, :].astype(f32) + resid_ref[at, :]
+                lowered = total.astype(bf16)
+                for other in range(dp_size):
+                    cols = pl.ds(pl.multiple_of(lax.rem(dp + other, dp_size) * part, part), part)
+                    seq_s[i, :, cols] = lowered[:, other * part : (other + 1) * part]
+                timed = jnp.sum(total * time_ref[at, :], axis=0, keepdims=True)
+                plain = jnp.sum(total, axis=0, keepdims=True)
+                return carry[0] + timed, carry[1] + plain
+
+            zero = jnp.zeros((1, width), f32)
+            timed, plain = lax.fori_loop(0, seqs, own_rows, (zero, zero))
+            for other in range(dp_size):
+                cols = pl.ds(pl.multiple_of(lax.rem(dp + other, dp_size) * part, part), part)
+                here = slice(other * part, (other + 1) * part)
+                small_s[0:1, cols] = timed[:, here]
+                small_s[1:2, cols] = plain[:, here]
+
+    own_seq = pltpu.make_async_copy(seq_s.at[0], seq_out.at[0], local_sem.at[0])
+
+    def send_small():
+        for by in range(1, seqs):
+            small(by).start()
+            slots(by).start()
+        for by in range(1, seqs):
+            sequence(by).start()
+        own_seq.start()
+
+    def add_small():
+        total, slot_total = small_s[...], slots_s[0]
+        for by in range(1, seqs):
+            small(by).wait()
+            slots(by).wait()
+            total = total + small_zs[by]
+            slot_total = slot_total + slots_zs[by]
+        small_all[0] = total
+        slots_dp[0] = slot_total
+        for by in range(1, dp_size * tp_size):
+            small_across(by).start()
+        slots_across().start()
+
+    small_s[...] = small_ref[...]
+    slots_s[...] = slots_ref[...]
     for kind in range(AHEAD):
         begin(kind)
-    for by in range(1, seqs):
-        small(by).start()
-        slots(by).start()
-    for by in range(1, seqs):
-        sequence(by).start()
-    own_seq = pltpu.make_async_copy(seq_ref.at[0], seq_out.at[0], local_sem.at[0])
-    own_seq.start()
-
-    total, slot_total = small_ref[...], slots_ref[0]
-    for by in range(1, seqs):
-        small(by).wait()
-        slots(by).wait()
-        total = total + small_zs[by]
-        slot_total = slot_total + slots_zs[by]
-    small_all[0] = total
-    slots_dp[0] = slot_total
-    for by in range(1, dp_size * tp_size):
-        small_across(by).start()
-    slots_across().start()
+    attention_start()
 
     def taken(kind):
         for slot in slot_order:
@@ -612,7 +766,16 @@
         for hop in range(seqs - 1):
             if 0 <= step - hop < len(kinds):
                 pass_on(step - hop, hop)
-
+        if step == 0:
+            attention_end()
+        if step == 1:
+            joined_parts()
+            input_grads()
+            send_small()
+        if step == 4:
+            add_small()
+
+    total, slot_total = small_all[0], slots_dp[0]
     for by in range(1, dp_size * tp_size):
         small_across(by).wait()
         total = total + small_all[by]
@@ -651,20 +814,30 @@
         sequence(by).wait()
 
 
-def scatter_all(by_block, small, slots, mine, theirs, tp_size):
-    seqs = by_block.shape[0]
+def scatter_all(rows, by_block, small, slots, mine, theirs, attended, tokens, gq_before, tp_size):
+    seqs, _, width = by_block.shape
     units, part = mine[0].shape[0] // seqs, mine[0].shape[1]
     hc = mine[2].shape[0] // seqs
+    length, heads_all = tokens[0].shape[0], gq_before.shape[1] // 3
+    own_count = length // tp_size
     dp_size = 2
     anywhere = pl.BlockSpec(memory_space=pl.ANY)
     inside = pl.BlockSpec(memory_space=pltpu.VMEM)
     wide = lambda *shape: jax.ShapeDtypeStruct(shape, f32)
+    low = lambda *shape: pltpu.VMEM(shape, bf16)
     dma = pltpu.SemaphoreType.DMA
-    like = [pltpu.VMEM(block.shape, bf16) for block in mine]
+    like = [low(*block.shape) for block in mine] + [low(part, 3 * heads_all)]
+    fewer = [low((seqs - 1) * units, part), low(part, (seqs - 1) * units), low((seqs - 1) * hc, part)]
+    fewer.append(low(part, 3 * heads_all))
     kinds = 8
     return pl.pallas_call(
-        functools.partial(scatter_kernel, seqs, dp_size, tp_size),
-        in_specs=[anywhere, inside, inside] + [inside] * 4 + [anywhere] * 4,
+        functools.partial(scatter_kernel, rows, seqs, dp_size, tp_size),
+        in_specs=[anywhere, inside, inside]
+        + [inside] * 3
+        + [anywhere] * 3
+        + [anywhere, anywhere]
+        + [inside] * 6
+        + [anywhere] * 3,
         out_specs=[anywhere] + [inside] * 8,
         out_shape=[
             jax.ShapeDtypeStruct(by_block.shape, bf16),
@@ -677,7 +850,8 @@
             wide(part, hc),
             wide(part, hc),
         ],
-        scratch_shapes=like * 3
+        scratch_shapes=like
+        + fewer * 2
         + [
             pltpu.VMEM((seqs,) + small.shape, f32),
             pltpu.VMEM((dp_size * tp_size,) + small.shape, f32),
@@ -685,16 +859,30 @@
             pltpu.VMEM((2,) + slots.shape[1:], f32),
             dma((seqs,)),
             dma((seqs,)),
-            dma((1,)),
+            dma((4,)),
             dma((4, max(seqs, dp_size * tp_size))),
             dma((4, max(seqs, dp_size * tp_size))),
         ]
-        + [dma((kinds, seqs))] * 6,
-        input_output_aliases={},
+        + [dma((kinds, seqs))] * 6
+        + [low(length, heads_all)] * 5
+        + [pltpu.VMEM((length, heads_all), f32)] * 2
+        + [
+            low(length, 3 * heads_all),
+            low(length, width),
+            low(own_count, width),
+            low(own_count, width),
+            low(*by_block.shape),
+            pltpu.VMEM(small.shape, f32),
+            pltpu.VMEM(slots.shape, f32),
+            low(part, 3 * heads_all),
+            low(part, 3 * heads_all),
+            dma((4, length // rows)),
+            dma((2,)),
+        ],
         compiler_params=pltpu.CompilerParams(
-            collective_id=1, has_side_effects=True, vmem_limit_bytes=56 * 1024 * 1024
+            collective_id=1, has_side_effects=True, vmem_limit_bytes=63 * 1024 * 1024
         ),
-    )(by_block, small, slots, *mine, *theirs)
+    )(by_block, small, slots, *mine, *theirs, *attended, *tokens, gq_before)
 
 
 def per_device(
@@ -830,7 +1018,8 @@
         return whole
 
     biases = jnp.concatenate([query_bias[0], value_bias[0], ffn_in_bias[0].astype(f32)])[None]
-    in_kernels = dp_size == 2 and head_cols % 128 == 0 and part % 128 == 0 and unit_cols % 128 == 0
+    in_kernels = sections == 2 and dp_size == 2 and tp_size == 2 and rows % 16 == 0
+    in_kernels = in_kernels and head_cols == 128 and part % 256 == 0 and unit_cols % 256 == 0
     if in_kernels:
         by_seq = rotated(jnp.transpose(states, (1, 0, 2)))
         blocks = (query_weight, key_weight, value_weight, out_weight, ffn_in, ffn_out)
@@ -995,16 +1184,20 @@
         if last:
             out_parts = chosen(lambda a, b: parts_of(a, b, 1), for_out)
             grad_mixed = after(grad_mixed, *out_parts)
-        grads = attend_back(qkv, segment, span, kernel_order, kernel_rows, grad_mixed, lse)
-        grad_qkv = jnp.concatenate([by_distance(grad) for grad in grads], axis=1)
-        bias_sums = token_sum(grad_qkv)
-        for_joined.append((rounded_all, grad_qkv))
-        if last:
-            joined_parts = chosen(lambda a, b: parts_of(a, b, 0), for_joined)
-            grad_resid = after(grad_resid, *joined_parts)
-        grad_input = grad_resid + returned(grad_qkv, joined, ((1,), (1,)))
-        tw_grad, tb_grad = token_sum(grad_input * time_rows), token_sum(grad_input)
-        grad_in = grad_input.astype(bf16)
+        if last and in_kernels:
+            attended = (qkv, grad_mixed, lse, segment[:, None], segment[None, :], joined, grad_resid, time_rows)
+            tw_grad, tb_grad = jnp.zeros((width,), f32), jnp.zeros((width,), f32)
+            bias_sums, grad_in = jnp.zeros((3 * heads_all,), f32), results[2]
+        else:
+            grads = attend_back(qkv, segment, span, kernel_order, kernel_rows, grad_mixed, lse)
+            grad_qkv = jnp.concatenate([by_distance(grad) for grad in grads], axis=1)
+            bias_sums = token_sum(grad_qkv)
+            for_joined.append((rounded_all, grad_qkv))
+            if last:
+                joined_parts = chosen(lambda a, b: parts_of(a, b, 0), for_joined)
+            grad_input = grad_resid + returned(grad_qkv, joined, ((1,), (1,)))
+            tw_grad, tb_grad = token_sum(grad_input * time_rows), token_sum(grad_input)
+            grad_in = grad_input.astype(bf16)
         slot_sums = jnp.concatenate(
             [
                 bias_sums[:heads_all].reshape(seqs, head_cols),
@@ -1031,14 +1224,18 @@
         small = jnp.concatenate([shared, jnp.zeros((7, width), f32)])
         padded = -(-slot_sums.shape[1] // 1024) * 1024
         slots = jnp.pad(slot_sums, ((0, 0), (0, padded - slot_sums.shape[1])))
-        all_parts = (ffn_out_parts, ffn_in_parts, out_parts, joined_parts)
+        all_parts = (ffn_out_parts, ffn_in_parts, out_parts)
         by_block = straightened(grad_in).reshape(seqs, rows, width)
         input_pieces, small, slots, *gradients = scatter_all(
+            rows,
             by_block,
             small,
             slots.reshape(seqs, 8, padded // 8),
             [parts[0] for parts in all_parts],
             [parts[1] for parts in all_parts],
+            attended,
+            (rounded_all, for_joined[0][0]),
+            for_joined[0][1],
             tp_size,
         )
         input_grad = in_positions([input_pieces[(seqs - by) % seqs][None] for by in range(seqs)])
@@ -1057,7 +1254,7 @@
         out_grad = owned(out_parts, 0, 1)
         joined_grad = owned(joined_parts, 1, 3)
         triple = [joined_grad[:, i * head_cols : (i + 1) * head_cols] for i in range(3)]
-    layer_out = in_positions(layer_pieces, grads[0])
+    layer_out = in_positions(layer_pieces, grad_mixed)
     element_count = float(SEQ_LEN * seqs * dp_size * width)
     stats = jnp.sqrt(shared[8:9, :3] / element_count)
     return (

time: 745 us -> 697 us (0.936)
  Pallas kernels: 423 us -> 404 us
  matrix products: 118 us -> 104 us
  waiting for transfers between devices: 87.1 us -> 76.4 us
    pallas_call x2 -> x1, Pallas kernels: 51.8 us -> 25.8 us  [attend_back(): pl.pallas_call(functools.partial(attend_back_kernel, rows), grid=(1,), in...]
    dot_general x30 -> x26, matrix products: 118 us -> 104 us  [mm(): return lax.dot_general(a, b, (dims, ((), ())), preferred_element_type=f32)]
    ppermute x2, waiting for transfers between devices: 54.3 us -> 44.1 us  [passed_along(): return lax.ppermute(shard, axis, pairs)]
    reduce_sum x9 -> x8, other arithmetic: 18.1 us -> 16.6 us  [token_sum(): return jnp.sum(values.astype(f32), axis=0)]
    unnamed x225 -> x281, local copies, waits for them, and re-layouts: 28.4 us -> 27.5 us
    ppermute x22 -> x21, waiting for transfers between devices: 32.8 us -> 32.3 us  [received(): lax.ppermute(shard, axis, [((i + by) % size, i) for i in range(size)])]
  transfers between devices with their start and end apart: 24 -> 23, of which waited for: 14 -> 14; matrix products, arithmetic and copies ran while one was open for 9% -> 12% of each run, Pallas kernels for 6% -> 27%
where the time goes in v3:
time: 697 us; the launch traced here: 690 us
  Pallas kernels  404 us (58%)
  matrix products  104 us (15%)
  waiting for transfers between devices  76.4 us (11%)
  other arithmetic  50.8 us (7%)
  local copies, waits for them, and re-layouts  35.2 us (5%)
  starting transfers between devices  16.5 us (2%)
    pallas_call x1, Pallas kernels, scatter_all(): pl.pallas_call(functools.partial(scatter_kernel, rows, seqs, dp_size, tp_...  171 us
    pallas_call x1, Pallas kernels, gather_all(): pl.pallas_call(functools.partial(gather_kernel, seqs, dp_size), in_specs=...  142 us
    dot_general x26, matrix products, mm(): return lax.dot_general(a, b, (dims, ((), ())), preferred_element_type=f32)  104 us
    ppermute x2, waiting for transfers between devices, passed_along(): return lax.ppermute(shard, axis, pairs)  44.1 us
    pallas_call x2, Pallas kernels, attend(): pl.pallas_call(functools.partial(attend_kernel, rows), grid=(1,), in_spec...  34 us
    ppermute x21, waiting for transfers between devices, received(): lax.ppermute(shard, axis, [((i + by) % size, i) for i in range(size)])  32.3 us
    pallas_call x2, Pallas kernels, widen(): pl.pallas_call(functools.partial(widen_kernel, 144), grid=(units // step,...  31.3 us
    unnamed x281, local copies, waits for them, and re-layouts  27.5 us
  transfers between devices with their start and end apart: 23, of which 14 were waited for; matrix products, arithmetic and copies ran while one was open for 12% of the time, Pallas kernels for 27%

profile of v3, /device:TPU:0, one launch (start us, length us, event | category | flops | bytes accessed | tf_op | source)
XLA Modules:
  0.0 689.6 jit_solution(10676138342459156243)
XLA Ops:
  8.9 141.6 %shard_map.365 = (bf16[4,144,1024]{2,1,0:T(8,128)(2,1)}, f32[4,1,768]{2,1,0:T(1,128)}, bf16[1024,1536]{1,0:T(8,128)(2,1)}, bf16[512,1024]{1,0:T(8,128)(2,1)}, bf...) custom-call(bf16[4,144,1024]{2,1,0:T(8,128)(2,1)} %fusion.91.refs_0_, f32[1,768]{1,0:T(1,128)} %broadcast_in_dim.76.refs_1_, ...), custom_call_target="tpu_custom_call" | custom-call | tf_op jit(solution)/shard_map/pallas_call | solution.py:448
  155.1 7.3 %fusion.24.q_ref.k_ref.v_ref.refs_9_ = bf16[1152,1536]{1,0:T(8,128)(2,1)S(1)} fusion(bf16[1024,1536]{1,0:T(8,128)(2,1)} %get-tuple-element.109.refs_14_, f32[1536]{0:T(1024)S(1)} %constant_dynamic-update-slice_fusion.22, bf16[576,1024]{1,0:T(8,128)(2,1)S(1)} %collective-permute-done, bf16[576,1024]{1,0:T(8,128)(2,1)S(1)} %fusion.92), kind=kOutput, calls=%fused_computation.30 | convolution fusion | flops 3632136192 | bytes 9050112 | tf_op jit(solution)/shard_map/dot_general | solution.py:74
  162.4 17.0 %shard_map.366 = (bf16[1152,512]{1,0:T(8,128)(2,1)S(1)}, f32[4,2,1152]{2,1,0:T(2,128)S(1)}) custom-call(s32[8]{0:T(128)S(1)} %add.390.order, s32[2,9]{1,0:T(2,128)S(1)} %pad_add_fusion.span, s32[1152,1]{1,0:T(8,128)S(1)} %broadcast_in_dim.162.seg_c.refs_12_, s32[1,1152]{1,0:T(1,128)S(1)} %broadcast_in_dim.84.seg_r.refs_13_, ...), custom_call_target="tpu_custom_call" | custom-call | tf_op jit(solution)/shard_map/pallas_call | solution.py:160
  180.5 2.7 collective-permute-done.1
  186.9 2.7 collective-permute-done.2
  189.8 15.7 %shard_map.367 = (bf16[1152,2048]{1,0:T(8,128)(2,1)S(1)}, bf16[1152,2048]{1,0:T(8,128)(2,1)}) custom-call(bf16[1152,1024]{1,0:T(8,128)(2,1)S(1)} %pad_maximum_fusion.1.x_ref, bf16[1024,2048]{1,0:T(8,128)(2,1)S(1)} %copy-done.4, f32[1,2048]{1,0:T(1,128)S(1)} %bitcast.163), custom_call_target="tpu_custom_call" | custom-call | tf_op jit(solution)/shard_map/pallas_call | solution.py:270
  205.6 6.6 fusion.70
  212.3 2.7 collective-permute-done.3
  215.1 4.4 fusion.125
  220.9 3.4 collective-permute-start.4
  224.4 25.4 %collective-permute-done.4 = bf16[576,1024]{1,0:T(8,128)(2,1)S(1)} collective-permute-done((bf16[576,1024]{1,0:T(8,128)(2,1)S(1)}, bf16[576,1024]{1,0:T(8,128)(2,1)S(1)}, u32[]{:S(2)}, u32[]{:S(2)}) %collective-permute-start.4) | collective-permute-done | bytes 1179680 | tf_op jit(solution)/shard_map/ppermute | solution.py:40
  253.0 3.8 collective-permute-start.6
  256.9 5.3 fusion.25.q_ref.k_ref.v_ref
  262.2 17.0 %shard_map.368 = (bf16[1152,512]{1,0:T(8,128)(2,1)S(1)}, f32[4,2,1152]{2,1,0:T(2,128)S(1)}) custom-call(s32[8]{0:T(128)S(1)} %add.390.order, s32[2,9]{1,0:T(2,128)S(1)} %pad_add_fusion.span, s32[1152,1]{1,0:T(8,128)S(1)} %broadcast_in_dim.162.seg_c.refs_12_, s32[1,1152]{1,0:T(1,128)S(1)} %broadcast_in_dim.84.seg_r.refs_13_, ...), custom_call_target="tpu_custom_call" | custom-call | tf_op jit(solution)/shard_map/pallas_call | solution.py:160
  279.4 3.2 collective-permute-done.7
  283.5 2.8 collective-permute-done.9
  290.2 2.7 collective-permute-done.10
  293.1 15.6 %shard_map.369 = (bf16[1152,2048]{1,0:T(8,128)(2,1)}, bf16[1152,2048]{1,0:T(8,128)(2,1)}) custom-call(bf16[1152,1024]{1,0:T(8,128)(2,1)S(1)} %pad_maximum_fusion.3.x_ref, bf16[1024,2048]{1,0:T(8,128)(2,1)S(1)} %copy-done.5, f32[1,2048]{1,0:T(1,128)S(1)} %bitcast.164), custom_call_target="tpu_custom_call" | custom-call | tf_op jit(solution)/shard_map/pallas_call | solution.py:270
  308.8 5.6 fusion.73
  314.7 2.7 collective-permute-done.11
  317.4 3.9 multiply_reduce_fusion
  329.0 7.6 %convert_reduce_fusion = (f32[2048]{0:T(1024)}, bf16[1152,2048]{1,0:T(8,128)(2,1)}) fusion(bf16[1152,2048]{1,0:T(8,128)(2,1)S(1)} %bitcast.255, bf16[2048,1024]{1,0:T(8,128)(2,1)S(1)} %copy-done.98, bf16[576,1024]{1,0:T(8,128)(2,1)S(1)} %collective-permute-done.12, bf16[576,1024]{1,0:T(8,128)(2,1)S(1)} %get-tuple-element.233), kind=kOutput, calls=%fused_computation.26 | convolution fusion | flops 4848351232 | bytes 15998976 | tf_op jit(solution)/shard_map/dot_general | solution.py:74
  336.6 4.5 fusion.76
  344.0 4.3 multiply_reduce_fusion.6
  349.4 2.7 collective-permute-done.14
  353.6 25.8 %shard_map.370 = (bf16[1152,512]{1,0:T(8,128)(2,1)S(1)}, bf16[1152,512]{1,0:T(8,128)(2,1)S(1)}, bf16[1152,512]{1,0:T(8,128)(2,1)S(1)}) custom-call(s32[8]{0:T(128)S(1)} %add.390.order, s32[2,9]{1,0:T(2,128)S(1)} %pad_add_fusion.span, s32[1152,1]{1,0:T(8,128)S(1)} %broadcast_in_dim.162.seg_c.refs_12_, s32[1,1152]{1,0:T(1,128)S(1)} %broadcast_in_dim.84.seg_r.refs_13_, ...), custom_call_target="tpu_custom_call" | custom-call | tf_op jit(solution)/shard_map/pallas_call | solution.py:226
  383.6 2.7 collective-permute-done.15
  386.3 4.1 fusion.118
  392.7 2.7 multiply_reduce_fusion.2
  395.5 3.3 pad_maximum_fusion.refs_17_
  398.8 3.2 pad_maximum_fusion.2.refs_18_
  402.0 18.7 %collective-permute-done.16 = bf16[576,1024]{1,0:T(8,128)(2,1)} collective-permute-done((bf16[576,1024]{1,0:T(8,128)(2,1)}, bf16[576,1024]{1,0:T(8,128)(2,1)}, u32[]{:S(2)}, u32[]{:S(2)}) %collective-permute-start.16) | collective-permute-done | bytes 1179680 | tf_op jit(solution)/shard_map/ppermute | solution.py:40
  423.2 3.9 convert_reduce_fusion.7
  432.1 2.9 collective-permute-start.20
  438.4 8.7 %convert_reduce_fusion.1 = (f32[2048]{0:T(1024)S(1)}, bf16[1152,2048]{1,0:T(8,128)(2,1)S(1)}) fusion(bf16[1152,2048]{1,0:T(8,128)(2,1)} %get-tuple-element.127, bf16[2048,1024]{1,0:T(8,128)(2,1)S(1)} %copy-done.99, bf16[576,1024]{1,0:T(8,128)(2,1)} %collective-permute-done.17, bf16[576,1024]{1,0:T(8,128)(2,1)} %get-tuple-element.238), kind=kOutput, calls=%fused_computation.27 | convolution fusion | flops 4848351232 | bytes 15998976 | tf_op jit(solution)/shard_map/dot_general | solution.py:74
  447.1 3.7 fusion.79
  455.2 6.7 conditional.6
  455.2 3.3 fusion.4
  458.5 3.3 fusion.6
  463.9 9.2 %conditional.7 = (bf16[512,2048]{1,0:T(8,128)(2,1)S(1)}, bf16[512,2048]{1,0:T(8,128)(2,1)S(1)}) conditional(s32[]{:T(128)} %clamp.29, (bf16[1152,1024]{1,0:T(8,128)(2,1)}, bf16[1152,2048]{1,0:T(8,128)(2,1)}) %tuple.145, (bf16[1152,1024]{1,0:T(8,128)(2,1)S(1)}, bf16[1152,2048]{1,0:T(8,128)(2,1)}) %tuple.151), branch_computations={%region_24.25_spmd, %region_25.26_spmd} | conditional | flops 4831838208 | bytes 44302408 | solution.py:1292
  464.3 5.6 fusion.12
  469.9 3.1 fusion.14
  475.0 5.3 fusion.44
  485.6 3.9 broadcast_select_fusion.1
  489.7 2.9 fusion.89
  496.3 3.4 conditional.8
  499.7 3.7 convolution_convert_fusion.refs_10_
  503.4 171.1 %shard_map.371 = (bf16[4,144,1024]{2,1,0:T(8,128)(2,1)}, f32[16,1024]{1,0:T(8,128)}, f32[8,128]{1,0:T(8,128)}, f32[512,512]{1,0:T(8,128)}, f32[512,512]{1,0:T(8,...) custom-call(bf16[4,144,1024]{2,1,0:T(8,128)(2,1)} %bitcast.165, ...), custom_call_target="tpu_custom_call" | custom-call | tf_op jit(solution)/shard_map/pallas_call | solution.py:833
  (429 shorter events, 92.8 us)
Async XLA Ops:
  4.5 245.3 %copy-start.61 = (f32[576]{0:T(1024)}, f32[576]{0:T(1024)S(1)}, u32[]{:S(2)}) copy-start(f32[576]{0:T(1024)S(1)} %broadcast_multiply_fusion.12) | copy-start | bytes 6916
  5.4 177.8 %copy-start.92 = (f32[1,1024]{1,0:T(1,128)}, f32[1,1024]{1,0:T(1,128)S(1)}, u32[]{:S(2)}) copy-start(f32[1,1024]{1,0:T(1,128)S(1)} %get-tuple-element.281) | copy-start | bytes 12292
  5.5 209.6 %copy-start.54 = (f32[1,1024]{1,0:T(1,128)}, f32[1,1024]{1,0:T(1,128)S(1)}, u32[]{:S(2)}) copy-start(f32[1,1024]{1,0:T(1,128)S(1)} %get-tuple-element.280) | copy-start | bytes 12292
  5.5 209.6 %copy-start.80 = (f32[1,1024]{1,0:T(1,128)}, f32[1,1024]{1,0:T(1,128)S(1)}, u32[]{:S(2)}) copy-start(f32[1,1024]{1,0:T(1,128)S(1)} %get-tuple-element.279) | copy-start | bytes 12292
  5.5 209.6 %copy-start.88 = (f32[1,1024]{1,0:T(1,128)}, f32[1,1024]{1,0:T(1,128)S(1)}, u32[]{:S(2)}) copy-start(f32[1,1024]{1,0:T(1,128)S(1)} %get-tuple-element.278) | copy-start | bytes 12292
  5.5 214.4 %copy-start.51 = (f32[1,1024]{1,0:T(1,128)}, f32[1,1024]{1,0:T(1,128)S(1)}, u32[]{:S(2)}) copy-start(f32[1,1024]{1,0:T(1,128)S(1)} %get-tuple-element.277) | copy-start | bytes 12292
  5.5 214.4 %copy-start.78 = (f32[1,1024]{1,0:T(1,128)}, f32[1,1024]{1,0:T(1,128)S(1)}, u32[]{:S(2)}) copy-start(f32[1,1024]{1,0:T(1,128)S(1)} %get-tuple-element.284) | copy-start | bytes 12292
  5.5 244.3 %copy-start.68 = (f32[1,1024]{1,0:T(1,128)}, f32[1,1024]{1,0:T(1,128)S(1)}, u32[]{:S(2)}) copy-start(f32[1,1024]{1,0:T(1,128)S(1)} %get-tuple-element.282) | copy-start | bytes 12292
  5.5 244.3 %copy-start.71 = (f32[1,1024]{1,0:T(1,128)}, f32[1,1024]{1,0:T(1,128)S(1)}, u32[]{:S(2)}) copy-start(f32[1,1024]{1,0:T(1,128)S(1)} %get-tuple-element.283) | copy-start | bytes 12292
  152.2 2.9 collective-permute-start
  152.4 201.1 %copy-start.8 = (s32[1,1152]{1,0:T(1,128)}, s32[1,1152]{1,0:T(1,128)S(1)}, u32[]{:S(2)}) copy-start(s32[1,1152]{1,0:T(1,128)S(1)} %broadcast_in_dim.84.seg_r.refs_13_) | copy-start | bytes 13828
  152.7 200.9 %copy-start.7 = (s32[1152,1]{1,0:T(8,128)}, s32[1152,1]{1,0:T(8,128)S(1)}, u32[]{:S(2)}) copy-start(s32[1152,1]{1,0:T(8,128)S(1)} %broadcast_in_dim.162.seg_c.refs_12_) | copy-start | bytes 13828
  162.4 17.1 %copy-start.108 = (bf16[512,1024]{1,0:T(8,128)(2,1)S(1)}, bf16[512,1024]{1,0:T(8,128)(2,1)}, u32[]{:S(2)}) copy-start(bf16[512,1024]{1,0:T(8,128)(2,1)} %get-tuple-element.112) | copy-start | bytes 3145732
  180.3 2.9 collective-permute-start.1
  185.6 29.5 %copy-start.10 = (f32[576,1024]{1,0:T(8,128)}, f32[576,1024]{1,0:T(8,128)S(1)}, u32[]{:S(2)}) copy-start(f32[576,1024]{1,0:T(8,128)S(1)} %get-tuple-element.293) | copy-start | bytes 7077892
  185.8 29.3 %copy-start.59 = (f32[576]{0:T(1024)}, f32[576]{0:T(1024)S(1)}, u32[]{:S(2)}) copy-start(f32[576]{0:T(1024)S(1)} %broadcast_multiply_fusion.11) | copy-start | bytes 6916
  186.2 28.9 %copy-start.74 = (f32[576]{0:T(1024)}, f32[576]{0:T(1024)S(1)}, u32[]{:S(2)}) copy-start(f32[576]{0:T(1024)S(1)} %add_rsqrt_fusion.3) | copy-start | bytes 6916
  186.7 2.9 collective-permute-start.2
  212.1 2.9 collective-permute-start.3
  219.9 31.4 %copy-start.64 = (f32[576]{0:T(1024)}, f32[576]{0:T(1024)S(1)}, u32[]{:S(2)}) copy-start(f32[576]{0:T(1024)S(1)} %add_rsqrt_fusion.2) | copy-start | bytes 6916
  219.9 31.5 %copy-start.36 = (bf16[144,4,1024]{2,1,0:T(4,128)(2,1)S(1)}, bf16[144,4,1024]{2,1,0:T(4,128)(2,1)}, u32[]{:S(2)}) copy-start(bf16[144,4,1024]{2,1,0:T(4,128)(2,1)} %param.29) | copy-start | bytes 3538948
  220.9 28.9 %collective-permute-start.4 = (bf16[576,1024]{1,0:T(8,128)(2,1)S(1)}, bf16[576,1024]{1,0:T(8,128)(2,1)S(1)}, u32[]{:S(2)}, u32[]{:S(2)}) collective-permute-start(bf16[576,1024]{1,0:T(8,128)(2,1)S(1)} %add_convert_fusion.1), channel_id=1, source_target_pairs={{0,16},{1,17},{2,18},{3,19},{4,20},{5,21},{6,22},{7,23},{8,24},{9,... | collective-permute-start | bytes 3538952 | tf_op jit(solution)/shard_map/ppermute | solution.py:40
  251.3 5.5 collective-permute-start.5
  252.9 26.4 %collective-permute-start.8 = (bf16[144,1024]{1,0:T(8,128)(2,1)S(1)}, bf16[144,1024]{1,0:T(8,128)(2,1)S(1)}, u32[]{:S(2)}, u32[]{:S(2)}) collective-permute-start(bf16[144,1024]{1,0:T(8,128)(2,1)S(1)} %get-tuple-element.265), channel_id=1, source_target_pairs={{6,0},{0,2},{2,4},{4,6},{7,1},{1,3},{3,5},{5,7},{14,8},{8,10},{10,... | collective-permute-start | bytes 884744 | tf_op jit(solution)/shard_map/ppermute | solution.py:34
  253.0 26.4 %collective-permute-start.6 = (bf16[144,1024]{1,0:T(8,128)(2,1)S(1)}, bf16[144,1024]{1,0:T(8,128)(2,1)S(1)}, u32[]{:S(2)}, u32[]{:S(2)}) collective-permute-start(bf16[144,1024]{1,0:T(8,128)(2,1)S(1)} %get-tuple-element.267), channel_id=1, source_target_pairs={{2,0},{4,2},{6,4},{0,6},{3,1},{5,3},{7,5},{1,7},{10,8},{12,10},{14... | collective-permute-start | bytes 884744 | tf_op jit(solution)/shard_map/ppermute | solution.py:34
  256.8 25.8 %collective-permute-start.7 = (bf16[144,1024]{1,0:T(8,128)(2,1)S(1)}, bf16[144,1024]{1,0:T(8,128)(2,1)S(1)}, u32[]{:S(2)}, u32[]{:S(2)}) collective-permute-start(bf16[144,1024]{1,0:T(8,128)(2,1)S(1)} %get-tuple-element.268), channel_id=1, source_target_pairs={{4,0},{6,2},{0,4},{2,6},{5,1},{7,3},{1,5},{3,7},{12,8},{14,10},{8,... | collective-permute-start | bytes 884744 | tf_op jit(solution)/shard_map/ppermute | solution.py:34
  262.2 20.4 %copy-start.109 = (bf16[512,1024]{1,0:T(8,128)(2,1)S(1)}, bf16[512,1024]{1,0:T(8,128)(2,1)}, u32[]{:S(2)}) copy-start(bf16[512,1024]{1,0:T(8,128)(2,1)} %get-tuple-element.112) | copy-start | bytes 3145732
  262.2 24.1 %copy-start.114 = (f32[576,1024]{1,0:T(8,128)S(1)}, f32[576,1024]{1,0:T(8,128)}, u32[]{:S(2)}) copy-start(f32[576,1024]{1,0:T(8,128)} %get-tuple-element.294) | copy-start | bytes 7077892
  283.4 2.9 collective-permute-start.9
  290.0 2.9 collective-permute-start.10
  314.4 2.9 collective-permute-start.11
  321.3 22.7 %copy-start.66 = (f32[576]{0:T(1024)}, f32[576]{0:T(1024)S(1)}, u32[]{:S(2)}) copy-start(f32[576]{0:T(1024)S(1)} %broadcast_multiply_fusion.8) | copy-start | bytes 6916
  321.9 22.1 %copy-start.76 = (f32[576]{0:T(1024)}, f32[576]{0:T(1024)S(1)}, u32[]{:S(2)}) copy-start(f32[576]{0:T(1024)S(1)} %add_rsqrt_fusion) | copy-start | bytes 6916
  326.1 2.8 collective-permute-start.12
  341.1 2.9 collective-permute-start.13
  349.2 2.9 collective-permute-start.14
  383.3 2.9 collective-permute-start.15
  390.4 30.3 %collective-permute-start.16 = (bf16[576,1024]{1,0:T(8,128)(2,1)}, bf16[576,1024]{1,0:T(8,128)(2,1)}, u32[]{:S(2)}, u32[]{:S(2)}) collective-permute-start(bf16[576,1024]{1,0:T(8,128)(2,1)} %get-tuple-element.255), channel_id=1, source_target_pairs={{16,0},{17,1},{18,2},{19,3},{20,4},{21,5},{22,6},{23,7},{24,8},{25... | collective-permute-start | bytes 3538952 | tf_op jit(solution)/shard_map/ppermute | solution.py:40
  398.8 21.9 %copy-start.13 = (f32[576,1024]{1,0:T(8,128)S(1)}, f32[576,1024]{1,0:T(8,128)}, u32[]{:S(2)}) copy-start(f32[576,1024]{1,0:T(8,128)} %copy-done.12) | copy-start | bytes 7077892
  398.8 21.9 %copy-start.53 = (f32[1,1024]{1,0:T(1,128)S(1)}, f32[1,1024]{1,0:T(1,128)}, u32[]{:S(2)}) copy-start(f32[1,1024]{1,0:T(1,128)} %copy-done.51) | copy-start | bytes 12292
  398.8 21.9 %copy-start.58 = (f32[576]{0:T(1024)S(1)}, f32[576]{0:T(1024)}, u32[]{:S(2)}) copy-start(f32[576]{0:T(1024)} %copy-done.57) | copy-start | bytes 6916
  398.8 21.9 %copy-start.65 = (f32[576]{0:T(1024)S(1)}, f32[576]{0:T(1024)}, u32[]{:S(2)}) copy-start(f32[576]{0:T(1024)} %copy-done.64) | copy-start | bytes 6916
  427.0 11.4 %collective-permute-start.17 = (bf16[576,1024]{1,0:T(8,128)(2,1)}, bf16[576,1024]{1,0:T(8,128)(2,1)}, u32[]{:S(2)}, u32[]{:S(2)}) collective-permute-start(bf16[576,1024]{1,0:T(8,128)(2,1)} %get-tuple-element.238), channel_id=1, source_target_pairs={{1,0},{0,1},{3,2},{2,3},{5,4},{4,5},{7,6},{6,7},{9,8},{8,9},{11,10... | collective-permute-start | bytes 3538952 | tf_op jit(solution)/shard_map/ppermute | solution.py:34
  429.6 248.0 %collective-permute-start.22 = (bf16[144,1024]{1,0:T(8,128)(2,1)}, bf16[144,1024]{1,0:T(8,128)(2,1)S(1)}, u32[]{:S(2)}, u32[]{:S(2)}) collective-permute-start(bf16[144,1024]{1,0:T(8,128)(2,1)} %get-tuple-element.261), channel_id=1, source_target_pairs={{6,0},{0,2},{2,4},{4,6},{7,1},{1,3},{3,5},{5,7},{14,8},{8,10},{10,... | collective-permute-start | bytes 884744 | tf_op jit(solution)/shard_map/ppermute | solution.py:34
  429.6 248.0 %collective-permute-start.21 = (bf16[144,1024]{1,0:T(8,128)(2,1)}, bf16[144,1024]{1,0:T(8,128)(2,1)S(1)}, u32[]{:S(2)}, u32[]{:S(2)}) collective-permute-start(bf16[144,1024]{1,0:T(8,128)(2,1)} %get-tuple-element.262), channel_id=1, source_target_pairs={{4,0},{6,2},{0,4},{2,6},{5,1},{7,3},{1,5},{3,7},{12,8},{14,10},{8,... | collective-permute-start | bytes 884744 | tf_op jit(solution)/shard_map/ppermute | solution.py:34
  432.1 246.0 %collective-permute-start.20 = (bf16[144,1024]{1,0:T(8,128)(2,1)}, bf16[144,1024]{1,0:T(8,128)(2,1)}, u32[]{:S(2)}, u32[]{:S(2)}) collective-permute-start(bf16[144,1024]{1,0:T(8,128)(2,1)} %get-tuple-element.263), channel_id=1, source_target_pairs={{2,0},{4,2},{6,4},{0,6},{3,1},{5,3},{7,5},{1,7},{10,8},{12,10},{14... | collective-permute-start | bytes 884744 | tf_op jit(solution)/shard_map/ppermute | solution.py:34
  450.8 29.5 %collective-permute-start.18 = (bf16[576,1024]{1,0:T(8,128)(2,1)}, bf16[576,1024]{1,0:T(8,128)(2,1)}, u32[]{:S(2)}, u32[]{:S(2)}) collective-permute-start(bf16[576,1024]{1,0:T(8,128)(2,1)} %fusion.79), channel_id=1, source_target_pairs={{1,0},{0,1},{3,2},{2,3},{5,4},{4,5},{7,6},{6,7},{9,8},{8,9},{11,10... | collective-permute-start | bytes 3538952 | tf_op jit(solution)/shard_map/ppermute | solution.py:34
  485.3 8.6 %collective-permute-start.19 = (bf16[576,1024]{1,0:T(8,128)(2,1)S(1)}, bf16[576,1024]{1,0:T(8,128)(2,1)S(1)}, u32[]{:S(2)}, u32[]{:S(2)}) collective-permute-start(bf16[576,1024]{1,0:T(8,128)(2,1)S(1)} %get-tuple-element.241), channel_id=1, source_target_pairs={{1,0},{0,1},{3,2},{2,3},{5,4},{4,5},{7,6},{6,7},{9,8},{8,9},{11,10... | collective-permute-start | bytes 3538952 | tf_op jit(solution)/shard_map/ppermute | solution.py:34
  (99 other events, 572.1 us)

commit v4 on v3

--- a/solution.py
+++ b/solution.py
@@ -125,6 +125,32 @@
     lax.fori_loop(0, tiles, step, 0)
 
 
+def forward_tile(at, to, seg_c, seg_r, lse_ref, q_s, k_s, v_s, mixed_s):
+    same_item = seg_c[at, :] == seg_r[:, to]
+    same_item = jnp.concatenate([same_item, same_item], axis=0)
+    for pair in range(q_s.shape[1] // PAIR):
+        cols = slice(pair * PAIR, (pair + 1) * PAIR)
+        scores = mm(two_heads(q_s[at, cols]), k_s[to, cols], ((1,), (1,))) * (SCALE * LOG2E)
+        scores = jnp.where(same_item, scores, -1e30)
+        top = jnp.max(scores, axis=1, keepdims=True)
+        weights = jnp.exp2(scores - top)
+        total = jnp.sum(weights, axis=1, keepdims=True)
+        mixed = mm(weights.astype(bf16), v_s[to, cols]) * (1.0 / total)
+        mixed_s[at, cols] = one_pair(mixed).astype(bf16)
+        sums = top + jnp.log2(total)
+        spread = one_pair(jnp.broadcast_to(sums, (2 * TILE, PAIR))).T
+        lse_ref[pair, 0:1, at] = spread[0:1]
+        lse_ref[pair, 1:2, at] = spread[HDIM : HDIM + 1]
+
+
+def banded(tiles, length, body):
+    reach = ITEM_MOST - 1
+    for tile in tiles:
+        low = max(0, (tile * TILE - reach) // TILE)
+        high = min(length, -(-((tile + 1) * TILE + reach) // TILE) * TILE)
+        body(slice(tile * TILE, (tile + 1) * TILE), slice(low * TILE, high))
+
+
 def attend_kernel(
     rows, order, span, seg_c, seg_r, q_ref, k_ref, v_ref, mixed_ref, lse_ref, q_s, k_s, v_s, mixed_s
 ):
@@ -132,21 +158,7 @@
         place(order, source, target, rows, True)
 
     def body(at, to):
-        same_item = seg_c[at, :] == seg_r[:, to]
-        same_item = jnp.concatenate([same_item, same_item], axis=0)
-        for pair in range(q_ref.shape[1] // PAIR):
-            cols = slice(pair * PAIR, (pair + 1) * PAIR)
-            scores = mm(two_heads(q_s[at, cols]), k_s[to, cols], ((1,), (1,))) * (SCALE * LOG2E)
-            scores = jnp.where(same_item, scores, -1e30)
-            top = jnp.max(scores, axis=1, keepdims=True)
-            weights = jnp.exp2(scores - top)
-            total = jnp.sum(weights, axis=1, keepdims=True)
-            mixed = mm(weights.astype(bf16), v_s[to, cols]) * (1.0 / total)
-            mixed_s[at, cols] = one_pair(mixed).astype(bf16)
-            sums = top + jnp.log2(total)
-            spread = one_pair(jnp.broadcast_to(sums, (2 * TILE, PAIR))).T
-            lse_ref[pair, 0:1, at] = spread[0:1]
-            lse_ref[pair, 1:2, at] = spread[HDIM : HDIM + 1]
+        forward_tile(at, to, seg_c, seg_r, lse_ref, q_s, k_s, v_s, mixed_s)
 
     each_tile(span, q_ref.shape[0], body)
     place(order, mixed_s, mixed_ref, rows, False)
@@ -282,12 +294,18 @@
     )(x, weight, bias[None])
 
 
-def gather_kernel(seqs, dp_size, *refs):
+def gather_kernel(seqs, dp_size, tp_size, *refs):
     seq_ref, bias_ref = refs[:2]
     blocks = refs[2:8]
-    start_ref, biases_ref, joined_ref, out_ref, in_ref, ffn_out_ref = refs[8:14]
-    local_sem, seq_send, seq_get, up_send, up_get, down_send, down_get, side_send, side_get = refs[14:]
-    zs, dp = lax.axis_index("zs"), lax.axis_index("dp")
+    time_ref, time_weight, time_bias, seg_c, seg_r = refs[8:13]
+    start_ref, biases_ref, joined_ref, out_ref, in_ref, ffn_out_ref = refs[13:19]
+    tokens_ref, qkv_ref, mixed_ref, lse_ref = refs[19:23]
+    local_sem, seq_send, seq_get, up_send, up_get, down_send, down_get, side_send, side_get = refs[23:32]
+    start_s, joined_s, q_s, k_s, v_s, mixed_s, x_sem, load_sem = refs[32:]
+    zs, dp, tp = lax.axis_index("zs"), lax.axis_index("dp"), lax.axis_index("tp")
+    rows = seq_ref.shape[1]
+    own_count = seqs * rows
+    length, heads_all = mixed_ref.shape
     width, hc = blocks[0].shape
     units = blocks[4].shape[1]
     part = width // dp_size
@@ -351,7 +369,7 @@
         return pltpu.make_async_copy(own(kind, other), home(kind, 0, other), local_sem.at[kind, other])
 
     barrier = pltpu.get_barrier_semaphore()
-    for axis, at, size in (("zs", zs, seqs), ("dp", dp, dp_size)):
+    for axis, at, size in (("zs", zs, seqs), ("dp", dp, dp_size), ("tp", tp, tp_size)):
         for by in range(1, size):
             pl.semaphore_signal(
                 barrier,
@@ -359,7 +377,7 @@
                 device_id={axis: lax.rem(at + by, size)},
                 device_id_type=pl.DeviceIdType.MESH,
             )
-    pl.semaphore_wait(barrier, seqs + dp_size - 2)
+    pl.semaphore_wait(barrier, seqs + dp_size + tp_size - 3)
 
     for by in range(1, seqs):
         sequence(by).start()
@@ -409,24 +427,95 @@
             for other in range(1, dp_size):
                 side(kind, hop, other).start()
 
+    def exchange():
+        here, there = tokens_ref.at[:own_count, :], tokens_ref.at[own_count:, :]
+        return to("tp", 1 - tp, here, there, x_sem.at[0], x_sem.at[1])
+
+    def placed(block):
+        member, chip = divmod(block, seqs)
+        at = lax.rem(zs + chip, seqs) * tp_size + lax.rem(tp + member, tp_size)
+        return pl.ds(pl.multiple_of(at * rows, 16), rows)
+
+    load_start = pltpu.make_async_copy(start_ref, start_s, load_sem.at[0])
+    load_joined = pltpu.make_async_copy(joined_ref, joined_s, load_sem.at[1])
+
+    def tokens():
+        own_seq.wait()
+        for by in range(1, seqs):
+            sequence(by).wait()
+        load_start.start()
+        load_start.wait()
+        for block in range(seqs):
+            at = slice(block * rows, (block + 1) * rows)
+            residual = start_s[block].astype(f32) + time_ref[at, :] * time_weight[...] + time_bias[...]
+            tokens_ref[at, :] = residual.astype(bf16)
+        exchange().start()
+
+    def joined_there():
+        for kind in range(3):
+            for other in range(dp_size):
+                local(kind, other).wait()
+            for slot in range(1, seqs):
+                for other in range(1, dp_size):
+                    side(kind, slot, other).wait()
+        load_joined.start()
+        own_bias.wait()
+        for by in range(1, seqs):
+            bias(by).wait()
+        exchange().wait()
+        load_joined.wait()
+
+    def project(member):
+        here = slice(member * own_count, (member + 1) * own_count)
+        for third, target in enumerate((q_s, k_s, v_s)):
+            cols = slice(third * heads_all, (third + 1) * heads_all)
+            found = mm(tokens_ref[here, :], joined_s[:, cols])
+            if third != 1:
+                at = slice(third // 2 * hc, third // 2 * hc + hc)
+                found = found + jnp.concatenate([biases_ref[slot, :, at] for slot in range(seqs)], axis=1)
+            found = found.astype(bf16)
+            qkv_ref[here, cols] = found
+            for chip in range(seqs):
+                target[placed(member * seqs + chip), :] = found[chip * rows : (chip + 1) * rows]
+
+    def attention(tiles):
+        def body(at, to):
+            forward_tile(at, to, seg_c, seg_r, lse_ref, q_s, k_s, v_s, mixed_s)
+
+        banded(tiles, length, body)
+
+    def mixed_out():
+        for block in range(seqs * tp_size):
+            mixed_ref[block * rows : (block + 1) * rows, :] = mixed_s[placed(block), :]
+
+    tiles = length // TILE
     for step in range(len(kinds) + seqs - 2):
         for hop in range(1, seqs):
             if 0 <= step - hop + 1 < len(kinds):
                 pass_on(step - hop + 1, hop)
         if step + AHEAD < len(kinds):
             begin(step + AHEAD)
-
-    own_seq.wait()
-    own_bias.wait()
-    for by in range(1, seqs):
-        sequence(by).wait()
-        bias(by).wait()
+        if step == 2:
+            tokens()
+        if step == seqs:
+            joined_there()
+            for member in range(tp_size):
+                project(member)
+        if step == seqs + 1:
+            attention(range(tiles // 3))
+        if step == seqs + 2:
+            attention(range(tiles // 3, 2 * tiles // 3))
+        if step == seqs + 3:
+            attention(range(2 * tiles // 3, tiles))
+            mixed_out()
+
     for kind in kinds:
-        for other in range(dp_size):
-            local(kind, other).wait()
-        for slot in range(1, seqs):
-            for other in range(1, dp_size):
-                side(kind, slot, other).wait()
+        if kind >= 3:
+            for other in range(dp_size):
+                local(kind, other).wait()
+            for slot in range(1, seqs):
+                for other in range(1, dp_size):
+                    side(kind, slot, other).wait()
         for hop in range(seqs - 1):
 
             @pl.when((zs >= hop) & (zs < seqs - 1))
@@ -438,24 +527,31 @@
                 down(kind, hop).wait_send()
 
 
-def gather_all(by_seq, biases, blocks, dp_size):
-    seqs, _, width = by_seq.shape
+def gather_all(by_seq, biases, blocks, tokenwise, dp_size, tp_size):
+    seqs, rows, width = by_seq.shape
     hc, units = blocks[0].shape[1], blocks[4].shape[1]
+    length, heads_all = seqs * rows * tp_size, seqs * hc
     anywhere = pl.BlockSpec(memory_space=pl.ANY)
+    inside = pl.BlockSpec(memory_space=pltpu.VMEM)
     low = lambda *shape: jax.ShapeDtypeStruct(shape, bf16)
+    held = lambda *shape: pltpu.VMEM(shape, bf16)
     dma = pltpu.SemaphoreType.DMA
     kinds = 8
     return pl.pallas_call(
-        functools.partial(gather_kernel, seqs, dp_size),
-        in_specs=[anywhere] * (2 + len(blocks)),
-        out_specs=[anywhere] * 6,
+        functools.partial(gather_kernel, seqs, dp_size, tp_size),
+        in_specs=[anywhere] * (2 + len(blocks)) + [inside] * 5,
+        out_specs=[anywhere, inside] + [anywhere] * 4 + [inside] * 4,
         out_shape=[
             jax.ShapeDtypeStruct(by_seq.shape, bf16),
             jax.ShapeDtypeStruct((seqs,) + biases.shape, f32),
-            low(width, 3 * seqs * hc),
-            low(seqs * hc, width),
+            low(width, 3 * heads_all),
+            low(heads_all, width),
             low(width, seqs * units),
             low(seqs * units, width),
+            low(length, width),
+            low(length, 3 * heads_all),
+            low(length, heads_all),
+            jax.ShapeDtypeStruct((heads_all // PAIR, 2, length), f32),
         ],
         scratch_shapes=[
             dma((kinds + 1, max(dp_size, 2))),
@@ -467,33 +563,45 @@
             dma((kinds, seqs - 1)),
             dma((kinds, seqs, dp_size)),
             dma((kinds, seqs, dp_size)),
+            held(*by_seq.shape),
+            held(width, 3 * heads_all),
+            held(length, heads_all),
+            held(length, heads_all),
+            held(length, heads_all),
+            held(length, heads_all),
+            dma((2,)),
+            dma((2,)),
         ],
-        compiler_params=pltpu.CompilerParams(collective_id=0, has_side_effects=True),
-    )(by_seq, biases, *blocks)
+        compiler_params=pltpu.CompilerParams(
+            collective_id=0, has_side_effects=True, vmem_limit_bytes=56 * 1024 * 1024
+        ),
+    )(by_seq, biases, *blocks, *tokenwise)
 
 
 def scatter_kernel(rows, seqs, dp_size, tp_size, *refs):
     seq_ref, small_ref, slots_ref = refs[:3]
-    mine, theirs = list(refs[3:6]), list(refs[6:9])
-    qkv_ref, up_ref, lse_ref, seg_c, seg_r, joined_ref, resid_ref, time_ref = refs[9:17]
-    tokens_last, tokens_before, gq_before = refs[17:20]
-    seq_out, small_out, slots_out = refs[20:23]
-    outs = refs[23:29]
-    sides, ups, downs = refs[29:33], refs[33:37], refs[37:41]
-    small_zs, small_all, slots_zs, slots_dp = refs[41:45]
-    seq_send, seq_get, local_sem, small_send, small_get = refs[45:50]
-    side_send, side_get, up_send, up_get, down_send, down_get = refs[50:56]
-    q_s, k_s, v_s, up_s, dq_s, dk_s, dv_s, gq_s, tokens_s = refs[56:65]
-    x_send, x_get, seq_s, small_s, slots_s, joined_mine, joined_theirs = refs[65:72]
-    place_sem, x_sem = refs[72:74]
-    mine.append(joined_mine)
-    theirs.append(joined_theirs)
+    operands_before, operands_last = refs[3:9], refs[9:15]
+    qkv_ref, up_ref, lse_ref, seg_c, seg_r, joined_ref, resid_ref, time_ref = refs[15:23]
+    tokens_last, tokens_before, gq_before = refs[23:26]
+    seq_out, small_out, slots_out = refs[26:29]
+    outs = refs[29:35]
+    sides, ups, downs = refs[35:39], refs[39:43], refs[43:47]
+    small_zs, small_all, slots_zs, slots_dp = refs[47:51]
+    seq_send, seq_get, local_sem, small_send, small_get = refs[51:56]
+    side_send, side_get, up_send, up_get, down_send, down_get = refs[56:62]
+    wide_s, dq_s, dk_s, dv_s, gq_s, tokens_s = refs[62:68]
+    x_send, x_get, seq_s, small_s, slots_s = refs[68:73]
+    mine, theirs = refs[73:77], refs[77:81]
+    place_sem, x_sem, load_sem = refs[81:84]
+    joined_mine, joined_theirs = mine[3], theirs[3]
+    heads_all = dq_s.shape[1]
+    q_s, k_s, v_s, up_s = [wide_s.at[:, i * heads_all : (i + 1) * heads_all] for i in range(4)]
     first_stage = lax.axis_index("pipe") == 0
     zs, dp, tp = lax.axis_index("zs"), lax.axis_index("dp"), lax.axis_index("tp")
     units = mine[0].shape[0] // seqs
     hc = mine[2].shape[0] // seqs
     half = units // 2
-    length, heads_all = q_s.shape
+    length = dq_s.shape[0]
     own_count, width = resid_ref.shape
     part = width // dp_size
     kinds = [(0, 0, 0, half), (0, 0, half, half), (1, 1, 0, half), (1, 1, half, half), (2, 0, 0, hc)]
@@ -517,7 +625,7 @@
 
     def sequence(by):
         at = lax.rem(zs + by, seqs)
-        return to({"zs": at}, seq_s.at[by], seq_out.at[by], seq_send.at[by], seq_get.at[by])
+        return to({"zs": at}, seq_s.at[by], seq_out.at[zs], seq_send.at[by], seq_get.at[by])
 
     def side(kind, slot):
         place = side_send.at[kind, slot], side_get.at[kind, slot]
@@ -599,24 +707,10 @@
     old_seq = pltpu.make_async_copy(seq_ref, seq_s, local_sem.at[3])
 
     def attention(tiles):
-        reach = ITEM_MOST - 1
-        for tile in tiles:
-            low = max(0, (tile * TILE - reach) // TILE)
-            high = min(length, -(-((tile + 1) * TILE + reach) // TILE) * TILE)
-            back_tile(
-                slice(tile * TILE, (tile + 1) * TILE),
-                slice(low * TILE, high),
-                seg_c,
-                seg_r,
-                lse_ref,
-                q_s,
-                k_s,
-                v_s,
-                up_s,
-                dq_s,
-                dk_s,
-                dv_s,
-            )
+        def body(at, to):
+            back_tile(at, to, seg_c, seg_r, lse_ref, q_s, k_s, v_s, up_s, dq_s, dk_s, dv_s)
+
+        banded(tiles, length, body)
 
     def attention_start():
         @pl.when(first_stage)
@@ -707,7 +801,7 @@
                 small_s[0:1, cols] = timed[:, here]
                 small_s[1:2, cols] = plain[:, here]
 
-    own_seq = pltpu.make_async_copy(seq_s.at[0], seq_out.at[0], local_sem.at[0])
+    own_seq = pltpu.make_async_copy(seq_s.at[0], seq_out.at[zs], local_sem.at[0])
 
     def send_small():
         for by in range(1, seqs):
@@ -732,8 +826,53 @@
 
     small_s[...] = small_ref[...]
     slots_s[...] = slots_ref[...]
-    for kind in range(AHEAD):
-        begin(kind)
+    def load(index, target):
+        def copies(operands):
+            return pltpu.make_async_copy(operands[index], target, load_sem.at[index])
+
+        @pl.when(first_stage)
+        def _():
+            copies(operands_last).start()
+
+        @pl.when(jnp.logical_not(first_stage))
+        def _():
+            copies(operands_before).start()
+
+        return copies(operands_last)
+
+    def product(kind, other):
+        array, axis, first, size = kinds[kind]
+        target = (mine if other == 0 else theirs)[array]
+        features = slice(other * part, (other + 1) * part)
+        for slot in range(seqs):
+            apart = units if array < 2 else hc
+            at = slice(first + slot * apart, first + slot * apart + size)
+            if axis == 0:
+                left = dq_s if array == 2 else wide_s
+                target[at, :] = mm(left[:, at], tokens_s[:, features], ((0,), (0,))).astype(bf16)
+            else:
+                found = mm(tokens_s[:, features], wide_s[:, at], ((0,), (0,)))
+                target[:, at] = found.astype(bf16)
+
+    hidden, grads = load(0, wide_s), load(1, tokens_s)
+    hidden.wait()
+    grads.wait()
+    for kind in (0, 1):
+        for other in reversed(range(dp_size)):
+            product(kind, other)
+            if other == 1:
+                begin(kind)
+    inputs, grads = load(2, tokens_s), load(3, wide_s)
+    inputs.wait()
+    grads.wait()
+    for kind in (2, 3):
+        for other in range(dp_size):
+            product(kind, other)
+    mixed, grads = load(4, dq_s), load(5, tokens_s)
+    mixed.wait()
+    grads.wait()
+    for other in range(dp_size):
+        product(4, other)
     attention_start()
 
     def taken(kind):
@@ -814,27 +953,26 @@
         sequence(by).wait()
 
 
-def scatter_all(rows, by_block, small, slots, mine, theirs, attended, tokens, gq_before, tp_size):
+def scatter_all(rows, by_block, small, slots, operands, attended, tokens, gq_before, tp_size):
     seqs, _, width = by_block.shape
-    units, part = mine[0].shape[0] // seqs, mine[0].shape[1]
-    hc = mine[2].shape[0] // seqs
+    dp_size = 2
+    units, part = operands[0].shape[1] // seqs, width // dp_size
     length, heads_all = tokens[0].shape[0], gq_before.shape[1] // 3
+    hc = heads_all // seqs
     own_count = length // tp_size
-    dp_size = 2
     anywhere = pl.BlockSpec(memory_space=pl.ANY)
     inside = pl.BlockSpec(memory_space=pltpu.VMEM)
     wide = lambda *shape: jax.ShapeDtypeStruct(shape, f32)
     low = lambda *shape: pltpu.VMEM(shape, bf16)
     dma = pltpu.SemaphoreType.DMA
-    like = [low(*block.shape) for block in mine] + [low(part, 3 * heads_all)]
+    like = [low(seqs * units, part), low(part, seqs * units), low(heads_all, part), low(part, 3 * heads_all)]
     fewer = [low((seqs - 1) * units, part), low(part, (seqs - 1) * units), low((seqs - 1) * hc, part)]
     fewer.append(low(part, 3 * heads_all))
     kinds = 8
     return pl.pallas_call(
         functools.partial(scatter_kernel, rows, seqs, dp_size, tp_size),
         in_specs=[anywhere, inside, inside]
-        + [inside] * 3
-        + [anywhere] * 3
+        + [anywhere] * 12
         + [anywhere, anywhere]
         + [inside] * 6
         + [anywhere] * 3,
@@ -864,7 +1002,7 @@
             dma((4, max(seqs, dp_size * tp_size))),
         ]
         + [dma((kinds, seqs))] * 6
-        + [low(length, heads_all)] * 5
+        + [low(length, 4 * heads_all), low(length, heads_all)]
         + [pltpu.VMEM((length, heads_all), f32)] * 2
         + [
             low(length, 3 * heads_all),
@@ -874,15 +1012,13 @@
             low(*by_block.shape),
             pltpu.VMEM(small.shape, f32),
             pltpu.VMEM(slots.shape, f32),
-            low(part, 3 * heads_all),
-            low(part, 3 * heads_all),
-            dma((4, length // rows)),
-            dma((2,)),
-        ],
+        ]
+        + like * 2
+        + [dma((4, length // rows)), dma((2,)), dma((6,))],
         compiler_params=pltpu.CompilerParams(
             collective_id=1, has_side_effects=True, vmem_limit_bytes=63 * 1024 * 1024
         ),
-    )(by_block, small, slots, *mine, *theirs, *attended, *tokens, gq_before)
+    )(by_block, small, slots, *operands, *attended, *tokens, gq_before)
 
 
 def per_device(
@@ -951,10 +1087,14 @@
         return [received(by_block[(seqs - by) % seqs], "zs", by)[None] for by in range(seqs)]
 
     def in_positions(got, *before):
-        got = [after(piece, *before) for piece in got]
-        twice = jnp.concatenate(got + got)
-        by_seq = lax.dynamic_slice_in_dim(twice, (seqs - zs_at) % seqs, seqs, 0)
-        return jnp.transpose(by_seq, (1, 0, 2))
+        got = [after(piece, *before)[0] for piece in got]
+        by_seq = []
+        for at in range(seqs):
+            found = got[0]
+            for by in range(1, seqs):
+                found = jnp.where((zs_at + by) % seqs == at, got[by], found)
+            by_seq.append(found)
+        return jnp.stack(by_seq, axis=1)
 
     item_ends = jnp.cumsum(lax.dynamic_index_in_dim(lengths, zs_at, 0, keepdims=False))
     own_times = lax.dynamic_index_in_dim(timesteps, zs_at, 0, keepdims=False).astype(f32)
@@ -1023,8 +1163,9 @@
     if in_kernels:
         by_seq = rotated(jnp.transpose(states, (1, 0, 2)))
         blocks = (query_weight, key_weight, value_weight, out_weight, ffn_in, ffn_out)
-        start, bias_slots, joined, out_all, in_all, ffn_out_all = gather_all(
-            by_seq, biases, [block[0] for block in blocks], dp_size
+        tokenwise = (time_rows, time_weight[None], time_bias[None], segment[:, None], segment[None, :])
+        start, bias_slots, joined, out_all, in_all, ffn_out_all, *attended_first = gather_all(
+            by_seq, biases, [block[0] for block in blocks], tokenwise, dp_size, tp_size
         )
         start_rows = start.reshape(own_count, width)
         bias_slots = bias_slots[:, 0]
@@ -1061,9 +1202,12 @@
     inputs = start_rows
     for tick in range(sections):
         residual = inputs.astype(f32) + time_rows * time_weight + time_bias
-        rounded_all = everyone(residual.astype(bf16))
-        qkv = by_position((mm(rounded_all, joined) + joined_bias).astype(bf16))
-        mixed, lse = attend(qkv, segment, span, kernel_order, kernel_rows)
+        if tick == 0 and in_kernels:
+            rounded_all, qkv, mixed, lse = attended_first
+        else:
+            rounded_all = everyone(residual.astype(bf16))
+            qkv = by_position((mm(rounded_all, joined) + joined_bias).astype(bf16))
+            mixed, lse = attend(qkv, segment, span, kernel_order, kernel_rows)
         if tick == 1:
             mixed = after(mixed, *upstream_pieces)
         mixed = by_distance(mixed)
@@ -1169,7 +1313,7 @@
         grad_pre = (mm(grad_ffn_all, ffn_out_all, ((1,), (1,))) * slope.astype(f32)).astype(bf16)
         in_bias_sum = token_sum(grad_pre)
         for_ffn.append((hidden, grad_ffn_all, first_all, grad_pre))
-        if last:
+        if last and not in_kernels:
             ffn_out_parts = chosen(lambda a, b, c, d: parts_of(a, b, 1), for_ffn)
             ffn_in_parts = chosen(lambda a, b, c, d: parts_of(c, d, 0), for_ffn)
             grad_second = after(grad_second, *ffn_out_parts, *ffn_in_parts)
@@ -1181,13 +1325,15 @@
         branch_all = everyone(grad_branch)
         grad_mixed = by_position(mm(branch_all, out_all, ((1,), (1,))).astype(bf16))
         for_out.append((mixed, branch_all))
-        if last:
+        if last and not in_kernels:
             out_parts = chosen(lambda a, b: parts_of(a, b, 1), for_out)
             grad_mixed = after(grad_mixed, *out_parts)
         if last and in_kernels:
             attended = (qkv, grad_mixed, lse, segment[:, None], segment[None, :], joined, grad_resid, time_rows)
             tw_grad, tb_grad = jnp.zeros((width,), f32), jnp.zeros((width,), f32)
-            bias_sums, grad_in = jnp.zeros((3 * heads_all,), f32), results[2]
+            bias_sums, grad_in_before = jnp.zeros((3 * heads_all,), f32), results[2]
+            grad_in = jnp.zeros((), bf16)
+            results = (results[0], results[1], grad_in)
         else:
             grads = attend_back(qkv, segment, span, kernel_order, kernel_rows, grad_mixed, lse)
             grad_qkv = jnp.concatenate([by_distance(grad) for grad in grads], axis=1)
@@ -1224,21 +1370,19 @@
         small = jnp.concatenate([shared, jnp.zeros((7, width), f32)])
         padded = -(-slot_sums.shape[1] // 1024) * 1024
         slots = jnp.pad(slot_sums, ((0, 0), (0, padded - slot_sums.shape[1])))
-        all_parts = (ffn_out_parts, ffn_in_parts, out_parts)
-        by_block = straightened(grad_in).reshape(seqs, rows, width)
+        by_block = straightened(grad_in_before).reshape(seqs, rows, width)
         input_pieces, small, slots, *gradients = scatter_all(
             rows,
             by_block,
             small,
             slots.reshape(seqs, 8, padded // 8),
-            [parts[0] for parts in all_parts],
-            [parts[1] for parts in all_parts],
+            [operand for each in zip(for_ffn, for_out) for pair in each for operand in pair],
             attended,
             (rounded_all, for_joined[0][0]),
             for_joined[0][1],
             tp_size,
         )
-        input_grad = in_positions([input_pieces[(seqs - by) % seqs][None] for by in range(seqs)])
+        input_grad = jnp.transpose(input_pieces, (1, 0, 2))
         shared, own_slot = small[:9], slots.reshape(1, padded)[:, : slot_sums.shape[1]]
         ffn_out_grad, ffn_in_grad, out_grad = gradients[:3]
         triple = gradients[3:]

time: 697 us -> 675 us (0.968)
  matrix products: 104 us -> 83.6 us
  waiting for transfers between devices: 76.4 us -> 84.6 us
  local copies, waits for them, and re-layouts: 35.2 us -> 28.2 us
    dot_general x26 -> x19, matrix products: 104 us -> 83.6 us  [mm(): return lax.dot_general(a, b, (dims, ((), ())), preferred_element_type=f32)]
    pallas_call x2 -> x1, Pallas kernels: 34 us -> 16.6 us  [attend(): pl.pallas_call(functools.partial(attend_kernel, rows), grid=(1,), in_spec...]
    pallas_call x1, Pallas kernels: 171 us -> 183 us  [scatter_all(): pl.pallas_call(functools.partial(scatter_kernel, rows, seqs, dp_size, tp_...]
    unnamed x281 -> x139, local copies, waits for them, and re-layouts: 27.5 us -> 17.5 us
    ppermute x2, waiting for transfers between devices: 44.1 us -> 54.1 us  [passed_along(): return lax.ppermute(shard, axis, pairs)]
    reduce_sum x8 -> x7, other arithmetic: 16.6 us -> 13.3 us  [token_sum(): return jnp.sum(values.astype(f32), axis=0)]
    ppermute x21 -> x20, waiting for transfers between devices: 32.3 us -> 30.5 us  [received(): lax.ppermute(shard, axis, [((i + by) % size, i) for i in range(size)])]
  transfers between devices with their start and end apart: 23 -> 22, of which waited for: 14 -> 13; matrix products, arithmetic and copies ran while one was open for 12% -> 10% of each run, Pallas kernels for 27% -> 30%
where the time goes in v4:
time: 675 us; the launch traced here: 665 us
  Pallas kernels  405 us (60%)
  waiting for transfers between devices  84.6 us (13%)
  matrix products  83.6 us (12%)
  other arithmetic  48.9 us (7%)
  local copies, waits for them, and re-layouts  28.2 us (4%)
  starting transfers between devices  13.2 us (2%)
    pallas_call x1, Pallas kernels, scatter_all(): pl.pallas_call(functools.partial(scatter_kernel, rows, seqs, dp_size, tp_...  183 us
    pallas_call x1, Pallas kernels, gather_all(): pl.pallas_call(functools.partial(gather_kernel, seqs, dp_size, tp_size),...  147 us
    dot_general x19, matrix products, mm(): return lax.dot_general(a, b, (dims, ((), ())), preferred_element_type=f32)  83.6 us
    ppermute x2, waiting for transfers between devices, passed_along(): return lax.ppermute(shard, axis, pairs)  54.1 us
    pallas_call x2, Pallas kernels, widen(): pl.pallas_call(functools.partial(widen_kernel, 144), grid=(units // step,...  33.3 us
    ppermute x20, waiting for transfers between devices, received(): lax.ppermute(shard, axis, [((i + by) % size, i) for i in range(size)])  30.5 us
    pallas_call x1, Pallas kernels, attend_back(): pl.pallas_call(functools.partial(attend_back_kernel, rows), grid=(1,), in...  24.9 us
    unnamed x139, local copies, waits for them, and re-layouts  17.5 us
  transfers between devices with their start and end apart: 22, of which 13 were waited for; matrix products, arithmetic and copies ran while one was open for 10% of the time, Pallas kernels for 30%

profile of v4, /device:TPU:0, one launch (start us, length us, event | category | flops | bytes accessed | tf_op | source)
XLA Modules:
  0.0 665.4 jit_solution(16835216102706879793)
XLA Ops:
  12.0 146.9 %shard_map.365 = (bf16[4,144,1024]{2,1,0:T(8,128)(2,1)}, f32[4,1,768]{2,1,0:T(1,128)}, bf16[1024,1536]{1,0:T(8,128)(2,1)}, bf16[512,1024]{1,0:T(8,128)(2,1)}, bf...) custom-call(bf16[4,144,1024]{2,1,0:T(8,128)(2,1)} %fusion.66.refs_0_, ...), custom_call_target="tpu_custom_call" | custom-call | tf_op jit(solution)/shard_map/pallas_call | solution.py:540
  159.0 2.3 convolution_convert_fusion.3
  161.4 2.8 collective-permute-done
  164.3 4.1 fusion.102
  169.9 2.3 collective-permute-done.1
  172.4 16.6 %shard_map.366 = (bf16[1152,2048]{1,0:T(8,128)(2,1)}, bf16[1152,2048]{1,0:T(8,128)(2,1)}) custom-call(bf16[1152,1024]{1,0:T(8,128)(2,1)S(1)} %pad_maximum_fusion.x_ref.refs_11_, bf16[1024,2048]{1,0:T(8,128)(2,1)} %get-tuple-element.57.w_ref, f32[1,2048]{1,0:T(1,128)S(1)} %bitcast.151), custom_call_target="tpu_custom_call" | custom-call | tf_op jit(solution)/shard_map/pallas_call | solution.py:282
  189.0 4.3 fusion.46
  193.6 2.6 collective-permute-done.2
  197.2 8.2 %fusion.100 = (f32[576]{0:T(1024)S(1)}, f32[576,1024]{1,0:T(8,128)S(1)}, f32[576,1024]{1,0:T(8,128)}) fusion(f32[1024]{0:T(1024)S(1)} %bitcast.220, bf16[576,1024]{1,0:T(8,128)(2,1)} %copy-done.53, f32[1024]{0:T(1024)S(1)} %bitcast.200, f32[1024]{0:T(1024)S(1)} %bitcast.179, f32[576]{0:T(1024)S(1)} %add_rsqrt_fusion.3, f32[576,1024]{1,0:T(8,128)} %copy-done.10, ...), kind=kOutput, calls=%fused_computation.252 | convolution fusion | flops 2421227008 | bytes 14830336 | tf_op jit(solution)/shard_map/dot_general | solution.py:74
  206.3 3.4 collective-permute-start.3
  209.9 25.1 %collective-permute-done.3 = bf16[576,1024]{1,0:T(8,128)(2,1)S(1)} collective-permute-done((bf16[576,1024]{1,0:T(8,128)(2,1)S(1)}, bf16[576,1024]{1,0:T(8,128)(2,1)S(1)}, u32[]{:S(2)}, u32[]{:S(2)}) %collective-permute-start.3) | collective-permute-done | bytes 1179680 | tf_op jit(solution)/shard_map/ppermute | solution.py:40
  239.6 3.8 collective-permute-start.5
  243.6 5.8 fusion.q_ref.k_ref.v_ref
  249.4 16.6 %shard_map.367 = (bf16[1152,512]{1,0:T(8,128)(2,1)S(1)}, f32[4,2,1152]{2,1,0:T(2,128)S(1)}) custom-call(s32[8]{0:T(128)S(1)} %add.434.order, s32[2,9]{1,0:T(2,128)S(1)} %pad_add_fusion.span, s32[1152,1]{1,0:T(8,128)S(1)} %copy-done.5, s32[1,1152]{1,0:T(1,128)S(1)} %copy-done.7, bf16[1152,1536]{1,0:T(8,128)(2,1)S(1)} %fusion.q_ref.k_ref.v_ref, ...), custom_call_target="tpu_custom_call" | custom-call | tf_op jit(solution)/shard_map/pallas_call | solution.py:172
  266.1 3.7 collective-permute-done.6
  270.7 2.8 collective-permute-done.8
  273.5 4.3 multiply_reduce_fusion.1
  278.8 2.7 collective-permute-done.9
  281.7 16.7 %shard_map.368 = (bf16[1152,2048]{1,0:T(8,128)(2,1)}, bf16[1152,2048]{1,0:T(8,128)(2,1)}) custom-call(bf16[1152,1024]{1,0:T(8,128)(2,1)S(1)} %pad_maximum_fusion.2.x_ref.refs_5_, bf16[1024,2048]{1,0:T(8,128)(2,1)} %get-tuple-element.57.w_ref, f32[1,2048]{1,0:T(1,128)S(1)} %bitcast.152), custom_call_target="tpu_custom_call" | custom-call | tf_op jit(solution)/shard_map/pallas_call | solution.py:282
  298.5 5.6 fusion.49
  304.4 2.7 collective-permute-done.10
  307.1 3.9 multiply_reduce_fusion
  315.6 2.7 collective-permute-done.12
  318.3 9.9 %convert_reduce_fusion = (f32[2048]{0:T(1024)S(1)}, bf16[1152,2048]{1,0:T(8,128)(2,1)S(1)}) fusion(bf16[1152,2048]{1,0:T(8,128)(2,1)} %get-tuple-element.66, bf16[2048,1024]{1,0:T(8,128)(2,1)} %get-tuple-element.60, bf16[576,1024]{1,0:T(8,128)(2,1)S(1)} %collective-permute-done.12, bf16[576,1024]{1,0:T(8,128)(2,1)S(1)} %get-tuple-element.173), kind=kOutput, calls=%fused_computation.2 | convolution fusion | flops 4848351232 | bytes 15998976 | tf_op jit(solution)/shard_map/dot_general | solution.py:74
  328.2 2.7 fusion.52
  331.1 2.7 collective-permute-done.13
  333.8 3.8 multiply_reduce_fusion.6
  337.6 2.2 convert_reduce_fusion.6
  339.9 2.7 collective-permute-done.14
  344.1 24.9 %shard_map.369 = (bf16[1152,512]{1,0:T(8,128)(2,1)S(1)}, bf16[1152,512]{1,0:T(8,128)(2,1)S(1)}, bf16[1152,512]{1,0:T(8,128)(2,1)S(1)}) custom-call(s32[8]{0:T(128)S(1)} %add.434.order, s32[2,9]{1,0:T(2,128)S(1)} %pad_add_fusion.span, s32[1152,1]{1,0:T(8,128)S(1)} %copy-done.5, s32[1,1152]{1,0:T(1,128)S(1)} %copy-done.7, bf16[1152,1536]{1,0:T(8,128)(2,1)} %copy-done.2, ...), custom_call_target="tpu_custom_call" | custom-call | tf_op jit(solution)/shard_map/pallas_call | solution.py:238
  369.3 2.0 fusion.58
  371.6 2.7 collective-permute-done.15
  374.3 4.1 fusion.93
  379.7 29.0 %collective-permute-done.16 = bf16[576,1024]{1,0:T(8,128)(2,1)} collective-permute-done((bf16[576,1024]{1,0:T(8,128)(2,1)}, bf16[576,1024]{1,0:T(8,128)(2,1)}, u32[]{:S(2)}, u32[]{:S(2)}) %collective-permute-start.16) | collective-permute-done | bytes 1179680 | tf_op jit(solution)/shard_map/ppermute | solution.py:40
  408.7 2.4 fusion.19
  411.1 3.2 convert_reduce_fusion.7
  415.8 3.4 pad_maximum_fusion.1.refs_24_
  421.6 2.2 collective-permute-start.21
  424.3 9.1 %convert_reduce_fusion.1 = (f32[2048]{0:T(1024)S(1)}, bf16[1152,2048]{1,0:T(8,128)(2,1)S(1)}) fusion(bf16[1152,2048]{1,0:T(8,128)(2,1)} %get-tuple-element.71, bf16[2048,1024]{1,0:T(8,128)(2,1)} %get-tuple-element.60, bf16[576,1024]{1,0:T(8,128)(2,1)} %collective-permute-done.17, bf16[576,1024]{1,0:T(8,128)(2,1)} %get-tuple-element.178), kind=kOutput, calls=%fused_computation.3 | convolution fusion | flops 4848351232 | bytes 15998976 | tf_op jit(solution)/shard_map/dot_general | solution.py:74
  433.5 2.6 fusion.55
  441.9 3.0 fusion.64
  444.9 5.1 multiply_reduce_fusion.8
  450.0 2.2 convert_reduce_fusion.8
  452.2 4.0 broadcast_select_fusion.1
  456.9 3.3 pad_maximum_fusion.5.refs_10_
  461.0 3.7 convolution_convert_fusion.refs_16_
  466.2 183.2 %shard_map.370 = (bf16[4,144,1024]{2,1,0:T(8,128)(2,1)}, f32[16,1024]{1,0:T(8,128)}, f32[8,128]{1,0:T(8,128)}, f32[512,512]{1,0:T(8,128)}, f32[512,512]{1,0:T(8,...) custom-call(bf16[4,144,1024]{2,1,0:T(8,128)(2,1)} %bitcast.153, ...), custom_call_target="tpu_custom_call" | custom-call | tf_op jit(solution)/shard_map/pallas_call | solution.py:972
  653.1 3.2 copy.64
  (262 shorter events, 56.3 us)
Async XLA Ops:
  159.0 5.3 copy-start.25
  161.3 2.9 collective-permute-start
  169.3 2.9 collective-permute-start.1
  172.4 16.6 %copy-start.3 = (bf16[1152,1024]{1,0:T(8,128)(2,1)}, bf16[1152,1024]{1,0:T(8,128)(2,1)S(1)}, u32[]{:S(2)}) copy-start(bf16[1152,1024]{1,0:T(8,128)(2,1)S(1)} %pad_maximum_fusion.x_ref.refs_11_) | copy-start | bytes 7077892
  172.4 16.6 %copy-start.49 = (bf16[2048,1024]{1,0:T(8,128)(2,1)S(1)}, bf16[2048,1024]{1,0:T(8,128)(2,1)}, u32[]{:S(2)}) copy-start(bf16[2048,1024]{1,0:T(8,128)(2,1)} %get-tuple-element.60) | copy-start | bytes 12582916
  193.3 2.9 collective-permute-start.2
  206.3 28.7 %collective-permute-start.3 = (bf16[576,1024]{1,0:T(8,128)(2,1)S(1)}, bf16[576,1024]{1,0:T(8,128)(2,1)S(1)}, u32[]{:S(2)}, u32[]{:S(2)}) collective-permute-start(bf16[576,1024]{1,0:T(8,128)(2,1)S(1)} %add_convert_fusion.1), channel_id=1, source_target_pairs={{0,16},{1,17},{2,18},{3,19},{4,20},{5,21},{6,22},{7,23},{8,24},{9,... | collective-permute-start | bytes 3538952 | tf_op jit(solution)/shard_map/ppermute | solution.py:40
  236.4 7.2 %collective-permute-start.4 = (bf16[576,1024]{1,0:T(8,128)(2,1)}, bf16[576,1024]{1,0:T(8,128)(2,1)}, u32[]{:S(2)}, u32[]{:S(2)}) collective-permute-start(bf16[576,1024]{1,0:T(8,128)(2,1)} %fusion.33), channel_id=1, source_target_pairs={{1,0},{0,1},{3,2},{2,3},{5,4},{4,5},{7,6},{6,7},{9,8},{8,9},{11,10... | collective-permute-start | bytes 3538952 | tf_op jit(solution)/shard_map/ppermute | solution.py:34
  236.6 7.0 %copy-start.23 = (bf16[1024,1536]{1,0:T(8,128)(2,1)S(1)}, bf16[1024,1536]{1,0:T(8,128)(2,1)}, u32[]{:S(2)}) copy-start(bf16[1024,1536]{1,0:T(8,128)(2,1)} %get-tuple-element.61.refs_20_) | copy-start | bytes 9437188
  239.5 26.5 %collective-permute-start.7 = (bf16[144,1024]{1,0:T(8,128)(2,1)S(1)}, bf16[144,1024]{1,0:T(8,128)(2,1)S(1)}, u32[]{:S(2)}, u32[]{:S(2)}) collective-permute-start(bf16[144,1024]{1,0:T(8,128)(2,1)S(1)} %get-tuple-element.206), channel_id=1, source_target_pairs={{6,0},{0,2},{2,4},{4,6},{7,1},{1,3},{3,5},{5,7},{14,8},{8,10},{10,... | collective-permute-start | bytes 884744 | tf_op jit(solution)/shard_map/ppermute | solution.py:34
  239.6 26.5 %collective-permute-start.5 = (bf16[144,1024]{1,0:T(8,128)(2,1)S(1)}, bf16[144,1024]{1,0:T(8,128)(2,1)S(1)}, u32[]{:S(2)}, u32[]{:S(2)}) collective-permute-start(bf16[144,1024]{1,0:T(8,128)(2,1)S(1)} %get-tuple-element.208), channel_id=1, source_target_pairs={{2,0},{4,2},{6,4},{0,6},{3,1},{5,3},{7,5},{1,7},{10,8},{12,10},{14... | collective-permute-start | bytes 884744 | tf_op jit(solution)/shard_map/ppermute | solution.py:34
  243.4 26.4 %collective-permute-start.6 = (bf16[144,1024]{1,0:T(8,128)(2,1)S(1)}, bf16[144,1024]{1,0:T(8,128)(2,1)S(1)}, u32[]{:S(2)}, u32[]{:S(2)}) collective-permute-start(bf16[144,1024]{1,0:T(8,128)(2,1)S(1)} %get-tuple-element.209), channel_id=1, source_target_pairs={{4,0},{6,2},{0,4},{2,6},{5,1},{7,3},{1,5},{3,7},{12,8},{14,10},{8,... | collective-permute-start | bytes 884744 | tf_op jit(solution)/shard_map/ppermute | solution.py:34
  243.6 5.8 copy-start.5
  243.6 5.8 copy-start.7
  249.4 16.6 %copy-start.2 = (bf16[1152,1536]{1,0:T(8,128)(2,1)}, bf16[1152,1536]{1,0:T(8,128)(2,1)S(1)}, u32[]{:S(2)}) copy-start(bf16[1152,1536]{1,0:T(8,128)(2,1)S(1)} %fusion.q_ref.k_ref.v_ref) | copy-start | bytes 10616836
  249.4 20.4 %copy-start.55 = (bf16[512,1024]{1,0:T(8,128)(2,1)S(1)}, bf16[512,1024]{1,0:T(8,128)(2,1)}, u32[]{:S(2)}) copy-start(bf16[512,1024]{1,0:T(8,128)(2,1)} %get-tuple-element.56) | copy-start | bytes 3145732
  266.0 11.7 %copy-start.6 = (bf16[1152,512]{1,0:T(8,128)(2,1)}, bf16[1152,512]{1,0:T(8,128)(2,1)S(1)}, u32[]{:S(2)}) copy-start(bf16[1152,512]{1,0:T(8,128)(2,1)S(1)} %get-tuple-element.64.refs_7_) | copy-start | bytes 3538948
  266.1 7.4 %copy-start.29 = (bf16[576,1024]{1,0:T(8,128)(2,1)S(1)}, bf16[576,1024]{1,0:T(8,128)(2,1)}, u32[]{:S(2)}) copy-start(bf16[576,1024]{1,0:T(8,128)(2,1)} %copy-done.28) | copy-start | bytes 3538948
  266.1 7.4 %copy-start.52 = (bf16[576,1024]{1,0:T(8,128)(2,1)S(1)}, bf16[576,1024]{1,0:T(8,128)(2,1)}, u32[]{:S(2)}) copy-start(bf16[576,1024]{1,0:T(8,128)(2,1)} %copy-done.51) | copy-start | bytes 3538948
  266.1 11.7 %copy-start.35 = (bf16[144,1024]{1,0:T(8,128)(2,1)}, bf16[144,1024]{1,0:T(8,128)(2,1)S(1)}, u32[]{:S(2)}) copy-start(bf16[144,1024]{1,0:T(8,128)(2,1)S(1)} %collective-permute-done.5) | copy-start | bytes 884740
  269.8 8.0 %copy-start.37 = (bf16[144,1024]{1,0:T(8,128)(2,1)}, bf16[144,1024]{1,0:T(8,128)(2,1)S(1)}, u32[]{:S(2)}) copy-start(bf16[144,1024]{1,0:T(8,128)(2,1)S(1)} %collective-permute-done.6) | copy-start | bytes 884740
  270.6 2.9 collective-permute-start.8
  278.6 2.9 collective-permute-start.9
  281.7 16.7 %copy-start.4 = (bf16[1152,1024]{1,0:T(8,128)(2,1)}, bf16[1152,1024]{1,0:T(8,128)(2,1)S(1)}, u32[]{:S(2)}) copy-start(bf16[1152,1024]{1,0:T(8,128)(2,1)S(1)} %pad_maximum_fusion.2.x_ref.refs_5_) | copy-start | bytes 7077892
  298.5 8.6 %copy-start.16 = (bf16[1152,2048]{1,0:T(8,128)(2,1)S(1)}, bf16[1152,2048]{1,0:T(8,128)(2,1)}, u32[]{:S(2)}) copy-start(bf16[1152,2048]{1,0:T(8,128)(2,1)} %get-tuple-element.65.refs_3_) | copy-start | bytes 14155780
  298.5 8.6 %copy-start.50 = (bf16[2048,1024]{1,0:T(8,128)(2,1)S(1)}, bf16[2048,1024]{1,0:T(8,128)(2,1)}, u32[]{:S(2)}) copy-start(bf16[2048,1024]{1,0:T(8,128)(2,1)} %get-tuple-element.60) | copy-start | bytes 12582916
  298.5 8.6 %copy-start.54 = (bf16[576,1024]{1,0:T(8,128)(2,1)S(1)}, bf16[576,1024]{1,0:T(8,128)(2,1)}, u32[]{:S(2)}) copy-start(bf16[576,1024]{1,0:T(8,128)(2,1)} %copy-done.53) | copy-start | bytes 3538948
  298.5 8.6 %copy-start.58 = (f32[576,1024]{1,0:T(8,128)S(1)}, f32[576,1024]{1,0:T(8,128)}, u32[]{:S(2)}) copy-start(f32[576,1024]{1,0:T(8,128)} %get-tuple-element.235) | copy-start | bytes 7077892
  304.1 2.9 collective-permute-start.10
  311.0 22.8 %copy-start.8 = (f32[576,1024]{1,0:T(8,128)}, f32[576,1024]{1,0:T(8,128)S(1)}, u32[]{:S(2)}) copy-start(f32[576,1024]{1,0:T(8,128)S(1)} %get-tuple-element.195) | copy-start | bytes 7077892
  315.4 12.8 %copy-start.21 = (bf16[576,1024]{1,0:T(8,128)(2,1)}, bf16[576,1024]{1,0:T(8,128)(2,1)S(1)}, u32[]{:S(2)}) copy-start(bf16[576,1024]{1,0:T(8,128)(2,1)S(1)} %get-tuple-element.173) | copy-start | bytes 3538948
  315.4 2.9 collective-permute-start.12
  318.3 9.9 %copy-start.31 = (bf16[576,1024]{1,0:T(8,128)(2,1)}, bf16[576,1024]{1,0:T(8,128)(2,1)S(1)}, u32[]{:S(2)}) copy-start(bf16[576,1024]{1,0:T(8,128)(2,1)S(1)} %collective-permute-done.12) | copy-start | bytes 3538948
  318.3 9.9 %copy-start.14 = (bf16[1024,2048]{1,0:T(8,128)(2,1)S(1)}, bf16[1024,2048]{1,0:T(8,128)(2,1)}, u32[]{:S(2)}) copy-start(bf16[1024,2048]{1,0:T(8,128)(2,1)} %get-tuple-element.57.w_ref) | copy-start | bytes 12582916
  328.2 5.6 copy-start.17
  330.9 2.9 collective-permute-start.13
  339.8 2.8 collective-permute-start.14
  371.4 2.9 collective-permute-start.15
  378.4 30.4 %collective-permute-start.16 = (bf16[576,1024]{1,0:T(8,128)(2,1)}, bf16[576,1024]{1,0:T(8,128)(2,1)}, u32[]{:S(2)}, u32[]{:S(2)}) collective-permute-start(bf16[576,1024]{1,0:T(8,128)(2,1)} %get-tuple-element.196), channel_id=1, source_target_pairs={{16,0},{17,1},{18,2},{19,3},{20,4},{21,5},{22,6},{23,7},{24,8},{25... | collective-permute-start | bytes 3538952 | tf_op jit(solution)/shard_map/ppermute | solution.py:40
  414.3 10.0 %collective-permute-start.17 = (bf16[576,1024]{1,0:T(8,128)(2,1)}, bf16[576,1024]{1,0:T(8,128)(2,1)}, u32[]{:S(2)}, u32[]{:S(2)}) collective-permute-start(bf16[576,1024]{1,0:T(8,128)(2,1)} %get-tuple-element.178), channel_id=1, source_target_pairs={{1,0},{0,1},{3,2},{2,3},{5,4},{4,5},{7,6},{6,7},{9,8},{8,9},{11,10... | collective-permute-start | bytes 3538952 | tf_op jit(solution)/shard_map/ppermute | solution.py:34
  421.6 234.7 %collective-permute-start.21 = (bf16[144,1024]{1,0:T(8,128)(2,1)}, bf16[144,1024]{1,0:T(8,128)(2,1)}, u32[]{:S(2)}, u32[]{:S(2)}) collective-permute-start(bf16[144,1024]{1,0:T(8,128)(2,1)} %get-tuple-element.203), channel_id=1, source_target_pairs={{2,0},{4,2},{6,4},{0,6},{3,1},{5,3},{7,5},{1,7},{10,8},{12,10},{14... | collective-permute-start | bytes 884744 | tf_op jit(solution)/shard_map/ppermute | solution.py:34
  423.8 232.6 %collective-permute-start.20 = (bf16[144,1024]{1,0:T(8,128)(2,1)S(1)}, bf16[144,1024]{1,0:T(8,128)(2,1)}, u32[]{:S(2)}, u32[]{:S(2)}) collective-permute-start(bf16[144,1024]{1,0:T(8,128)(2,1)S(1)} %get-tuple-element.204), channel_id=1, source_target_pairs={{4,0},{6,2},{0,4},{2,6},{5,1},{7,3},{1,5},{3,7},{12,8},{14,10},{8,... | collective-permute-start | bytes 884744 | tf_op jit(solution)/shard_map/ppermute | solution.py:34
  424.3 232.6 %collective-permute-start.11 = (bf16[144,1024]{1,0:T(8,128)(2,1)S(1)}, bf16[144,1024]{1,0:T(8,128)(2,1)}, u32[]{:S(2)}, u32[]{:S(2)}) collective-permute-start(bf16[144,1024]{1,0:T(8,128)(2,1)S(1)} %get-tuple-element.205), channel_id=1, source_target_pairs={{6,0},{0,2},{2,4},{4,6},{7,1},{1,3},{3,5},{5,7},{14,8},{8,10},{10,... | collective-permute-start | bytes 884744 | tf_op jit(solution)/shard_map/ppermute | solution.py:34
  424.3 9.1 %copy-start.15 = (bf16[1024,2048]{1,0:T(8,128)(2,1)S(1)}, bf16[1024,2048]{1,0:T(8,128)(2,1)}, u32[]{:S(2)}) copy-start(bf16[1024,2048]{1,0:T(8,128)(2,1)} %get-tuple-element.57.w_ref) | copy-start | bytes 12582916
  433.4 11.5 %copy-start.18 = (bf16[1152,2048]{1,0:T(8,128)(2,1)}, bf16[1152,2048]{1,0:T(8,128)(2,1)S(1)}, u32[]{:S(2)}) copy-start(bf16[1152,2048]{1,0:T(8,128)(2,1)S(1)} %get-tuple-element.240.refs_12_) | copy-start | bytes 14155780
  436.1 8.8 %collective-permute-start.18 = (bf16[576,1024]{1,0:T(8,128)(2,1)S(1)}, bf16[576,1024]{1,0:T(8,128)(2,1)S(1)}, u32[]{:S(2)}, u32[]{:S(2)}) collective-permute-start(bf16[576,1024]{1,0:T(8,128)(2,1)S(1)} %fusion.55), channel_id=1, source_target_pairs={{1,0},{0,1},{3,2},{2,3},{5,4},{4,5},{7,6},{6,7},{9,8},{8,9},{11,10... | collective-permute-start | bytes 3538952 | tf_op jit(solution)/shard_map/ppermute | solution.py:34
  452.2 8.8 %collective-permute-start.19 = (bf16[576,1024]{1,0:T(8,128)(2,1)S(1)}, bf16[576,1024]{1,0:T(8,128)(2,1)S(1)}, u32[]{:S(2)}, u32[]{:S(2)}) collective-permute-start(bf16[576,1024]{1,0:T(8,128)(2,1)S(1)} %get-tuple-element.180), channel_id=1, source_target_pairs={{1,0},{0,1},{3,2},{2,3},{5,4},{4,5},{7,6},{6,7},{9,8},{8,9},{11,10... | collective-permute-start | bytes 3538952 | tf_op jit(solution)/shard_map/ppermute | solution.py:34
  649.5 6.9 %copy-start.47 = (f32[16,1024]{1,0:T(8,128)S(1)}, f32[16,1024]{1,0:T(8,128)}, u32[]{:S(2)}) copy-start(f32[16,1024]{1,0:T(8,128)} %get-tuple-element.80) | copy-start | bytes 196612
  (33 other events, 103.7 us)

commit v5 on v4

--- a/solution.py
+++ b/solution.py
@@ -193,7 +193,7 @@
 
 
 def back_tile(at, to, seg_c, seg_r, lse_ref, q_s, k_s, v_s, up_s, dq_s, dk_s, dv_s):
-    same_item = seg_c[to, :] == seg_r[:, at]
+    same_item = seg_c[to, 0:1] == seg_r[:, at]
     same_item = jnp.concatenate([same_item, same_item], axis=1)
     for pair in range(q_s.shape[1] // PAIR):
         cols = slice(pair * PAIR, (pair + 1) * PAIR)
@@ -580,19 +580,20 @@
 
 def scatter_kernel(rows, seqs, dp_size, tp_size, *refs):
     seq_ref, small_ref, slots_ref = refs[:3]
-    operands_before, operands_last = refs[3:9], refs[9:15]
-    qkv_ref, up_ref, lse_ref, seg_c, seg_r, joined_ref, resid_ref, time_ref = refs[15:23]
-    tokens_last, tokens_before, gq_before = refs[23:26]
-    seq_out, small_out, slots_out = refs[26:29]
-    outs = refs[29:35]
-    sides, ups, downs = refs[35:39], refs[39:43], refs[43:47]
-    small_zs, small_all, slots_zs, slots_dp = refs[47:51]
-    seq_send, seq_get, local_sem, small_send, small_get = refs[51:56]
-    side_send, side_get, up_send, up_get, down_send, down_get = refs[56:62]
-    wide_s, dq_s, dk_s, dv_s, gq_s, tokens_s = refs[62:68]
-    x_send, x_get, seq_s, small_s, slots_s = refs[68:73]
-    mine, theirs = refs[73:77], refs[77:81]
-    place_sem, x_sem, load_sem = refs[81:84]
+    operands_before, operands_last = refs[3:9], refs[9:13]
+    qkv_ref, lse_ref, column_ref, seg_r, joined_ref = refs[13:18]
+    tokens_last, tokens_before, gq_before = refs[18:21]
+    ffn_out_ref, slope_ref, in_ref, out_ref, second_ref, normed_ref, gain_ref = refs[21:28]
+    seq_out, small_out, slots_out = refs[28:31]
+    outs = refs[31:37]
+    sides, ups, downs = refs[37:41], refs[41:45], refs[45:49]
+    small_zs, small_all, slots_zs, slots_dp = refs[49:53]
+    seq_send, seq_get, local_sem, small_send, small_get = refs[53:58]
+    side_send, side_get, up_send, up_get, down_send, down_get = refs[58:64]
+    wide_s, dq_s, dk_s, dv_s, gq_s, tokens_s = refs[64:70]
+    x_send, x_get, seq_s, small_s, slots_s = refs[70:75]
+    mine, theirs = refs[75:79], refs[79:83]
+    place_sem, x_sem, load_sem, resid_ref, branch_s, more_sem = refs[83:89]
     joined_mine, joined_theirs = mine[3], theirs[3]
     heads_all = dq_s.shape[1]
     q_s, k_s, v_s, up_s = [wide_s.at[:, i * heads_all : (i + 1) * heads_all] for i in range(4)]
@@ -603,6 +604,7 @@
     half = units // 2
     length = dq_s.shape[0]
     own_count, width = resid_ref.shape
+    seg_c = column_ref
     part = width // dp_size
     kinds = [(0, 0, 0, half), (0, 0, half, half), (1, 1, 0, half), (1, 1, half, half), (2, 0, 0, hc)]
     kinds += [(3, 1, third * seqs * hc, hc) for third in range(3)]
@@ -689,15 +691,12 @@
         at = lax.rem(zs + chip, seqs) * tp_size + lax.rem(tp + member, tp_size)
         at = pl.ds(pl.multiple_of(at * rows, 16), rows)
         here = slice(block * rows, (block + 1) * rows)
-        if array < 3:
-            source = qkv_ref.at[here, array * heads_all : (array + 1) * heads_all]
-        else:
-            source = up_ref.at[here, :]
-        target = (q_s, k_s, v_s, up_s)[array].at[at, :]
+        source = qkv_ref.at[here, array * heads_all : (array + 1) * heads_all]
+        target = (q_s, k_s, v_s)[array].at[at, :]
         return pltpu.make_async_copy(source, target, place_sem.at[array, block])
 
     def each_placed(act):
-        for array in range(4):
+        for array in range(3):
             for block in range(length // rows):
                 act(placed(block, array))
 
@@ -759,8 +758,90 @@
                     left = tokens_s[:, other * part + at : other * part + at + step]
                     target[at : at + step, cols] = mm(left, gq_s[:, cols], ((0,), (0,))).astype(bf16)
 
-    def exchange():
-        return to({"tp": 1 - tp}, x_send, x_get, x_sem.at[0], x_sem.at[1])
+    def exchange(time):
+        return to({"tp": 1 - tp}, x_send, x_get, x_sem.at[0, time], x_sem.at[1, time])
+
+    def branch_exchange():
+        here, there = branch_s.at[:own_count, :], branch_s.at[own_count:, :]
+        return to({"tp": 1 - tp}, here, there, x_sem.at[0, 2], x_sem.at[1, 2])
+
+    def fetched(*pairs):
+        copies = [pltpu.make_async_copy(*pair, more_sem.at[i]) for i, pair in enumerate(pairs)]
+        for copy in copies:
+            copy.start()
+        for copy in copies:
+            copy.wait()
+
+    def keep_sums(first, sums):
+        for other in range(dp_size):
+            cols = pl.ds(pl.multiple_of(lax.rem(dp + other, dp_size) * part, part), part)
+            for i, values in enumerate(sums):
+                small_s[first + i : first + i + 1, cols] = values[:, other * part : (other + 1) * part]
+
+    members = [slice(member * own_count, (member + 1) * own_count) for member in range(tp_size)]
+
+    def hidden_grads():
+        for slot in range(seqs):
+            at = slice(slot * units, (slot + 1) * units)
+            fetched((ffn_out_ref.at[at, :], branch_s.at[:units, :]), (slope_ref.at[:, at], dq_s))
+            total = jnp.zeros((1, units), f32)
+            for here in members:
+                found = mm(tokens_s[here, :], branch_s[:units, :], ((1,), (1,)))
+                found = (found * dq_s[here, :].astype(f32)).astype(bf16)
+                wide_s[here, at] = found
+                total = total + jnp.sum(found.astype(f32), axis=0, keepdims=True)
+            for i in range(units // 128):
+                slots_s[slot, 2 + i : 3 + i, :] = total[:, i * 128 : (i + 1) * 128]
+
+    def first_grads():
+        half = seqs * units // 2
+        low, high = mine[3].at[:, :half], theirs[3].at[:, :half]
+        for other in range(dp_size):
+            at = slice(other * part, (other + 1) * part)
+            fetched((in_ref.at[at, :half], low), (in_ref.at[at, half:], high))
+
+            def found(here):
+                total = mm(wide_s[here, :half], low[...], ((1,), (1,)))
+                return total + mm(wide_s[here, half:], high[...], ((1,), (1,)))
+
+            x_send[:, at] = found(members[1]).astype(bf16)
+            resid_ref[:, at] = found(members[0])
+        exchange(0).start()
+
+    def norm_grads():
+        pairs = []
+        for source, target in ((second_ref, dk_s), (normed_ref, dv_s)):
+            for i, here in enumerate(members):
+                pairs.append((source.at[:, i * heads_all : (i + 1) * heads_all], target.at[here, :]))
+        fetched(*pairs)
+        exchange(0).wait()
+
+        def block(i, carry):
+            at = pl.ds(pl.multiple_of(i * rows, 16), rows)
+            late = pl.ds(pl.multiple_of(own_count + i * rows, 16), rows)
+            grads = resid_ref[at, :] + x_get[at, :].astype(f32)
+            grads = grads + jnp.concatenate([dk_s[at, :], dk_s[late, :]], axis=1)
+            normed = jnp.concatenate([dv_s[at, :], dv_s[late, :]], axis=1)
+            found = norm_back(grads, normed, column_ref[at, 2:3], gain_ref[...])
+            lowered = found.astype(bf16)
+            resid_ref[at, :] = found
+            branch_s[at, :] = lowered
+            terms = (lowered.astype(f32), grads * normed, grads)
+            return tuple(c + jnp.sum(term, axis=0, keepdims=True) for c, term in zip(carry, terms))
+
+        zero = jnp.zeros((1, width), f32)
+        keep_sums(2, lax.fori_loop(0, seqs, block, (zero, zero, zero)))
+        branch_exchange().start()
+        fetched((operands_last[3], dq_s), (out_ref, x_send.at[:heads_all, :]))
+        branch_exchange().wait()
+
+    def mixed_grads():
+        for member, here in enumerate(members):
+            found = mm(branch_s[here, :], x_send[:heads_all, :], ((1,), (1,))).astype(bf16)
+            for chip in range(seqs):
+                at = lax.rem(zs + chip, seqs) * tp_size + lax.rem(tp + member, tp_size)
+                at = pl.ds(pl.multiple_of(at * rows, 16), rows)
+                up_s[at, :] = found[chip * rows : (chip + 1) * rows]
 
     def input_grads():
         @pl.when(first_stage)
@@ -773,13 +854,13 @@
                 return carry
 
             lax.fori_loop(0, seqs, theirs_rows, 0)
-            exchange().start()
+            exchange(1).start()
             for slot in range(seqs):
                 cols = slice(slot * hc, (slot + 1) * hc)
                 slots_s[slot, 0:1, :] = jnp.sum(gq_s[:, cols].astype(f32), axis=0, keepdims=True)
                 cols = slice(2 * heads_all + slot * hc, 2 * heads_all + (slot + 1) * hc)
                 slots_s[slot, 1:2, :] = jnp.sum(gq_s[:, cols].astype(f32), axis=0, keepdims=True)
-            exchange().wait()
+            exchange(1).wait()
 
             def own_rows(i, carry):
                 at = pl.ds(pl.multiple_of(i * rows, 16), rows)
@@ -789,17 +870,13 @@
                 for other in range(dp_size):
                     cols = pl.ds(pl.multiple_of(lax.rem(dp + other, dp_size) * part, part), part)
                     seq_s[i, :, cols] = lowered[:, other * part : (other + 1) * part]
-                timed = jnp.sum(total * time_ref[at, :], axis=0, keepdims=True)
+                timed = jnp.sum(total * column_ref[at, 1:2], axis=0, keepdims=True)
                 plain = jnp.sum(total, axis=0, keepdims=True)
                 return carry[0] + timed, carry[1] + plain
 
             zero = jnp.zeros((1, width), f32)
             timed, plain = lax.fori_loop(0, seqs, own_rows, (zero, zero))
-            for other in range(dp_size):
-                cols = pl.ds(pl.multiple_of(lax.rem(dp + other, dp_size) * part, part), part)
-                here = slice(other * part, (other + 1) * part)
-                small_s[0:1, cols] = timed[:, here]
-                small_s[1:2, cols] = plain[:, here]
+            keep_sums(0, (timed, plain))
 
     own_seq = pltpu.make_async_copy(seq_s.at[0], seq_out.at[zs], local_sem.at[0])
 
@@ -826,9 +903,32 @@
 
     small_s[...] = small_ref[...]
     slots_s[...] = slots_ref[...]
+    def taken(kind):
+        for slot in slot_order:
+            side(kind, slot).wait()
+            added(cut(sides, kind, slot), cut(mine, kind, slot))
+
+    def pass_on(kind, hop):
+        @pl.when((zs == hop) & (zs < seqs - 1))
+        def _():
+            for far in range(seqs - 1 - hop, 0, -1):
+                if hop > 0:
+                    up(kind, far + 1).wait_recv()
+                    added(cut(sides, kind, far), cut(ups, kind, far))
+                up(kind, far).start()
+
+        @pl.when((zs == seqs - 1 - hop) & (zs > 0))
+        def _():
+            for far in range(seqs - 1 - hop, 0, -1):
+                if hop > 0:
+                    down(kind, far + 1).wait_recv()
+                    added(cut(sides, kind, seqs - far), cut(downs, kind, far))
+                down(kind, far).start()
+
     def load(index, target):
         def copies(operands):
             return pltpu.make_async_copy(operands[index], target, load_sem.at[index])
+
 
         @pl.when(first_stage)
         def _():
@@ -849,10 +949,21 @@
             at = slice(first + slot * apart, first + slot * apart + size)
             if axis == 0:
                 left = dq_s if array == 2 else wide_s
-                target[at, :] = mm(left[:, at], tokens_s[:, features], ((0,), (0,))).astype(bf16)
+                right = branch_s if array == 2 else tokens_s
+                target[at, :] = mm(left[:, at], right[:, features], ((0,), (0,))).astype(bf16)
             else:
                 found = mm(tokens_s[:, features], wide_s[:, at], ((0,), (0,)))
                 target[:, at] = found.astype(bf16)
+
+    def old(index, target):
+        return pltpu.make_async_copy(operands_before[index], target, load_sem.at[index])
+
+    def relay(step):
+        if step < len(kinds):
+            taken(step)
+        for hop in range(seqs - 1):
+            if 0 <= step - hop < len(kinds):
+                pass_on(step - hop, hop)
 
     hidden, grads = load(0, wide_s), load(1, tokens_s)
     hidden.wait()
@@ -862,56 +973,60 @@
             product(kind, other)
             if other == 1:
                 begin(kind)
-    inputs, grads = load(2, tokens_s), load(3, wide_s)
-    inputs.wait()
-    grads.wait()
+
+    @pl.when(first_stage)
+    def _():
+        hidden_grads()
+
+    @pl.when(jnp.logical_not(first_stage))
+    def _():
+        old(3, wide_s).start()
+        old(3, wide_s).wait()
+
+    load(2, tokens_s).wait()
     for kind in (2, 3):
-        for other in range(dp_size):
+        for other in reversed(range(dp_size)):
             product(kind, other)
-    mixed, grads = load(4, dq_s), load(5, tokens_s)
-    mixed.wait()
-    grads.wait()
-    for other in range(dp_size):
+        begin(kind)
+
+    @pl.when(first_stage)
+    def _():
+        first_grads()
+
+    relay(0)
+
+    @pl.when(first_stage)
+    def _():
+        norm_grads()
+
+    @pl.when(jnp.logical_not(first_stage))
+    def _():
+        old(4, dq_s).start()
+        old(5, branch_s).start()
+        old(4, dq_s).wait()
+        old(5, branch_s).wait()
+
+    for other in reversed(range(dp_size)):
         product(4, other)
+    begin(4)
+
+    @pl.when(first_stage)
+    def _():
+        mixed_grads()
+
+    relay(1)
     attention_start()
-
-    def taken(kind):
-        for slot in slot_order:
-            side(kind, slot).wait()
-            added(cut(sides, kind, slot), cut(mine, kind, slot))
-
-    def pass_on(kind, hop):
-        @pl.when((zs == hop) & (zs < seqs - 1))
-        def _():
-            for far in range(seqs - 1 - hop, 0, -1):
-                if hop > 0:
-                    up(kind, far + 1).wait_recv()
-                    added(cut(sides, kind, far), cut(ups, kind, far))
-                up(kind, far).start()
-
-        @pl.when((zs == seqs - 1 - hop) & (zs > 0))
-        def _():
-            for far in range(seqs - 1 - hop, 0, -1):
-                if hop > 0:
-                    down(kind, far + 1).wait_recv()
-                    added(cut(sides, kind, seqs - far), cut(downs, kind, far))
-                down(kind, far).start()
-
-    for step in range(len(kinds) + seqs - 2):
-        if step < len(kinds):
-            taken(step)
-            if step + AHEAD < len(kinds):
-                begin(step + AHEAD)
-        for hop in range(seqs - 1):
-            if 0 <= step - hop < len(kinds):
-                pass_on(step - hop, hop)
-        if step == 0:
-            attention_end()
-        if step == 1:
-            joined_parts()
-            input_grads()
-            send_small()
-        if step == 4:
+    relay(2)
+    attention_end()
+    relay(3)
+    joined_parts()
+    for kind in range(5, len(kinds)):
+        begin(kind)
+    input_grads()
+    send_small()
+    for step in range(4, len(kinds) + seqs - 2):
+        relay(step)
+        if step == 6:
             add_small()
 
     total, slot_total = small_all[0], slots_dp[0]
@@ -953,7 +1068,7 @@
         sequence(by).wait()
 
 
-def scatter_all(rows, by_block, small, slots, operands, attended, tokens, gq_before, tp_size):
+def scatter_all(rows, by_block, small, slots, operands, attended, tokens, gq_before, onward, tp_size):
     seqs, _, width = by_block.shape
     dp_size = 2
     units, part = operands[0].shape[1] // seqs, width // dp_size
@@ -972,10 +1087,10 @@
     return pl.pallas_call(
         functools.partial(scatter_kernel, rows, seqs, dp_size, tp_size),
         in_specs=[anywhere, inside, inside]
-        + [anywhere] * 12
-        + [anywhere, anywhere]
-        + [inside] * 6
-        + [anywhere] * 3,
+        + [anywhere] * 11
+        + [inside] * 4
+        + [anywhere] * 9
+        + [inside],
         out_specs=[anywhere] + [inside] * 8,
         out_shape=[
             jax.ShapeDtypeStruct(by_block.shape, bf16),
@@ -1014,11 +1129,18 @@
             pltpu.VMEM(slots.shape, f32),
         ]
         + like * 2
-        + [dma((4, length // rows)), dma((2,)), dma((6,))],
+        + [
+            dma((3, length // rows)),
+            dma((2, 3)),
+            dma((6,)),
+            pltpu.VMEM((own_count, width), f32),
+            low(length, width),
+            dma((4,)),
+        ],
         compiler_params=pltpu.CompilerParams(
             collective_id=1, has_side_effects=True, vmem_limit_bytes=63 * 1024 * 1024
         ),
-    )(by_block, small, slots, *operands, *attended, *tokens, gq_before)
+    )(by_block, small, slots, *operands, *attended, *tokens, gq_before, *onward)
 
 
 def per_device(
@@ -1160,6 +1282,7 @@
     biases = jnp.concatenate([query_bias[0], value_bias[0], ffn_in_bias[0].astype(f32)])[None]
     in_kernels = sections == 2 and dp_size == 2 and tp_size == 2 and rows % 16 == 0
     in_kernels = in_kernels and head_cols == 128 and part % 256 == 0 and unit_cols % 256 == 0
+    in_kernels = in_kernels and heads_all == unit_cols == part
     if in_kernels:
         by_seq = rotated(jnp.transpose(states, (1, 0, 2)))
         blocks = (query_weight, key_weight, value_weight, out_weight, ffn_in, ffn_out)
@@ -1310,31 +1433,46 @@
         grad_ffn = grad_second.astype(bf16)
         ffn_out_bias_grad = token_sum(grad_ffn)
         grad_ffn_all = everyone(grad_ffn)
-        grad_pre = (mm(grad_ffn_all, ffn_out_all, ((1,), (1,))) * slope.astype(f32)).astype(bf16)
-        in_bias_sum = token_sum(grad_pre)
-        for_ffn.append((hidden, grad_ffn_all, first_all, grad_pre))
-        if last and not in_kernels:
-            ffn_out_parts = chosen(lambda a, b, c, d: parts_of(a, b, 1), for_ffn)
-            ffn_in_parts = chosen(lambda a, b, c, d: parts_of(c, d, 0), for_ffn)
-            grad_second = after(grad_second, *ffn_out_parts, *ffn_in_parts)
-        grad_first = grad_second + returned(grad_pre, in_all, ((1,), (1,)))
-        gain_one, shift_one = token_sum(grad_first * first_normed), token_sum(grad_first)
-        grad_resid = norm_back(grad_first, first_normed, first_inverse, attn_gain)
-        grad_branch = grad_resid.astype(bf16)
-        out_bias_grad = token_sum(grad_branch)
-        branch_all = everyone(grad_branch)
-        grad_mixed = by_position(mm(branch_all, out_all, ((1,), (1,))).astype(bf16))
-        for_out.append((mixed, branch_all))
-        if last and not in_kernels:
-            out_parts = chosen(lambda a, b: parts_of(a, b, 1), for_out)
-            grad_mixed = after(grad_mixed, *out_parts)
         if last and in_kernels:
-            attended = (qkv, grad_mixed, lse, segment[:, None], segment[None, :], joined, grad_resid, time_rows)
-            tw_grad, tb_grad = jnp.zeros((width,), f32), jnp.zeros((width,), f32)
-            bias_sums, grad_in_before = jnp.zeros((3 * heads_all,), f32), results[2]
-            grad_in = jnp.zeros((), bf16)
+            by_token = jnp.concatenate([time_rows, first_inverse], axis=1)
+            by_token = jnp.pad(by_token, ((0, length - own_count), (0, 0)))
+            columns = jnp.concatenate([segment.astype(f32)[:, None], by_token], axis=1)
+            attended = (qkv, lse, columns, segment.astype(f32)[None, :], joined)
+            onward = (
+                ffn_out_all,
+                slope,
+                in_all,
+                out_all,
+                grad_second,
+                first_normed,
+                attn_gain[None],
+            )
+            (before,), (before_out,) = for_ffn, for_out
+            operands = (*before, *before_out, hidden, grad_ffn_all, first_all, mixed)
+            nothing = jnp.zeros((width,), f32)
+            tw_grad, tb_grad, out_bias_grad, gain_one, shift_one = [nothing] * 5
+            in_bias_sum, bias_sums = jnp.zeros((units_all,), f32), jnp.zeros((3 * heads_all,), f32)
+            grad_in_before, grad_in = results[2], jnp.zeros((), bf16)
             results = (results[0], results[1], grad_in)
         else:
+            grad_pre = (mm(grad_ffn_all, ffn_out_all, ((1,), (1,))) * slope.astype(f32)).astype(bf16)
+            in_bias_sum = token_sum(grad_pre)
+            for_ffn.append((hidden, grad_ffn_all, first_all, grad_pre))
+            if last:
+                ffn_out_parts = chosen(lambda a, b, c, d: parts_of(a, b, 1), for_ffn)
+                ffn_in_parts = chosen(lambda a, b, c, d: parts_of(c, d, 0), for_ffn)
+                grad_second = after(grad_second, *ffn_out_parts, *ffn_in_parts)
+            grad_first = grad_second + returned(grad_pre, in_all, ((1,), (1,)))
+            gain_one, shift_one = token_sum(grad_first * first_normed), token_sum(grad_first)
+            grad_resid = norm_back(grad_first, first_normed, first_inverse, attn_gain)
+            grad_branch = grad_resid.astype(bf16)
+            out_bias_grad = token_sum(grad_branch)
+            branch_all = everyone(grad_branch)
+            grad_mixed = by_position(mm(branch_all, out_all, ((1,), (1,))).astype(bf16))
+            for_out.append((mixed, branch_all))
+            if last:
+                out_parts = chosen(lambda a, b: parts_of(a, b, 1), for_out)
+                grad_mixed = after(grad_mixed, *out_parts)
             grads = attend_back(qkv, segment, span, kernel_order, kernel_rows, grad_mixed, lse)
             grad_qkv = jnp.concatenate([by_distance(grad) for grad in grads], axis=1)
             bias_sums = token_sum(grad_qkv)
@@ -1376,10 +1514,11 @@
             by_block,
             small,
             slots.reshape(seqs, 8, padded // 8),
-            [operand for each in zip(for_ffn, for_out) for pair in each for operand in pair],
+            operands,
             attended,
             (rounded_all, for_joined[0][0]),
             for_joined[0][1],
+            onward,
             tp_size,
         )
         input_grad = jnp.transpose(input_pieces, (1, 0, 2))
@@ -1398,7 +1537,7 @@
         out_grad = owned(out_parts, 0, 1)
         joined_grad = owned(joined_parts, 1, 3)
         triple = [joined_grad[:, i * head_cols : (i + 1) * head_cols] for i in range(3)]
-    layer_out = in_positions(layer_pieces, grad_mixed)
+    layer_out = in_positions(layer_pieces, grad_ffn_all)
     element_count = float(SEQ_LEN * seqs * dp_size * width)
     stats = jnp.sqrt(shared[8:9, :3] / element_count)
     return (

time: 675 us -> 665 us (0.985)
  waiting for transfers between devices: 84.6 us -> 64.3 us
  matrix products: 83.6 us -> 64.7 us
  local copies, waits for them, and re-layouts: 28.2 us -> 44.2 us
  Pallas kernels: 405 us -> 413 us
    dot_general x19 -> x15, matrix products: 83.6 us -> 64.7 us  [mm(): return lax.dot_general(a, b, (dims, ((), ())), preferred_element_type=f32)]
    ppermute x2, waiting for transfers between devices: 54.1 us -> 38.9 us  [passed_along(): return lax.ppermute(shard, axis, pairs)]
    unnamed x139 -> x249, local copies, waits for them, and re-layouts: 17.5 us -> 27.9 us
    pallas_call x1, Pallas kernels: 183 us -> 191 us  [scatter_all(): pl.pallas_call(functools.partial(scatter_kernel, rows, seqs, dp_size, tp_...]
    ppermute x20 -> x18, waiting for transfers between devices: 30.5 us -> 25.5 us  [received(): lax.ppermute(shard, axis, [((i + by) % size, i) for i in range(size)])]
    reduce_sum x7 -> x6, other arithmetic: 13.3 us -> 14.1 us  [token_sum(): return jnp.sum(values.astype(f32), axis=0)]
  transfers between devices with their start and end apart: 22 -> 20, of which waited for: 13 -> 11; matrix products, arithmetic and copies ran while one was open for 10% -> 10% of each run, Pallas kernels for 30% -> 32%
where the time goes in v5:
time: 665 us; the launch traced here: 654 us
  Pallas kernels  413 us (62%)
  matrix products  64.7 us (10%)
  waiting for transfers between devices  64.3 us (10%)
  other arithmetic  51.2 us (8%)
  local copies, waits for them, and re-layouts  44.2 us (7%)
  starting transfers between devices  14.4 us (2%)
    pallas_call x1, Pallas kernels, scatter_all(): pl.pallas_call(functools.partial(scatter_kernel, rows, seqs, dp_size, tp_...  191 us
    pallas_call x1, Pallas kernels, gather_all(): pl.pallas_call(functools.partial(gather_kernel, seqs, dp_size, tp_size),...  147 us
    dot_general x15, matrix products, mm(): return lax.dot_general(a, b, (dims, ((), ())), preferred_element_type=f32)  64.7 us
    ppermute x2, waiting for transfers between devices, passed_along(): return lax.ppermute(shard, axis, pairs)  38.9 us
    pallas_call x2, Pallas kernels, widen(): pl.pallas_call(functools.partial(widen_kernel, 144), grid=(units // step,...  33.4 us
    unnamed x249, local copies, waits for them, and re-layouts  27.9 us
    ppermute x18, waiting for transfers between devices, received(): lax.ppermute(shard, axis, [((i + by) % size, i) for i in range(size)])  25.5 us
    pallas_call x1, Pallas kernels, attend_back(): pl.pallas_call(functools.partial(attend_back_kernel, rows), grid=(1,), in...  24.9 us
  transfers between devices with their start and end apart: 20, of which 11 were waited for; matrix products, arithmetic and copies ran while one was open for 10% of the time, Pallas kernels for 32%

profile of v5, /device:TPU:0, one launch (start us, length us, event | category | flops | bytes accessed | tf_op | source)
XLA Modules:
  0.0 654.2 jit_solution(660391416807758386)
XLA Ops:
  10.5 1.7 fusion.58.refs_0_
  12.2 146.9 %shard_map.365 = (bf16[4,144,1024]{2,1,0:T(8,128)(2,1)}, f32[4,1,768]{2,1,0:T(1,128)}, bf16[1024,1536]{1,0:T(8,128)(2,1)}, bf16[512,1024]{1,0:T(8,128)(2,1)}, bf...) custom-call(bf16[4,144,1024]{2,1,0:T(8,128)(2,1)} %fusion.58.refs_0_, ...), custom_call_target="tpu_custom_call" | custom-call | tf_op jit(solution)/shard_map/pallas_call | solution.py:540
  159.2 2.3 convolution_convert_fusion.2
  161.6 2.8 collective-permute-done
  164.5 4.1 fusion.93
  169.8 2.7 collective-permute-done.1
  172.7 16.6 %shard_map.366 = (bf16[1152,2048]{1,0:T(8,128)(2,1)}, bf16[1152,2048]{1,0:T(8,128)(2,1)}) custom-call(bf16[1152,1024]{1,0:T(8,128)(2,1)S(1)} %pad_maximum_fusion.x_ref.refs_11_, bf16[1024,2048]{1,0:T(8,128)(2,1)} %get-tuple-element.57.w_ref.refs_23_, f32[1,2048]{1,0:T(1,128)S(1)} %bitcast.144), custom_call_target="tpu_custom_call" | custom-call | tf_op jit(solution)/shard_map/pallas_call | solution.py:282
  189.3 5.3 fusion.41
  195.0 2.8 collective-permute-done.2
  197.8 7.3 %fusion.91 = (f32[576]{0:T(1024)S(1)}, f32[576,1024]{1,0:T(8,128)S(1)}, f32[576,1024]{1,0:T(8,128)}) fusion(f32[1024]{0:T(1024)S(1)} %bitcast.209, bf16[576,1024]{1,0:T(8,128)(2,1)} %collective-permute-done.2, f32[1024]{0:T(1024)S(1)} %bitcast.190, f32[576,1024]{1,0:T(8,128)S(1)} %get-tuple-element.204.refs_26_, f32[1024]{0:T(1024)S(1)} %bitcast.171, ...), kind=kOutput, calls=%fused_computation.235 | convolution fusion | flops 2420047360 | bytes 14825728 | tf_op jit(solution)/shard_map/dot_general | solution.py:74
  206.7 3.6 collective-permute-start.3
  215.6 20.0 %collective-permute-done.3 = bf16[576,1024]{1,0:T(8,128)(2,1)S(1)} collective-permute-done((bf16[576,1024]{1,0:T(8,128)(2,1)S(1)}, bf16[576,1024]{1,0:T(8,128)(2,1)S(1)}, u32[]{:S(2)}, u32[]{:S(2)}) %collective-permute-start.3) | collective-permute-done | bytes 1179680 | tf_op jit(solution)/shard_map/ppermute | solution.py:40
  245.4 3.8 collective-permute-start.5
  249.3 5.8 fusion.q_ref.k_ref.v_ref
  255.2 16.6 %shard_map.367 = (bf16[1152,512]{1,0:T(8,128)(2,1)S(1)}, f32[4,2,1152]{2,1,0:T(2,128)S(1)}) custom-call(s32[8]{0:T(128)S(1)} %copy-done.13, s32[2,9]{1,0:T(2,128)S(1)} %copy-done.11, s32[1152,1]{1,0:T(8,128)S(1)} %copy-done.5, s32[1,1152]{1,0:T(1,128)S(1)} %copy-done.8, bf16[1152,1536]{1,0:T(8,128)(2,1)S(1)} %fusion.q_ref.k_ref.v_ref, ...), custom_call_target="tpu_custom_call" | custom-call | tf_op jit(solution)/shard_map/pallas_call | solution.py:172
  271.9 3.5 collective-permute-done.6
  276.3 2.8 collective-permute-done.8
  279.1 4.0 multiply_reduce_fusion.1
  284.5 2.7 collective-permute-done.9
  287.4 16.8 %shard_map.368 = (bf16[1152,2048]{1,0:T(8,128)(2,1)}, bf16[1152,2048]{1,0:T(8,128)(2,1)}) custom-call(bf16[1152,1024]{1,0:T(8,128)(2,1)S(1)} %pad_maximum_fusion.2.x_ref.refs_5_, bf16[1024,2048]{1,0:T(8,128)(2,1)} %get-tuple-element.57.w_ref.refs_23_, f32[1,2048]{1,0:T(1,128)S(1)} %bitcast.145), custom_call_target="tpu_custom_call" | custom-call | tf_op jit(solution)/shard_map/pallas_call | solution.py:282
  304.3 4.5 fusion.44
  309.0 2.7 collective-permute-done.10
  311.7 5.3 multiply_reduce_fusion
  319.2 2.4 convert_reduce_fusion.4
  321.8 2.7 collective-permute-done.12
  324.5 6.2 convert_reduce_fusion
  330.7 2.6 fusion.47
  333.6 2.7 collective-permute-done.13
  336.3 4.3 multiply_reduce_fusion.6
  340.6 2.7 convert_reduce_fusion.5
  346.1 2.2 multiply_reduce_fusion.2
  349.0 3.1 convolution_convert_fusion.up_ref
  352.2 24.9 %shard_map.369 = (bf16[1152,512]{1,0:T(8,128)(2,1)S(1)}, bf16[1152,512]{1,0:T(8,128)(2,1)S(1)}, bf16[1152,512]{1,0:T(8,128)(2,1)S(1)}) custom-call(s32[8]{0:T(128)S(1)} %copy-done.14, s32[2,9]{1,0:T(2,128)S(1)} %copy-done.12, s32[1152,1]{1,0:T(8,128)S(1)} %copy-done.6, s32[1,1152]{1,0:T(1,128)S(1)} %copy-done.8, bf16[1152,1536]{1,0:T(8,128)(2,1)} %copy-done.2, ...), custom_call_target="tpu_custom_call" | custom-call | tf_op jit(solution)/shard_map/pallas_call | solution.py:238
  377.3 1.7 copy-done.31
  379.1 3.1 fusion.50
  383.6 3.4 pad_maximum_fusion.1.refs_19_
  390.5 6.0 fusion.84
  399.5 2.4 collective-permute-start.18
  403.9 3.4 pad_maximum_fusion.3.refs_4_
  408.0 18.9 %collective-permute-done.16 = bf16[576,1024]{1,0:T(8,128)(2,1)} collective-permute-done((bf16[576,1024]{1,0:T(8,128)(2,1)}, bf16[576,1024]{1,0:T(8,128)(2,1)}, u32[]{:S(2)}, u32[]{:S(2)}) %collective-permute-start.16) | collective-permute-done | bytes 1179680 | tf_op jit(solution)/shard_map/ppermute | solution.py:40
  426.9 2.9 fusion.18
  429.8 4.0 convert_reduce_fusion.6
  436.1 4.0 broadcast_select_fusion.1
  440.3 2.9 fusion.56
  444.0 2.9 pad_maximum_fusion.5.refs_10_
  446.9 191.3 %shard_map.370 = (bf16[4,144,1024]{2,1,0:T(8,128)(2,1)}, f32[16,1024]{1,0:T(8,128)}, f32[8,128]{1,0:T(8,128)}, f32[512,512]{1,0:T(8,128)}, f32[512,512]{1,0:T(8,...) custom-call(bf16[4,144,1024]{2,1,0:T(8,128)(2,1)} %bitcast.148, ...), custom_call_target="tpu_custom_call" | custom-call | tf_op jit(solution)/shard_map/pallas_call | solution.py:1087
  642.0 3.2 copy.73
  647.3 1.9 copy.72
  (369 shorter events, 61.3 us)
Async XLA Ops:
  5.3 159.1 %copy-start.72 = (f32[576]{0:T(1024)}, f32[576]{0:T(1024)S(1)}, u32[]{:S(2)}) copy-start(f32[576]{0:T(1024)S(1)} %broadcast_multiply_fusion.10) | copy-start | bytes 6916
  6.9 157.6 %copy-start.97 = (f32[1,1024]{1,0:T(1,128)}, f32[1,1024]{1,0:T(1,128)S(1)}, u32[]{:S(2)}) copy-start(f32[1,1024]{1,0:T(1,128)S(1)} %get-tuple-element.237) | copy-start | bytes 12292
  6.9 162.1 %copy-start.78 = (f32[1,1024]{1,0:T(1,128)}, f32[1,1024]{1,0:T(1,128)S(1)}, u32[]{:S(2)}) copy-start(f32[1,1024]{1,0:T(1,128)S(1)} %get-tuple-element.235) | copy-start | bytes 12292
  6.9 190.9 %copy-start.58 = (f32[1,1024]{1,0:T(1,128)}, f32[1,1024]{1,0:T(1,128)S(1)}, u32[]{:S(2)}) copy-start(f32[1,1024]{1,0:T(1,128)S(1)} %get-tuple-element.236.refs_27_) | copy-start | bytes 12292
  6.9 198.7 %copy-start.53 = (f32[1,1024]{1,0:T(1,128)}, f32[1,1024]{1,0:T(1,128)S(1)}, u32[]{:S(2)}) copy-start(f32[1,1024]{1,0:T(1,128)S(1)} %get-tuple-element.233) | copy-start | bytes 12292
  161.5 2.9 collective-permute-start
  169.6 28.2 %copy-start.23 = (f32[576,1024]{1,0:T(8,128)}, f32[576,1024]{1,0:T(8,128)S(1)}, u32[]{:S(2)}) copy-start(f32[576,1024]{1,0:T(8,128)S(1)} %get-tuple-element.204.refs_26_) | copy-start | bytes 7077892
  169.6 2.8 collective-permute-start.1
  172.7 16.6 %copy-start.3 = (bf16[1152,1024]{1,0:T(8,128)(2,1)}, bf16[1152,1024]{1,0:T(8,128)(2,1)S(1)}, u32[]{:S(2)}) copy-start(bf16[1152,1024]{1,0:T(8,128)(2,1)S(1)} %pad_maximum_fusion.x_ref.refs_11_) | copy-start | bytes 7077892
  172.7 16.6 %copy-start.28 = (bf16[2048,1024]{1,0:T(8,128)(2,1)S(1)}, bf16[2048,1024]{1,0:T(8,128)(2,1)}, u32[]{:S(2)}) copy-start(bf16[2048,1024]{1,0:T(8,128)(2,1)} %get-tuple-element.60.refs_21_) | copy-start | bytes 12582916
  189.3 8.5 %copy-start.79 = (f32[1,1024]{1,0:T(1,128)S(1)}, f32[1,1024]{1,0:T(1,128)}, u32[]{:S(2)}) copy-start(f32[1,1024]{1,0:T(1,128)} %copy-done.78) | copy-start | bytes 12292
  189.3 8.5 %copy-start.95 = (f32[1,1024]{1,0:T(1,128)S(1)}, f32[1,1024]{1,0:T(1,128)}, u32[]{:S(2)}) copy-start(f32[1,1024]{1,0:T(1,128)} %get-tuple-element.234) | copy-start | bytes 12292
  194.6 3.2 collective-permute-start.2
  205.5 30.0 %copy-start.65 = (f32[1,1024]{1,0:T(1,128)S(1)}, f32[1,1024]{1,0:T(1,128)}, u32[]{:S(2)}) copy-start(f32[1,1024]{1,0:T(1,128)} %get-tuple-element.238.refs_10_) | copy-start | bytes 12292
  205.6 30.0 %copy-start.69 = (f32[1,1024]{1,0:T(1,128)S(1)}, f32[1,1024]{1,0:T(1,128)}, u32[]{:S(2)}) copy-start(f32[1,1024]{1,0:T(1,128)} %get-tuple-element.239.refs_9_) | copy-start | bytes 12292
  205.6 30.0 %copy-start.73 = (f32[576]{0:T(1024)S(1)}, f32[576]{0:T(1024)}, u32[]{:S(2)}) copy-start(f32[576]{0:T(1024)} %copy-done.72) | copy-start | bytes 6916
  206.2 37.7 %copy-start.34 = (bf16[144,4,1024]{2,1,0:T(4,128)(2,1)S(1)}, bf16[144,4,1024]{2,1,0:T(4,128)(2,1)}, u32[]{:S(2)}) copy-start(bf16[144,4,1024]{2,1,0:T(4,128)(2,1)} %param.23) | copy-start | bytes 3538948
  206.7 30.2 %copy-start.104 = (s32[2,4]{1,0:T(2,128)S(1)}, s32[2,4]{1,0:T(2,128)}, u32[]{:S(2)}) copy-start(s32[2,4]{1,0:T(2,128)} %copy-done.103) | copy-start | bytes 100
  206.7 28.9 %collective-permute-start.3 = (bf16[576,1024]{1,0:T(8,128)(2,1)S(1)}, bf16[576,1024]{1,0:T(8,128)(2,1)S(1)}, u32[]{:S(2)}, u32[]{:S(2)}) collective-permute-start(bf16[576,1024]{1,0:T(8,128)(2,1)S(1)} %add_convert_fusion.1), channel_id=1, source_target_pairs={{0,16},{1,17},{2,18},{3,19},{4,20},{5,21},{6,22},{7,23},{8,24},{9,... | collective-permute-start | bytes 3538952 | tf_op jit(solution)/shard_map/ppermute | solution.py:40
  235.6 8.6 %copy-start.37 = (bf16[576,1024]{1,0:T(8,128)(2,1)}, bf16[576,1024]{1,0:T(8,128)(2,1)S(1)}, u32[]{:S(2)}) copy-start(bf16[576,1024]{1,0:T(8,128)(2,1)S(1)} %collective-permute-done.3) | copy-start | bytes 3538948
  236.0 13.2 %copy-start.24 = (bf16[576,1024]{1,0:T(8,128)(2,1)}, bf16[576,1024]{1,0:T(8,128)(2,1)S(1)}, u32[]{:S(2)}) copy-start(bf16[576,1024]{1,0:T(8,128)(2,1)S(1)} %fusion.28) | copy-start | bytes 3538948
  236.0 13.2 %collective-permute-start.4 = (bf16[576,1024]{1,0:T(8,128)(2,1)S(1)}, bf16[576,1024]{1,0:T(8,128)(2,1)}, u32[]{:S(2)}, u32[]{:S(2)}) collective-permute-start(bf16[576,1024]{1,0:T(8,128)(2,1)S(1)} %fusion.28), channel_id=1, source_target_pairs={{1,0},{0,1},{3,2},{2,3},{5,4},{4,5},{7,6},{6,7},{9,8},{8,9},{11,10... | collective-permute-start | bytes 3538952 | tf_op jit(solution)/shard_map/ppermute | solution.py:34
  245.4 26.5 %collective-permute-start.7 = (bf16[144,1024]{1,0:T(8,128)(2,1)S(1)}, bf16[144,1024]{1,0:T(8,128)(2,1)S(1)}, u32[]{:S(2)}, u32[]{:S(2)}) collective-permute-start(bf16[144,1024]{1,0:T(8,128)(2,1)S(1)} %get-tuple-element.221), channel_id=1, source_target_pairs={{6,0},{0,2},{2,4},{4,6},{7,1},{1,3},{3,5},{5,7},{14,8},{8,10},{10,... | collective-permute-start | bytes 884744 | tf_op jit(solution)/shard_map/ppermute | solution.py:34
  245.4 26.5 %collective-permute-start.5 = (bf16[144,1024]{1,0:T(8,128)(2,1)S(1)}, bf16[144,1024]{1,0:T(8,128)(2,1)S(1)}, u32[]{:S(2)}, u32[]{:S(2)}) collective-permute-start(bf16[144,1024]{1,0:T(8,128)(2,1)S(1)} %get-tuple-element.223), channel_id=1, source_target_pairs={{2,0},{4,2},{6,4},{0,6},{3,1},{5,3},{7,5},{1,7},{10,8},{12,10},{14... | collective-permute-start | bytes 884744 | tf_op jit(solution)/shard_map/ppermute | solution.py:34
  249.3 26.1 %collective-permute-start.6 = (bf16[144,1024]{1,0:T(8,128)(2,1)S(1)}, bf16[144,1024]{1,0:T(8,128)(2,1)S(1)}, u32[]{:S(2)}, u32[]{:S(2)}) collective-permute-start(bf16[144,1024]{1,0:T(8,128)(2,1)S(1)} %get-tuple-element.224), channel_id=1, source_target_pairs={{4,0},{6,2},{0,4},{2,6},{5,1},{7,3},{1,5},{3,7},{12,8},{14,10},{8,... | collective-permute-start | bytes 884744 | tf_op jit(solution)/shard_map/ppermute | solution.py:34
  255.1 16.6 %copy-start.2 = (bf16[1152,1536]{1,0:T(8,128)(2,1)}, bf16[1152,1536]{1,0:T(8,128)(2,1)S(1)}, u32[]{:S(2)}) copy-start(bf16[1152,1536]{1,0:T(8,128)(2,1)S(1)} %fusion.q_ref.k_ref.v_ref) | copy-start | bytes 10616836
  255.1 20.2 %copy-start.44 = (bf16[512,1024]{1,0:T(8,128)(2,1)S(1)}, bf16[512,1024]{1,0:T(8,128)(2,1)}, u32[]{:S(2)}) copy-start(bf16[512,1024]{1,0:T(8,128)(2,1)} %get-tuple-element.56.refs_24_) | copy-start | bytes 3145732
  271.8 11.3 %copy-start.7 = (bf16[1152,512]{1,0:T(8,128)(2,1)}, bf16[1152,512]{1,0:T(8,128)(2,1)S(1)}, u32[]{:S(2)}) copy-start(bf16[1152,512]{1,0:T(8,128)(2,1)S(1)} %get-tuple-element.64.refs_7_) | copy-start | bytes 3538948
  271.8 11.3 %copy-start.9 = (f32[4,2,1152]{2,1,0:T(2,128)}, f32[4,2,1152]{2,1,0:T(2,128)S(1)}, u32[]{:S(2)}) copy-start(f32[4,2,1152]{2,1,0:T(2,128)S(1)} %get-tuple-element.67.lse_ref) | copy-start | bytes 110596
  276.2 2.9 collective-permute-start.8
  284.3 2.9 collective-permute-start.9
  287.4 16.9 %copy-start.4 = (bf16[1152,1024]{1,0:T(8,128)(2,1)}, bf16[1152,1024]{1,0:T(8,128)(2,1)S(1)}, u32[]{:S(2)}) copy-start(bf16[1152,1024]{1,0:T(8,128)(2,1)S(1)} %pad_maximum_fusion.2.x_ref.refs_5_) | copy-start | bytes 7077892
  287.4 16.9 %copy-start.29 = (bf16[2048,1024]{1,0:T(8,128)(2,1)S(1)}, bf16[2048,1024]{1,0:T(8,128)(2,1)}, u32[]{:S(2)}) copy-start(bf16[2048,1024]{1,0:T(8,128)(2,1)} %get-tuple-element.60.refs_21_) | copy-start | bytes 12582916
  308.8 2.9 collective-permute-start.10
  317.0 19.3 %copy-start.18 = (f32[576,1024]{1,0:T(8,128)}, f32[576,1024]{1,0:T(8,128)S(1)}, u32[]{:S(2)}) copy-start(f32[576,1024]{1,0:T(8,128)S(1)} %get-tuple-element.210) | copy-start | bytes 7077892
  317.0 19.3 %copy-start.62 = (f32[576]{0:T(1024)}, f32[576]{0:T(1024)S(1)}, u32[]{:S(2)}) copy-start(f32[576]{0:T(1024)S(1)} %broadcast_multiply_fusion.6) | copy-start | bytes 6916
  317.7 18.6 %copy-start.76 = (f32[576]{0:T(1024)}, f32[576]{0:T(1024)S(1)}, u32[]{:S(2)}) copy-start(f32[576]{0:T(1024)S(1)} %add_rsqrt_fusion) | copy-start | bytes 6916
  321.7 9.1 %copy-start.25 = (bf16[576,1024]{1,0:T(8,128)(2,1)}, bf16[576,1024]{1,0:T(8,128)(2,1)S(1)}, u32[]{:S(2)}) copy-start(bf16[576,1024]{1,0:T(8,128)(2,1)S(1)} %get-tuple-element.189) | copy-start | bytes 3538948
  321.7 2.8 collective-permute-start.12
  333.4 2.9 collective-permute-start.13
  343.4 5.6 collective-permute-start.14
  382.1 7.4 %collective-permute-start.15 = (bf16[576,1024]{1,0:T(8,128)(2,1)}, bf16[576,1024]{1,0:T(8,128)(2,1)}, u32[]{:S(2)}, u32[]{:S(2)}) collective-permute-start(bf16[576,1024]{1,0:T(8,128)(2,1)} %fusion.50), channel_id=1, source_target_pairs={{1,0},{0,1},{3,2},{2,3},{5,4},{4,5},{7,6},{6,7},{9,8},{8,9},{11,10... | collective-permute-start | bytes 3538952 | tf_op jit(solution)/shard_map/ppermute | solution.py:34
  396.6 30.3 %collective-permute-start.16 = (bf16[576,1024]{1,0:T(8,128)(2,1)}, bf16[576,1024]{1,0:T(8,128)(2,1)}, u32[]{:S(2)}, u32[]{:S(2)}) collective-permute-start(bf16[576,1024]{1,0:T(8,128)(2,1)} %get-tuple-element.211), channel_id=1, source_target_pairs={{16,0},{17,1},{18,2},{19,3},{20,4},{21,5},{22,6},{23,7},{24,8},{25... | collective-permute-start | bytes 3538952 | tf_op jit(solution)/shard_map/ppermute | solution.py:40
  398.9 246.3 %collective-permute-start.19 = (bf16[144,1024]{1,0:T(8,128)(2,1)}, bf16[144,1024]{1,0:T(8,128)(2,1)}, u32[]{:S(2)}, u32[]{:S(2)}) collective-permute-start(bf16[144,1024]{1,0:T(8,128)(2,1)} %get-tuple-element.218), channel_id=1, source_target_pairs={{2,0},{4,2},{6,4},{0,6},{3,1},{5,3},{7,5},{1,7},{10,8},{12,10},{14... | collective-permute-start | bytes 884744 | tf_op jit(solution)/shard_map/ppermute | solution.py:34
  399.5 245.7 %collective-permute-start.18 = (bf16[144,1024]{1,0:T(8,128)(2,1)}, bf16[144,1024]{1,0:T(8,128)(2,1)}, u32[]{:S(2)}, u32[]{:S(2)}) collective-permute-start(bf16[144,1024]{1,0:T(8,128)(2,1)} %get-tuple-element.219), channel_id=1, source_target_pairs={{4,0},{6,2},{0,4},{2,6},{5,1},{7,3},{1,5},{3,7},{12,8},{14,10},{8,... | collective-permute-start | bytes 884744 | tf_op jit(solution)/shard_map/ppermute | solution.py:34
  401.9 243.9 %collective-permute-start.11 = (bf16[144,1024]{1,0:T(8,128)(2,1)}, bf16[144,1024]{1,0:T(8,128)(2,1)}, u32[]{:S(2)}, u32[]{:S(2)}) collective-permute-start(bf16[144,1024]{1,0:T(8,128)(2,1)} %get-tuple-element.220), channel_id=1, source_target_pairs={{6,0},{0,2},{2,4},{4,6},{7,1},{1,3},{3,5},{5,7},{14,8},{8,10},{10,... | collective-permute-start | bytes 884744 | tf_op jit(solution)/shard_map/ppermute | solution.py:34
  433.8 10.1 %collective-permute-start.17 = (bf16[576,1024]{1,0:T(8,128)(2,1)}, bf16[576,1024]{1,0:T(8,128)(2,1)S(1)}, u32[]{:S(2)}, u32[]{:S(2)}) collective-permute-start(bf16[576,1024]{1,0:T(8,128)(2,1)} %get-tuple-element.194), channel_id=1, source_target_pairs={{1,0},{0,1},{3,2},{2,3},{5,4},{4,5},{7,6},{6,7},{9,8},{8,9},{11,10... | collective-permute-start | bytes 3538952 | tf_op jit(solution)/shard_map/ppermute | solution.py:34
  638.2 7.5 %copy-start.33 = (bf16[1,144,1024]{2,1,0:T(8,128)(2,1)S(1)}, bf16[1,144,1024]{2,1,0:T(8,128)(2,1)}, u32[]{:S(2)}) copy-start(bf16[1,144,1024]{2,1,0:T(8,128)(2,1)} %get-tuple-element.74) | copy-start | bytes 884740
  (86 other events, 375.1 us)

commit v6 on v5

--- a/solution.py
+++ b/solution.py
@@ -1342,9 +1342,7 @@
         ffn_branch = returned(hidden, ffn_out_all, ((1,), (0,))) + ffn_out_bias
         second_normed, second_inverse = norm_parts(first_out + ffn_branch)
         layer_y = (second_normed * ffn_gain + ffn_shift).astype(bf16)
-        terms = jnp.stack(
-            [jnp.sum(residual * residual), jnp.sum(branch * branch), jnp.sum(ffn_branch * ffn_branch)]
-        )
+        terms = jnp.stack([token_sum(each * each) for each in (residual, branch, ffn_branch)])
         kept.append(
             (
                 rounded_all,
@@ -1502,10 +1500,9 @@
         if not last:
             upstream_rows = passed_along(grad_in, "pipe", -1)
     vector_sums, slot_sums, grad_in = results
-    stat_row = jnp.concatenate([stat_terms, jnp.zeros((width - 3,), f32)])[None]
-    shared = jnp.concatenate([straightened(vector_sums), stat_row])
+    shared = straightened(jnp.concatenate([vector_sums, stat_terms]))
     if in_kernels:
-        small = jnp.concatenate([shared, jnp.zeros((7, width), f32)])
+        small = jnp.concatenate([shared, jnp.zeros((5, width), f32)])
         padded = -(-slot_sums.shape[1] // 1024) * 1024
         slots = jnp.pad(slot_sums, ((0, 0), (0, padded - slot_sums.shape[1])))
         by_block = straightened(grad_in_before).reshape(seqs, rows, width)
@@ -1522,7 +1519,7 @@
             tp_size,
         )
         input_grad = jnp.transpose(input_pieces, (1, 0, 2))
-        shared, own_slot = small[:9], slots.reshape(1, padded)[:, : slot_sums.shape[1]]
+        shared, own_slot = small[:11], slots.reshape(1, padded)[:, : slot_sums.shape[1]]
         ffn_out_grad, ffn_in_grad, out_grad = gradients[:3]
         triple = gradients[3:]
     else:
@@ -1539,7 +1536,7 @@
         triple = [joined_grad[:, i * head_cols : (i + 1) * head_cols] for i in range(3)]
     layer_out = in_positions(layer_pieces, grad_ffn_all)
     element_count = float(SEQ_LEN * seqs * dp_size * width)
-    stats = jnp.sqrt(shared[8:9, :3] / element_count)
+    stats = jnp.sqrt(jnp.sum(shared[8:11], axis=1) / element_count)
     return (
         layer_out[None],
         input_grad[None],
@@ -1560,7 +1557,7 @@
         shared[5:6],
         shared[6:7],
         shared[7:8],
-        stats,
+        stats[None],
     )
 
 

time: 665 us -> 656 us (0.986)
  other arithmetic: 51.2 us -> 43.6 us
    unnamed x249 -> x267, local copies, waits for them, and re-layouts: 27.9 us -> 26.8 us
    reduce_sum x6 -> x7, other arithmetic: 14.1 us -> 15.3 us  [token_sum(): return jnp.sum(values.astype(f32), axis=0)]
  transfers between devices with their start and end apart: 20 -> 20, of which waited for: 11 -> 12; matrix products, arithmetic and copies ran while one was open for 10% -> 9% of each run, Pallas kernels for 32% -> 32%
where the time goes in v6:
time: 656 us; the launch traced here: 647 us
  Pallas kernels  414 us (63%)
  waiting for transfers between devices  67 us (10%)
  matrix products  66.7 us (10%)
  other arithmetic  43.6 us (7%)
  local copies, waits for them, and re-layouts  40.4 us (6%)
  starting transfers between devices  12.4 us (2%)
    pallas_call x1, Pallas kernels, scatter_all(): pl.pallas_call(functools.partial(scatter_kernel, rows, seqs, dp_size, tp_...  193 us
    pallas_call x1, Pallas kernels, gather_all(): pl.pallas_call(functools.partial(gather_kernel, seqs, dp_size, tp_size),...  147 us
    dot_general x15, matrix products, mm(): return lax.dot_general(a, b, (dims, ((), ())), preferred_element_type=f32)  66.7 us
    ppermute x2, waiting for transfers between devices, passed_along(): return lax.ppermute(shard, axis, pairs)  39.3 us
    pallas_call x2, Pallas kernels, widen(): pl.pallas_call(functools.partial(widen_kernel, 144), grid=(units // step,...  33.4 us
    ppermute x18, waiting for transfers between devices, received(): lax.ppermute(shard, axis, [((i + by) % size, i) for i in range(size)])  27.7 us
    unnamed x267, local copies, waits for them, and re-layouts  26.8 us
    pallas_call x1, Pallas kernels, attend_back(): pl.pallas_call(functools.partial(attend_back_kernel, rows), grid=(1,), in...  25.1 us
  transfers between devices with their start and end apart: 20, of which 12 were waited for; matrix products, arithmetic and copies ran while one was open for 9% of the time, Pallas kernels for 32%

profile of v6, /device:TPU:0, one launch (start us, length us, event | category | flops | bytes accessed | tf_op | source)
XLA Modules:
  0.0 647.0 jit_solution(2465465726411926023)
XLA Ops:
  8.9 1.6 copy.79
  10.5 1.7 fusion.58.refs_0_
  12.2 146.9 %shard_map.365 = (bf16[4,144,1024]{2,1,0:T(8,128)(2,1)}, f32[4,1,768]{2,1,0:T(1,128)}, bf16[1024,1536]{1,0:T(8,128)(2,1)}, bf16[512,1024]{1,0:T(8,128)(2,1)}, bf...) custom-call(bf16[4,144,1024]{2,1,0:T(8,128)(2,1)} %fusion.58.refs_0_, ...), custom_call_target="tpu_custom_call" | custom-call | tf_op jit(solution)/shard_map/pallas_call | solution.py:540
  159.2 2.3 convolution_convert_fusion.2
  161.6 2.8 collective-permute-done
  164.5 4.1 fusion.95
  169.8 2.7 collective-permute-done.1
  172.7 16.6 %shard_map.366 = (bf16[1152,2048]{1,0:T(8,128)(2,1)}, bf16[1152,2048]{1,0:T(8,128)(2,1)}) custom-call(bf16[1152,1024]{1,0:T(8,128)(2,1)S(1)} %pad_maximum_fusion.x_ref.refs_11_, bf16[1024,2048]{1,0:T(8,128)(2,1)} %get-tuple-element.57.w_ref.refs_23_, f32[1,2048]{1,0:T(1,128)S(1)} %bitcast.145), custom_call_target="tpu_custom_call" | custom-call | tf_op jit(solution)/shard_map/pallas_call | solution.py:282
  189.3 5.3 fusion.41
  195.0 2.8 collective-permute-done.2
  197.8 7.3 %fusion.93 = (f32[576]{0:T(1024)S(1)}, f32[576,1024]{1,0:T(8,128)S(1)}, f32[576,1024]{1,0:T(8,128)}) fusion(f32[1024]{0:T(1024)S(1)} %bitcast.210, bf16[576,1024]{1,0:T(8,128)(2,1)} %collective-permute-done.2, f32[1024]{0:T(1024)S(1)} %bitcast.191, f32[576,1024]{1,0:T(8,128)S(1)} %get-tuple-element.204.refs_26_, f32[1024]{0:T(1024)S(1)} %bitcast.172, ...), kind=kOutput, calls=%fused_computation.239 | convolution fusion | flops 2420047360 | bytes 14825728 | tf_op jit(solution)/shard_map/dot_general | solution.py:74
  206.7 3.7 collective-permute-start.3
  215.7 20.0 %collective-permute-done.3 = bf16[576,1024]{1,0:T(8,128)(2,1)S(1)} collective-permute-done((bf16[576,1024]{1,0:T(8,128)(2,1)S(1)}, bf16[576,1024]{1,0:T(8,128)(2,1)S(1)}, u32[]{:S(2)}, u32[]{:S(2)}) %collective-permute-start.3) | collective-permute-done | bytes 1179680 | tf_op jit(solution)/shard_map/ppermute | solution.py:40
  245.5 3.8 collective-permute-start.5
  249.4 5.8 fusion.q_ref.k_ref.v_ref
  255.2 16.5 %shard_map.367 = (bf16[1152,512]{1,0:T(8,128)(2,1)S(1)}, f32[4,2,1152]{2,1,0:T(2,128)S(1)}) custom-call(s32[8]{0:T(128)S(1)} %copy-done.13, s32[2,9]{1,0:T(2,128)S(1)} %copy-done.11, s32[1152,1]{1,0:T(8,128)S(1)} %copy-done.5, s32[1,1152]{1,0:T(1,128)S(1)} %copy-done.8, bf16[1152,1536]{1,0:T(8,128)(2,1)S(1)} %fusion.q_ref.k_ref.v_ref, ...), custom_call_target="tpu_custom_call" | custom-call | tf_op jit(solution)/shard_map/pallas_call | solution.py:172
  271.8 3.7 collective-permute-done.6
  276.3 2.8 collective-permute-done.8
  279.2 4.1 multiply_reduce_fusion.1
  284.6 2.7 collective-permute-done.9
  287.5 16.9 %shard_map.368 = (bf16[1152,2048]{1,0:T(8,128)(2,1)}, bf16[1152,2048]{1,0:T(8,128)(2,1)}) custom-call(bf16[1152,1024]{1,0:T(8,128)(2,1)S(1)} %pad_maximum_fusion.2.x_ref.refs_5_, bf16[1024,2048]{1,0:T(8,128)(2,1)} %get-tuple-element.57.w_ref.refs_23_, f32[1,2048]{1,0:T(1,128)S(1)} %bitcast.146), custom_call_target="tpu_custom_call" | custom-call | tf_op jit(solution)/shard_map/pallas_call | solution.py:282
  304.5 4.5 fusion.44
  309.1 2.7 collective-permute-done.10
  311.9 5.5 multiply_reduce_fusion
  319.6 2.4 convert_reduce_fusion.4
  322.1 2.7 collective-permute-done.12
  324.9 8.3 %convert_reduce_fusion = (f32[2048]{0:T(1024)}, bf16[1152,2048]{1,0:T(8,128)(2,1)S(1)}) fusion(bf16[1152,2048]{1,0:T(8,128)(2,1)} %get-tuple-element.66, bf16[2048,1024]{1,0:T(8,128)(2,1)S(1)} %copy-done.30, bf16[576,1024]{1,0:T(8,128)(2,1)S(1)} %collective-permute-done.12, bf16[576,1024]{1,0:T(8,128)(2,1)S(1)} %get-tuple-element.189), kind=kOutput, calls=%fused_computation.1 | convolution fusion | flops 4848351232 | bytes 15998976 | tf_op jit(solution)/shard_map/dot_general | solution.py:74
  333.2 2.6 fusion.47
  336.0 2.7 collective-permute-done.13
  338.8 4.3 multiply_reduce_fusion.6
  343.1 2.7 convert_reduce_fusion.5
  346.7 2.0 collective-permute-done.14
  350.1 25.1 %shard_map.369 = (bf16[1152,512]{1,0:T(8,128)(2,1)S(1)}, bf16[1152,512]{1,0:T(8,128)(2,1)S(1)}, bf16[1152,512]{1,0:T(8,128)(2,1)S(1)}) custom-call(s32[8]{0:T(128)S(1)} %copy-done.14, s32[2,9]{1,0:T(2,128)S(1)} %copy-done.12, s32[1152,1]{1,0:T(8,128)S(1)} %copy-done.6, s32[1,1152]{1,0:T(1,128)S(1)} %copy-done.8, bf16[1152,1536]{1,0:T(8,128)(2,1)} %copy-done.2, ...), custom_call_target="tpu_custom_call" | custom-call | tf_op jit(solution)/shard_map/pallas_call | solution.py:238
  375.5 1.7 copy-done.32
  377.2 3.1 fusion.50
  383.3 3.0 pad_maximum_fusion.1.refs_19_
  386.4 7.3 %fusion.86 = (f32[1024]{0:T(1024)}, f32[1024]{0:T(1024)}, f32[1024]{0:T(1024)}, bf16[576,1024]{1,0:T(8,128)(2,1)}) fusion(f32[576]{0:T(1024)} %copy-done.73, f32[1024]{0:T(1024)} %bitcast.177, f32[1024]{0:T(1024)} %bitcast.182, bf16[576,1024]{1,0:T(8,128)(2,1)S(1)} %copy-done.39, f32[576,1024]{1,0:T(8,128)} %get-tuple-element.192, ...), kind=kOutput, calls=%fused_computation.236 | convolution fusion | flops 1819603968 | bytes 10836224 | tf_op jit(solution)/shard_map/dot_general | solution.py:74
  397.7 2.0 collective-permute-start.11
  401.0 3.4 pad_maximum_fusion.3.refs_4_
  405.0 19.3 %collective-permute-done.16 = bf16[576,1024]{1,0:T(8,128)(2,1)} collective-permute-done((bf16[576,1024]{1,0:T(8,128)(2,1)}, bf16[576,1024]{1,0:T(8,128)(2,1)}, u32[]{:S(2)}, u32[]{:S(2)}) %collective-permute-start.16) | collective-permute-done | bytes 1179680 | tf_op jit(solution)/shard_map/ppermute | solution.py:40
  424.3 2.9 fusion.18
  427.2 4.0 convert_reduce_fusion.6
  432.0 1.6 pad_maximum_fusion.4.refs_8_
  433.8 2.9 fusion.56
  437.4 2.9 pad_maximum_fusion.5.refs_10_
  440.4 192.5 %shard_map.370 = (bf16[4,144,1024]{2,1,0:T(8,128)(2,1)}, f32[16,1024]{1,0:T(8,128)}, f32[8,128]{1,0:T(8,128)}, f32[512,512]{1,0:T(8,128)}, f32[512,512]{1,0:T(8,...) custom-call(bf16[4,144,1024]{2,1,0:T(8,128)(2,1)} %bitcast.149, ...), custom_call_target="tpu_custom_call" | custom-call | tf_op jit(solution)/shard_map/pallas_call | solution.py:1087
  632.9 3.2 copy.73
  639.5 1.9 copy.72
  (384 shorter events, 53.1 us)
Async XLA Ops:
  5.3 159.1 %copy-start.73 = (f32[576]{0:T(1024)}, f32[576]{0:T(1024)S(1)}, u32[]{:S(2)}) copy-start(f32[576]{0:T(1024)S(1)} %broadcast_multiply_fusion.10) | copy-start | bytes 6916
  6.9 157.6 %copy-start.103 = (f32[1,1024]{1,0:T(1,128)}, f32[1,1024]{1,0:T(1,128)S(1)}, u32[]{:S(2)}) copy-start(f32[1,1024]{1,0:T(1,128)S(1)} %get-tuple-element.237) | copy-start | bytes 12292
  6.9 162.1 %copy-start.82 = (f32[1,1024]{1,0:T(1,128)}, f32[1,1024]{1,0:T(1,128)S(1)}, u32[]{:S(2)}) copy-start(f32[1,1024]{1,0:T(1,128)S(1)} %get-tuple-element.235) | copy-start | bytes 12292
  6.9 190.9 %copy-start.59 = (f32[1,1024]{1,0:T(1,128)}, f32[1,1024]{1,0:T(1,128)S(1)}, u32[]{:S(2)}) copy-start(f32[1,1024]{1,0:T(1,128)S(1)} %get-tuple-element.236.refs_27_) | copy-start | bytes 12292
  6.9 198.7 %copy-start.54 = (f32[1,1024]{1,0:T(1,128)}, f32[1,1024]{1,0:T(1,128)S(1)}, u32[]{:S(2)}) copy-start(f32[1,1024]{1,0:T(1,128)S(1)} %get-tuple-element.233) | copy-start | bytes 12292
  161.5 2.9 collective-permute-start
  169.6 28.2 %copy-start.23 = (f32[576,1024]{1,0:T(8,128)}, f32[576,1024]{1,0:T(8,128)S(1)}, u32[]{:S(2)}) copy-start(f32[576,1024]{1,0:T(8,128)S(1)} %get-tuple-element.204.refs_26_) | copy-start | bytes 7077892
  169.6 2.9 collective-permute-start.1
  172.7 16.6 %copy-start.3 = (bf16[1152,1024]{1,0:T(8,128)(2,1)}, bf16[1152,1024]{1,0:T(8,128)(2,1)S(1)}, u32[]{:S(2)}) copy-start(bf16[1152,1024]{1,0:T(8,128)(2,1)S(1)} %pad_maximum_fusion.x_ref.refs_11_) | copy-start | bytes 7077892
  172.7 16.6 %copy-start.29 = (bf16[2048,1024]{1,0:T(8,128)(2,1)S(1)}, bf16[2048,1024]{1,0:T(8,128)(2,1)}, u32[]{:S(2)}) copy-start(bf16[2048,1024]{1,0:T(8,128)(2,1)} %get-tuple-element.60.refs_21_) | copy-start | bytes 12582916
  194.6 3.2 collective-permute-start.2
  205.5 30.1 %copy-start.66 = (f32[1,1024]{1,0:T(1,128)S(1)}, f32[1,1024]{1,0:T(1,128)}, u32[]{:S(2)}) copy-start(f32[1,1024]{1,0:T(1,128)} %get-tuple-element.238.refs_10_) | copy-start | bytes 12292
  205.6 30.1 %copy-start.70 = (f32[1,1024]{1,0:T(1,128)S(1)}, f32[1,1024]{1,0:T(1,128)}, u32[]{:S(2)}) copy-start(f32[1,1024]{1,0:T(1,128)} %get-tuple-element.239.refs_9_) | copy-start | bytes 12292
  205.6 30.1 %copy-start.74 = (f32[576]{0:T(1024)S(1)}, f32[576]{0:T(1024)}, u32[]{:S(2)}) copy-start(f32[576]{0:T(1024)} %copy-done.73) | copy-start | bytes 6916
  206.2 37.7 %copy-start.34 = (bf16[144,4,1024]{2,1,0:T(4,128)(2,1)S(1)}, bf16[144,4,1024]{2,1,0:T(4,128)(2,1)}, u32[]{:S(2)}) copy-start(bf16[144,4,1024]{2,1,0:T(4,128)(2,1)} %param.23) | copy-start | bytes 3538948
  206.7 30.2 %copy-start.116 = (s32[2,4]{1,0:T(2,128)S(1)}, s32[2,4]{1,0:T(2,128)}, u32[]{:S(2)}) copy-start(s32[2,4]{1,0:T(2,128)} %copy-done.115) | copy-start | bytes 100
  206.7 29.0 %collective-permute-start.3 = (bf16[576,1024]{1,0:T(8,128)(2,1)S(1)}, bf16[576,1024]{1,0:T(8,128)(2,1)S(1)}, u32[]{:S(2)}, u32[]{:S(2)}) collective-permute-start(bf16[576,1024]{1,0:T(8,128)(2,1)S(1)} %add_convert_fusion.1), channel_id=1, source_target_pairs={{0,16},{1,17},{2,18},{3,19},{4,20},{5,21},{6,22},{7,23},{8,24},{9,... | collective-permute-start | bytes 3538952 | tf_op jit(solution)/shard_map/ppermute | solution.py:40
  236.1 13.2 %copy-start.24 = (bf16[576,1024]{1,0:T(8,128)(2,1)}, bf16[576,1024]{1,0:T(8,128)(2,1)S(1)}, u32[]{:S(2)}) copy-start(bf16[576,1024]{1,0:T(8,128)(2,1)S(1)} %fusion.28) | copy-start | bytes 3538948
  236.1 13.2 %collective-permute-start.4 = (bf16[576,1024]{1,0:T(8,128)(2,1)S(1)}, bf16[576,1024]{1,0:T(8,128)(2,1)}, u32[]{:S(2)}, u32[]{:S(2)}) collective-permute-start(bf16[576,1024]{1,0:T(8,128)(2,1)S(1)} %fusion.28), channel_id=1, source_target_pairs={{1,0},{0,1},{3,2},{2,3},{5,4},{4,5},{7,6},{6,7},{9,8},{8,9},{11,10... | collective-permute-start | bytes 3538952 | tf_op jit(solution)/shard_map/ppermute | solution.py:34
  245.4 26.3 %collective-permute-start.7 = (bf16[144,1024]{1,0:T(8,128)(2,1)S(1)}, bf16[144,1024]{1,0:T(8,128)(2,1)S(1)}, u32[]{:S(2)}, u32[]{:S(2)}) collective-permute-start(bf16[144,1024]{1,0:T(8,128)(2,1)S(1)} %get-tuple-element.221), channel_id=1, source_target_pairs={{6,0},{0,2},{2,4},{4,6},{7,1},{1,3},{3,5},{5,7},{14,8},{8,10},{10,... | collective-permute-start | bytes 884744 | tf_op jit(solution)/shard_map/ppermute | solution.py:34
  245.5 26.3 %collective-permute-start.5 = (bf16[144,1024]{1,0:T(8,128)(2,1)S(1)}, bf16[144,1024]{1,0:T(8,128)(2,1)S(1)}, u32[]{:S(2)}, u32[]{:S(2)}) collective-permute-start(bf16[144,1024]{1,0:T(8,128)(2,1)S(1)} %get-tuple-element.223), channel_id=1, source_target_pairs={{2,0},{4,2},{6,4},{0,6},{3,1},{5,3},{7,5},{1,7},{10,8},{12,10},{14... | collective-permute-start | bytes 884744 | tf_op jit(solution)/shard_map/ppermute | solution.py:34
  249.3 26.2 %collective-permute-start.6 = (bf16[144,1024]{1,0:T(8,128)(2,1)S(1)}, bf16[144,1024]{1,0:T(8,128)(2,1)S(1)}, u32[]{:S(2)}, u32[]{:S(2)}) collective-permute-start(bf16[144,1024]{1,0:T(8,128)(2,1)S(1)} %get-tuple-element.224), channel_id=1, source_target_pairs={{4,0},{6,2},{0,4},{2,6},{5,1},{7,3},{1,5},{3,7},{12,8},{14,10},{8,... | collective-permute-start | bytes 884744 | tf_op jit(solution)/shard_map/ppermute | solution.py:34
  255.2 16.5 %copy-start.2 = (bf16[1152,1536]{1,0:T(8,128)(2,1)}, bf16[1152,1536]{1,0:T(8,128)(2,1)S(1)}, u32[]{:S(2)}) copy-start(bf16[1152,1536]{1,0:T(8,128)(2,1)S(1)} %fusion.q_ref.k_ref.v_ref) | copy-start | bytes 10616836
  255.2 20.3 %copy-start.44 = (bf16[512,1024]{1,0:T(8,128)(2,1)S(1)}, bf16[512,1024]{1,0:T(8,128)(2,1)}, u32[]{:S(2)}) copy-start(bf16[512,1024]{1,0:T(8,128)(2,1)} %get-tuple-element.56.refs_24_) | copy-start | bytes 3145732
  271.7 11.6 %copy-start.7 = (bf16[1152,512]{1,0:T(8,128)(2,1)}, bf16[1152,512]{1,0:T(8,128)(2,1)S(1)}, u32[]{:S(2)}) copy-start(bf16[1152,512]{1,0:T(8,128)(2,1)S(1)} %get-tuple-element.64.refs_7_) | copy-start | bytes 3538948
  271.7 11.6 %copy-start.9 = (f32[4,2,1152]{2,1,0:T(2,128)}, f32[4,2,1152]{2,1,0:T(2,128)S(1)}, u32[]{:S(2)}) copy-start(f32[4,2,1152]{2,1,0:T(2,128)S(1)} %get-tuple-element.67.lse_ref) | copy-start | bytes 110596
  276.2 2.9 collective-permute-start.8
  284.4 2.9 collective-permute-start.9
  287.5 16.9 %copy-start.4 = (bf16[1152,1024]{1,0:T(8,128)(2,1)}, bf16[1152,1024]{1,0:T(8,128)(2,1)S(1)}, u32[]{:S(2)}) copy-start(bf16[1152,1024]{1,0:T(8,128)(2,1)S(1)} %pad_maximum_fusion.2.x_ref.refs_5_) | copy-start | bytes 7077892
  287.5 16.9 %copy-start.30 = (bf16[2048,1024]{1,0:T(8,128)(2,1)S(1)}, bf16[2048,1024]{1,0:T(8,128)(2,1)}, u32[]{:S(2)}) copy-start(bf16[2048,1024]{1,0:T(8,128)(2,1)} %get-tuple-element.60.refs_21_) | copy-start | bytes 12582916
  308.9 2.9 collective-permute-start.10
  317.4 21.4 %copy-start.18 = (f32[576,1024]{1,0:T(8,128)}, f32[576,1024]{1,0:T(8,128)S(1)}, u32[]{:S(2)}) copy-start(f32[576,1024]{1,0:T(8,128)S(1)} %get-tuple-element.210) | copy-start | bytes 7077892
  317.4 21.4 %copy-start.63 = (f32[576]{0:T(1024)}, f32[576]{0:T(1024)S(1)}, u32[]{:S(2)}) copy-start(f32[576]{0:T(1024)S(1)} %broadcast_multiply_fusion.6) | copy-start | bytes 6916
  318.0 20.7 %copy-start.77 = (f32[576]{0:T(1024)}, f32[576]{0:T(1024)S(1)}, u32[]{:S(2)}) copy-start(f32[576]{0:T(1024)S(1)} %add_rsqrt_fusion) | copy-start | bytes 6916
  322.0 11.2 %copy-start.26 = (bf16[576,1024]{1,0:T(8,128)(2,1)}, bf16[576,1024]{1,0:T(8,128)(2,1)S(1)}, u32[]{:S(2)}) copy-start(bf16[576,1024]{1,0:T(8,128)(2,1)S(1)} %get-tuple-element.189) | copy-start | bytes 3538948
  322.0 2.8 collective-permute-start.12
  335.8 2.9 collective-permute-start.13
  345.8 2.8 collective-permute-start.14
  380.3 6.0 collective-permute-start.15
  386.3 8.7 %copy-start.16 = (f32[576,1024]{1,0:T(8,128)S(1)}, f32[576,1024]{1,0:T(8,128)}, u32[]{:S(2)}) copy-start(f32[576,1024]{1,0:T(8,128)} %copy-done.15) | copy-start | bytes 7077892
  386.3 8.7 %copy-start.19 = (f32[576,1024]{1,0:T(8,128)S(1)}, f32[576,1024]{1,0:T(8,128)}, u32[]{:S(2)}) copy-start(f32[576,1024]{1,0:T(8,128)} %copy-done.18) | copy-start | bytes 7077892
  386.4 8.7 %copy-start.56 = (f32[1,1024]{1,0:T(1,128)S(1)}, f32[1,1024]{1,0:T(1,128)}, u32[]{:S(2)}) copy-start(f32[1,1024]{1,0:T(1,128)} %copy-done.54) | copy-start | bytes 12292
  386.4 8.7 %copy-start.58 = (f32[576]{0:T(1024)S(1)}, f32[576]{0:T(1024)}, u32[]{:S(2)}) copy-start(f32[576]{0:T(1024)} %copy-done.57) | copy-start | bytes 6916
  393.7 30.6 %collective-permute-start.16 = (bf16[576,1024]{1,0:T(8,128)(2,1)}, bf16[576,1024]{1,0:T(8,128)(2,1)}, u32[]{:S(2)}, u32[]{:S(2)}) collective-permute-start(bf16[576,1024]{1,0:T(8,128)(2,1)} %get-tuple-element.211), channel_id=1, source_target_pairs={{16,0},{17,1},{18,2},{19,3},{20,4},{21,5},{22,6},{23,7},{24,8},{25... | collective-permute-start | bytes 3538952 | tf_op jit(solution)/shard_map/ppermute | solution.py:40
  397.7 238.5 %collective-permute-start.19 = (bf16[144,1024]{1,0:T(8,128)(2,1)}, bf16[144,1024]{1,0:T(8,128)(2,1)}, u32[]{:S(2)}, u32[]{:S(2)}) collective-permute-start(bf16[144,1024]{1,0:T(8,128)(2,1)} %get-tuple-element.218), channel_id=1, source_target_pairs={{2,0},{4,2},{6,4},{0,6},{3,1},{5,3},{7,5},{1,7},{10,8},{12,10},{14... | collective-permute-start | bytes 884744 | tf_op jit(solution)/shard_map/ppermute | solution.py:34
  397.7 239.6 %collective-permute-start.18 = (bf16[144,1024]{1,0:T(8,128)(2,1)}, bf16[144,1024]{1,0:T(8,128)(2,1)}, u32[]{:S(2)}, u32[]{:S(2)}) collective-permute-start(bf16[144,1024]{1,0:T(8,128)(2,1)} %get-tuple-element.219), channel_id=1, source_target_pairs={{4,0},{6,2},{0,4},{2,6},{5,1},{7,3},{1,5},{3,7},{12,8},{14,10},{8,... | collective-permute-start | bytes 884744 | tf_op jit(solution)/shard_map/ppermute | solution.py:34
  397.7 240.3 %collective-permute-start.11 = (bf16[144,1024]{1,0:T(8,128)(2,1)}, bf16[144,1024]{1,0:T(8,128)(2,1)}, u32[]{:S(2)}, u32[]{:S(2)}) collective-permute-start(bf16[144,1024]{1,0:T(8,128)(2,1)} %get-tuple-element.220), channel_id=1, source_target_pairs={{6,0},{0,2},{2,4},{4,6},{7,1},{1,3},{3,5},{5,7},{14,8},{8,10},{10,... | collective-permute-start | bytes 884744 | tf_op jit(solution)/shard_map/ppermute | solution.py:34
  431.2 6.2 collective-permute-start.17
  (95 other events, 397.8 us)
